TPU v7x, 32 devices: a whole 2x2x4 slice. The times are simulated.
32 devices in a mesh: sec: 4 (over x, core), elem: 8 (over z, y).
Axes of the slice: x: 2, y: 2, z: 4, core: 2. Of those that a mesh axis runs over, the one named last changes fastest.
Arguments:
- thermal_level_points: float32 [4, 8, 8, 8, 1024], P('sec', None, None, None, 'elem'), may hold values from -6 to 6
- flow_speed_vector: float32 [3, 4, 8, 8, 8, 1024], P(None, 'sec', None, None, None, 'elem'), may hold values from -3 to 3
- thermal_diffusivity_cell: float32 [4, 1024], P('sec', 'elem'), may hold values from 0.3 to 3
- metal_cell_indicator: int32 [4, 1024], P('sec', 'elem'), may hold values 0 or 1
- adjoining_patch: int32 [4, 1024], P('sec', 'elem'), may hold values from 0 to 3, as said below
Outputs:
- temperature_out: float32 [4, 8, 8, 8, 1024], P('sec', None, None, None, 'elem')
Inputs may be any that keep to these rules, and one draw needn't show every extreme that they name: adjoining_patch[adjoining_patch[s, e], e] = s and adjoining_patch[s, e] != s: at every chain position the sections are paired; within each aligned block of 128 chain positions a pair of sections shares at most 43 positions, and some pair shares exactly 43.
All inputs are finite; a program needn't handle non-finite values. No bound on the sum of `metal_cell_indicator` on one device may be relied on, other than what follows from the above.
Results may differ from a plain program's by a relative error of at most 0.0001.
Values sent between devices are 32-bit elements; how exact they have to be, the bound alone decides.
No kernel may reach another device: no remote copies, remote signals or barrier semaphores. Data moves between devices by JAX's collectives and lax.ppermute only.
A program may use at most 64 MiB of HBM per device.

v0:
```python
import jax
import jax.numpy as jnp
import numpy as np
from jax import lax
from jax.sharding import PartitionSpec as P

LINE_POINT_TOTAL = 8
FINE = 11
SWEEPS = 4
STEPS = 2


highest = lax.Precision.HIGHEST
time_step = 0.05
relaxation = 0.4
penalty = 30.0


def padded(block, sides, width):
    for axis, dim in sides:
        count = lax.axis_size(axis)
        forward = [(i, i + 1) for i in range(count - 1)]
        backward = [(target, source) for source, target in forward]
        low = lax.ppermute(
            lax.slice_in_dim(block, block.shape[dim] - width, None, axis=dim), axis, forward
        )
        high = lax.ppermute(lax.slice_in_dim(block, 0, width, axis=dim), axis, backward)
        block = jnp.concatenate([low, block, high], axis=dim)
    return block


def legendre_pair(order, points):
    previous = points * 0.0 + 1.0
    current = points * 1.0
    for level in range(2, order + 1):
        previous, current = (
            current,
            ((2 * level - 1) * points * current - (level - 1) * previous) / level,
        )
    return (current, previous)


def make_tables():
    degree = LINE_POINT_TOTAL - 1
    gll_nodes = -np.cos(np.pi * np.arange(LINE_POINT_TOTAL) / degree)
    for repeat in range(100):
        current, previous = legendre_pair(degree, gll_nodes)
        gll_nodes = gll_nodes - (gll_nodes * current - previous) / (LINE_POINT_TOTAL * current)
    values, lower_values = legendre_pair(degree, gll_nodes)
    weights = 2.0 / (degree * (degree + 1) * values**2)
    spatial_derivative = np.zeros((LINE_POINT_TOTAL, LINE_POINT_TOTAL))
    for row_index in range(LINE_POINT_TOTAL):
        for column_index in range(LINE_POINT_TOTAL):
            if row_index != column_index:
                spatial_derivative[row_index, column_index] = values[row_index] / (
                    values[column_index] * (gll_nodes[row_index] - gll_nodes[column_index])
                )
    spatial_derivative[0, 0] = -degree * (degree + 1) / 4.0
    spatial_derivative[-1, -1] = degree * (degree + 1) / 4.0
    fine_nodes = -np.cos(np.pi * (np.arange(FINE) + 0.75) / (FINE + 0.5))
    for repeat in range(100):
        current, previous = legendre_pair(FINE, fine_nodes)
        slope = FINE * (fine_nodes * current - previous) / (fine_nodes * fine_nodes - 1.0)
        fine_nodes = fine_nodes - current / slope
    current, previous = legendre_pair(FINE, fine_nodes)
    slope = FINE * (fine_nodes * current - previous) / (fine_nodes * fine_nodes - 1.0)
    fine_weights = 2.0 / ((1.0 - fine_nodes * fine_nodes) * slope * slope)
    interpolation = np.ones((FINE, LINE_POINT_TOTAL))
    for column_index in range(LINE_POINT_TOTAL):
        for other_index in range(LINE_POINT_TOTAL):
            if other_index != column_index:
                interpolation[:, column_index] *= (fine_nodes - gll_nodes[other_index]) / (
                    gll_nodes[column_index] - gll_nodes[other_index]
                )
    stiffness_1d = spatial_derivative.T @ (weights[:, None] * spatial_derivative)
    return (
        jnp.asarray(spatial_derivative, jnp.float32),
        jnp.asarray(interpolation, jnp.float32),
        jnp.asarray(stiffness_1d, jnp.float32),
        jnp.asarray(weights, jnp.float32),
        jnp.asarray(fine_weights, jnp.float32),
    )


def act_along_coordinate(matrix, grid_values, coordinate_axis_label):
    if coordinate_axis_label == 0:
        return jnp.einsum("qa,sabce->sqbce", matrix, grid_values, precision=highest)
    if coordinate_axis_label == 1:
        return jnp.einsum("qb,sabce->saqce", matrix, grid_values, precision=highest)
    return jnp.einsum("qc,sabce->sabqe", matrix, grid_values, precision=highest)


def lift_fine(matrix, grid_values):
    result = grid_values
    for coordinate_axis_label in range(3):
        result = act_along_coordinate(matrix, result, coordinate_axis_label)
    return result


def point_weights(weights):
    return (
        weights[None, :, None, None, None],
        weights[None, None, :, None, None],
        weights[None, None, None, :, None],
    )


def mass_grid(weights):
    weight_a, weight_b, weight_c = point_weights(weights)
    return weight_a * weight_b * weight_c


def transport_flux(
    thermal_level_points, flow_speed_vector, liquid_cell_indicator, spectral_matrix_bundle
):
    spatial_derivative, interpolation, stiffness_1d, weights, fine_weights = spectral_matrix_bundle
    fluid_grid = liquid_cell_indicator[:, None, None, None, :]
    product_sum = None
    for coordinate_axis_label in range(3):
        slope_vector_values = act_along_coordinate(
            spatial_derivative, thermal_level_points, coordinate_axis_label
        )
        term = lift_fine(
            interpolation, flow_speed_vector[coordinate_axis_label] * fluid_grid
        ) * lift_fine(interpolation, slope_vector_values)
        product_sum = term if coordinate_axis_label == 0 else product_sum + term
    cube = fine_weights[:, None, None] * fine_weights[None, :, None] * fine_weights[None, None, :]
    return lift_fine(interpolation.T, product_sum * cube[None, :, :, :, None])


def stiffness_apply(grid_values, spectral_matrix_bundle):
    stiffness_1d = spectral_matrix_bundle[2]
    weight_a, weight_b, weight_c = point_weights(spectral_matrix_bundle[3])
    return (
        act_along_coordinate(stiffness_1d, grid_values, 0) * (weight_b * weight_c)
        + act_along_coordinate(stiffness_1d, grid_values, 1) * (weight_a * weight_c)
        + act_along_coordinate(stiffness_1d, grid_values, 2) * (weight_a * weight_b)
    )


def face_terms(grid_values, near_minus, near_plus, far_wall, coefficients, spectral_matrix_bundle):
    coef_left, coef_right, coef_wall = coefficients
    weights = spectral_matrix_bundle[3]
    face_weight = (weights[:, None] * weights[None, :])[None, :, :, None]
    result = jnp.zeros_like(grid_values)
    result = result.at[:, 0].add(
        coef_left[:, None, None, :] * face_weight * (grid_values[:, 0] - near_plus)
    )
    result = result.at[:, -1].add(
        coef_right[:, None, None, :] * face_weight * (grid_values[:, -1] - near_minus)
    )
    result = result.at[:, :, :, 0].add(
        coef_wall[:, None, None, :] * face_weight * (grid_values[:, :, :, 0] - far_wall)
    )
    return result


def diagonal_h(thermal_diffusivity_cell, coefficients, spectral_matrix_bundle):
    coef_left, coef_right, coef_wall = coefficients
    stiffness_1d, weights = (spectral_matrix_bundle[2], spectral_matrix_bundle[3])
    weight_a, weight_b, weight_c = point_weights(weights)
    stiff_diag = jnp.diagonal(stiffness_1d)
    k_diag = (
        stiff_diag[None, :, None, None, None] * weight_b * weight_c
        + weight_a * stiff_diag[None, None, :, None, None] * weight_c
        + weight_a * weight_b * stiff_diag[None, None, None, :, None]
    )
    result = (
        mass_grid(weights) / time_step + thermal_diffusivity_cell[:, None, None, None, :] * k_diag
    )
    face_weight = (weights[:, None] * weights[None, :])[None, :, :, None]
    result = result.at[:, 0].add(coef_left[:, None, None, :] * face_weight)
    result = result.at[:, -1].add(coef_right[:, None, None, :] * face_weight)
    result = result.at[:, :, :, 0].add(coef_wall[:, None, None, :] * face_weight)
    return result


def sweep_update(
    iterate, right_side, diagonal, faces_part, thermal_diffusivity_cell, spectral_matrix_bundle
):
    applied = (
        mass_grid(spectral_matrix_bundle[3]) / time_step * iterate
        + thermal_diffusivity_cell[:, None, None, None, :]
        * stiffness_apply(iterate, spectral_matrix_bundle)
        + faces_part
    )
    return iterate + relaxation * (right_side - applied) / diagonal


def select_rows(partner_row, partial_value, pieces, first_row):
    span = pieces.shape[0]
    onehot = (partner_row[None, :] == first_row + lax.iota(jnp.int32, span)[:, None]).astype(
        jnp.float32
    )
    shaped = onehot.reshape((span,) + (1,) * (pieces.ndim - 2) + (partner_row.shape[0],))
    return partial_value + jnp.sum(shaped * pieces, axis=0, keepdims=True)


def wall_partner(wall_face, partner_row):
    return select_rows(
        partner_row,
        jnp.zeros_like(wall_face),
        lax.all_gather(wall_face, "sec", axis=0, tiled=True),
        jnp.int32(0),
    )


def body(
    thermal_level_points,
    flow_speed_vector,
    thermal_diffusivity_cell,
    metal_cell_indicator,
    adjoining_patch,
):
    spectral_matrix_bundle = make_tables()
    elem_count = thermal_diffusivity_cell.shape[1]
    chain_total = elem_count * lax.axis_size("elem")
    own_index = lax.axis_index("elem") * elem_count + lax.iota(jnp.int32, elem_count)
    conductivity_rim = padded(thermal_diffusivity_cell, (("elem", 1),), 1)
    coef_right = jnp.where(
        own_index < chain_total - 1,
        penalty * (thermal_diffusivity_cell + conductivity_rim[:, 2:]) * 0.5,
        0.0,
    )
    coef_left = jnp.where(
        own_index > 0, penalty * (thermal_diffusivity_cell + conductivity_rim[:, :-2]) * 0.5, 0.0
    )
    solid_float = metal_cell_indicator.astype(jnp.float32)
    partner_row = adjoining_patch[0]
    first_row = jnp.int32(0)
    partner_k = select_rows(
        partner_row,
        jnp.zeros_like(thermal_diffusivity_cell),
        lax.all_gather(thermal_diffusivity_cell, "sec", axis=0, tiled=True),
        first_row,
    )
    partner_solid = select_rows(
        partner_row,
        jnp.zeros_like(thermal_diffusivity_cell),
        lax.all_gather(solid_float, "sec", axis=0, tiled=True),
        first_row,
    )
    coef_wall = jnp.where(
        solid_float != partner_solid, penalty * (thermal_diffusivity_cell + partner_k) * 0.5, 0.0
    )
    coefficients = (coef_left, coef_right, coef_wall)
    liquid_cell_indicator = 1.0 - solid_float
    diagonal = diagonal_h(thermal_diffusivity_cell, coefficients, spectral_matrix_bundle)
    iteration_snapshot = thermal_level_points
    for step_index in range(STEPS):
        convected = transport_flux(
            iteration_snapshot, flow_speed_vector, liquid_cell_indicator, spectral_matrix_bundle
        )
        right_side = (
            mass_grid(spectral_matrix_bundle[3]) / time_step * iteration_snapshot - convected
        )
        iterate = iteration_snapshot
        for sweep_index in range(SWEEPS):
            stacked = jnp.stack([iterate[:, 0], iterate[:, -1]], 0)
            rimmed = padded(stacked, (("elem", 4),), 1)
            near_minus = rimmed[0][..., 2:]
            near_plus = rimmed[1][..., :-2]
            far_wall = wall_partner(iterate[:, :, :, 0], partner_row)
            faces_part = face_terms(
                iterate, near_minus, near_plus, far_wall, coefficients, spectral_matrix_bundle
            )
            iterate = sweep_update(
                iterate,
                right_side,
                diagonal,
                faces_part,
                thermal_diffusivity_cell,
                spectral_matrix_bundle,
            )
        iteration_snapshot = iterate
    return iteration_snapshot


def solution(mesh):
    return jax.shard_map(
        body,
        mesh=mesh,
        in_specs=(
            P("sec", None, None, None, "elem"),
            P(None, "sec", None, None, None, "elem"),
            P("sec", "elem"),
            P("sec", "elem"),
            P("sec", "elem"),
        ),
        out_specs=P("sec", None, None, None, "elem"),
        check_vma=False,
    )
```

profile of v0, /device:TPU:5, one launch (start us, length us, event | category | flops | bytes accessed | tf_op | source)
XLA Modules:
  0.0 209.0 jit_solution(16491866317113112972)
XLA Ops:
  1.6 2.1 collective-permute-start.2
  3.6 4.3 %collective-permute-start.1 = (f32[2,1,8,8,1]{4,3,2,1,0:T(8,128)}, f32[2,1,8,8,1]{4,3,2,1,0:T(8,128)}, u32[]{:S(2)}, u32[]{:S(2)}) collective-permute-start(f32[2,1,8,8,1]{4,3,2,1,0:T(8,128)} %get-tuple-element.380), channel_id=1, source_target_pairs={{0,1},{1,2},{2,3},{3,4},{4,5},{5,6},{6,7},{8,9},{9,10},{10,11},{11... | collective-permute-start | bytes 1544 | tf_op jit(solution)/shard_map/ppermute | solution.py:24
  8.5 2.2 %collective-permute-start = (f32[1,1]{1,0:T(1,128)}, f32[1,1]{1,0:T(1,128)}, u32[]{:S(2)}, u32[]{:S(2)}) collective-permute-start(f32[1,1]{1,0:T(1,128)} %get-tuple-element.393), channel_id=1, source_target_pairs={{0,1},{1,2},{2,3},{3,4},{4,5},{5,6},{6,7},{8,9},{9,10},{10,11},{11... | collective-permute-start | bytes 20 | tf_op jit(solution)/shard_map/ppermute | solution.py:24
  10.8 3.6 %collective-permute-start.3 = (f32[1,1]{1,0:T(1,128)}, f32[1,1]{1,0:T(1,128)}, u32[]{:S(2)}, u32[]{:S(2)}) collective-permute-start(f32[1,1]{1,0:T(1,128)} %get-tuple-element.392), channel_id=1, source_target_pairs={{1,0},{2,1},{3,2},{4,3},{5,4},{6,5},{7,6},{9,8},{10,9},{11,10},{12... | collective-permute-start | bytes 20 | tf_op jit(solution)/shard_map/ppermute | solution.py:27
  18.9 6.6 %all-gather.8 = f32[4,1,128]{2,1,0:T(1,128)S(1)} all-gather(f32[1,1,128]{2,1,0:T(1,128)S(1)} %convert_bitcast_fusion), channel_id=1, replica_groups=mesh['sec'=4,'elem'=8] {'sec'}, dimensions={0}, use_global_device_ids=true | all-gather | bytes 2560 | tf_op jit(solution)/shard_map/all_gather | solution.py:240
  25.5 5.2 %all-gather.9 = f32[4,1,128]{2,1,0:T(1,128)S(1)} all-gather(f32[1,1,128]{2,1,0:T(1,128)S(1)} %bitcast.983), channel_id=1, replica_groups=mesh['sec'=4,'elem'=8] {'sec'}, dimensions={0}, use_global_device_ids=true | all-gather | bytes 2560 | tf_op jit(solution)/shard_map/all_gather | solution.py:234
  32.1 5.7 %all-gather = f32[4,8,8,1,128]{4,2,3,1,0:T(8,128)S(1)} all-gather(f32[1,8,8,1,128]{4,2,3,1,0:T(8,128)S(1)} %bitcast.964), channel_id=2, replica_groups=mesh['sec'=4,'elem'=8] {'sec'}, dimensions={0}, use_global_device_ids=true | all-gather | bytes 163840 | tf_op jit(solution)/shard_map/all_gather | solution.py:203
  74.9 4.3 %collective-permute-start.4 = (f32[2,1,8,8,1]{4,3,2,1,0:T(8,128)S(1)}, f32[2,1,8,8,1]{4,3,2,1,0:T(8,128)S(1)}, u32[]{:S(2)}, u32[]{:S(2)}) collective-permute-start(f32[2,1,8,8,1]{4,3,2,1,0:T(8,128)S(1)} %get-tuple-element.378), channel_id=1, source_target_pairs={{0,1},{1,2},{2,3},{3,4},{4,5},{5,6},{6,7},{8,9},{9,10},{10,11},{11... | collective-permute-start | bytes 1544 | tf_op jit(solution)/shard_map/ppermute | solution.py:24
  79.2 6.0 %all-gather.1 = f32[4,8,8,1,128]{4,2,3,1,0:T(8,128)S(1)} all-gather(f32[1,8,8,1,128]{4,2,3,1,0:T(8,128)S(1)} %bitcast.965), channel_id=3, replica_groups=mesh['sec'=4,'elem'=8] {'sec'}, dimensions={0}, use_global_device_ids=true | all-gather | bytes 163840 | tf_op jit(solution)/shard_map/all_gather | solution.py:203
  97.0 4.3 %collective-permute-start.6 = (f32[2,1,8,8,1]{4,3,2,1,0:T(8,128)S(1)}, f32[2,1,8,8,1]{4,3,2,1,0:T(8,128)S(1)}, u32[]{:S(2)}, u32[]{:S(2)}) collective-permute-start(f32[2,1,8,8,1]{4,3,2,1,0:T(8,128)S(1)} %get-tuple-element.376), channel_id=1, source_target_pairs={{0,1},{1,2},{2,3},{3,4},{4,5},{5,6},{6,7},{8,9},{9,10},{10,11},{11... | collective-permute-start | bytes 1544 | tf_op jit(solution)/shard_map/ppermute | solution.py:24
  101.3 6.0 %all-gather.2 = f32[4,8,8,1,128]{4,2,3,1,0:T(8,128)S(1)} all-gather(f32[1,8,8,1,128]{4,2,3,1,0:T(8,128)S(1)} %bitcast.966), channel_id=4, replica_groups=mesh['sec'=4,'elem'=8] {'sec'}, dimensions={0}, use_global_device_ids=true | all-gather | bytes 163840 | tf_op jit(solution)/shard_map/all_gather | solution.py:203
  119.1 4.3 %collective-permute-start.8 = (f32[2,1,8,8,1]{4,3,2,1,0:T(8,128)S(1)}, f32[2,1,8,8,1]{4,3,2,1,0:T(8,128)S(1)}, u32[]{:S(2)}, u32[]{:S(2)}) collective-permute-start(f32[2,1,8,8,1]{4,3,2,1,0:T(8,128)S(1)} %get-tuple-element.374), channel_id=1, source_target_pairs={{0,1},{1,2},{2,3},{3,4},{4,5},{5,6},{6,7},{8,9},{9,10},{10,11},{11... | collective-permute-start | bytes 1544 | tf_op jit(solution)/shard_map/ppermute | solution.py:24
  123.4 6.2 %all-gather.3 = f32[4,8,8,1,128]{4,2,3,1,0:T(8,128)S(1)} all-gather(f32[1,8,8,1,128]{4,2,3,1,0:T(8,128)S(1)} %bitcast.967), channel_id=5, replica_groups=mesh['sec'=4,'elem'=8] {'sec'}, dimensions={0}, use_global_device_ids=true | all-gather | bytes 163840 | tf_op jit(solution)/shard_map/all_gather | solution.py:203
  149.3 1.9 collective-permute-start.11
  151.2 4.3 %collective-permute-start.10 = (f32[2,1,8,8,1]{4,3,2,1,0:T(8,128)S(1)}, f32[2,1,8,8,1]{4,3,2,1,0:T(8,128)S(1)}, u32[]{:S(2)}, u32[]{:S(2)}) collective-permute-start(f32[2,1,8,8,1]{4,3,2,1,0:T(8,128)S(1)} %get-tuple-element.372), channel_id=1, source_target_pairs={{0,1},{1,2},{2,3},{3,4},{4,5},{5,6},{6,7},{8,9},{9,10},{10,11},{11... | collective-permute-start | bytes 1544 | tf_op jit(solution)/shard_map/ppermute | solution.py:24
  155.5 6.0 %all-gather.4 = f32[4,8,8,1,128]{4,2,3,1,0:T(8,128)S(1)} all-gather(f32[1,8,8,1,128]{4,2,3,1,0:T(8,128)S(1)} %bitcast.963), channel_id=6, replica_groups=mesh['sec'=4,'elem'=8] {'sec'}, dimensions={0}, use_global_device_ids=true | all-gather | bytes 163840 | tf_op jit(solution)/shard_map/all_gather | solution.py:203
  165.9 1.9 collective-permute-start.13
  167.8 4.3 %collective-permute-start.12 = (f32[2,1,8,8,1]{4,3,2,1,0:T(8,128)S(1)}, f32[2,1,8,8,1]{4,3,2,1,0:T(8,128)S(1)}, u32[]{:S(2)}, u32[]{:S(2)}) collective-permute-start(f32[2,1,8,8,1]{4,3,2,1,0:T(8,128)S(1)} %get-tuple-element.370), channel_id=1, source_target_pairs={{0,1},{1,2},{2,3},{3,4},{4,5},{5,6},{6,7},{8,9},{9,10},{10,11},{11... | collective-permute-start | bytes 1544 | tf_op jit(solution)/shard_map/ppermute | solution.py:24
  172.1 6.0 %all-gather.5 = f32[4,8,8,1,128]{4,2,3,1,0:T(8,128)S(1)} all-gather(f32[1,8,8,1,128]{4,2,3,1,0:T(8,128)S(1)} %bitcast.968), channel_id=7, replica_groups=mesh['sec'=4,'elem'=8] {'sec'}, dimensions={0}, use_global_device_ids=true | all-gather | bytes 163840 | tf_op jit(solution)/shard_map/all_gather | solution.py:203
  180.3 1.9 collective-permute-start.15
  182.2 4.3 %collective-permute-start.14 = (f32[2,1,8,8,1]{4,3,2,1,0:T(8,128)S(1)}, f32[2,1,8,8,1]{4,3,2,1,0:T(8,128)S(1)}, u32[]{:S(2)}, u32[]{:S(2)}) collective-permute-start(f32[2,1,8,8,1]{4,3,2,1,0:T(8,128)S(1)} %get-tuple-element.368), channel_id=1, source_target_pairs={{0,1},{1,2},{2,3},{3,4},{4,5},{5,6},{6,7},{8,9},{9,10},{10,11},{11... | collective-permute-start | bytes 1544 | tf_op jit(solution)/shard_map/ppermute | solution.py:24
  186.5 6.0 %all-gather.6 = f32[4,8,8,1,128]{4,2,3,1,0:T(8,128)S(1)} all-gather(f32[1,8,8,1,128]{4,2,3,1,0:T(8,128)S(1)} %bitcast.969), channel_id=8, replica_groups=mesh['sec'=4,'elem'=8] {'sec'}, dimensions={0}, use_global_device_ids=true | all-gather | bytes 163840 | tf_op jit(solution)/shard_map/all_gather | solution.py:203
  196.6 4.3 %collective-permute-start.16 = (f32[2,1,8,8,1]{4,3,2,1,0:T(8,128)S(1)}, f32[2,1,8,8,1]{4,3,2,1,0:T(8,128)S(1)}, u32[]{:S(2)}, u32[]{:S(2)}) collective-permute-start(f32[2,1,8,8,1]{4,3,2,1,0:T(8,128)S(1)} %get-tuple-element.366), channel_id=1, source_target_pairs={{0,1},{1,2},{2,3},{3,4},{4,5},{5,6},{6,7},{8,9},{9,10},{10,11},{11... | collective-permute-start | bytes 1544 | tf_op jit(solution)/shard_map/ppermute | solution.py:24
  200.9 6.0 %all-gather.7 = f32[4,8,8,1,128]{4,2,3,1,0:T(8,128)S(1)} all-gather(f32[1,8,8,1,128]{4,2,3,1,0:T(8,128)S(1)} %bitcast.970), channel_id=9, replica_groups=mesh['sec'=4,'elem'=8] {'sec'}, dimensions={0}, use_global_device_ids=true | all-gather | bytes 163840 | tf_op jit(solution)/shard_map/all_gather | solution.py:203
  (259 shorter events, 100.2 us)
Async XLA Ops:
  0.0 14.4 %copy-start.1 = (f32[1,8,8,8,128]{4,3,2,1,0:T(8,128)S(1)}, f32[1,8,8,8,128]{4,3,2,1,0:T(8,128)}, u32[]{:S(2)}) copy-start(f32[1,8,8,8,128]{4,3,2,1,0:T(8,128)} %param.64) | copy-start | bytes 786436
  1.6 6.3 %copy-start.28 = (f32[1,128]{1,0:T(1,128)S(1)}, f32[1,128]{1,0:T(1,128)}, u32[]{:S(2)}) copy-start(f32[1,128]{1,0:T(1,128)} %param.66) | copy-start | bytes 1540
  1.6 61.2 %collective-permute-start.2 = (f32[2,1,8,8,1]{4,3,2,1,0:T(8,128)}, f32[2,1,8,8,1]{4,3,2,1,0:T(8,128)}, u32[]{:S(2)}, u32[]{:S(2)}) collective-permute-start(f32[2,1,8,8,1]{4,3,2,1,0:T(8,128)} %get-tuple-element.381), channel_id=1, source_target_pairs={{1,0},{2,1},{3,2},{4,3},{5,4},{6,5},{7,6},{9,8},{10,9},{11,10},{12... | collective-permute-start | bytes 1544 | tf_op jit(solution)/shard_map/ppermute | solution.py:27
  3.6 59.2 %collective-permute-start.1 = (f32[2,1,8,8,1]{4,3,2,1,0:T(8,128)}, f32[2,1,8,8,1]{4,3,2,1,0:T(8,128)}, u32[]{:S(2)}, u32[]{:S(2)}) collective-permute-start(f32[2,1,8,8,1]{4,3,2,1,0:T(8,128)} %get-tuple-element.380), channel_id=1, source_target_pairs={{0,1},{1,2},{2,3},{3,4},{4,5},{5,6},{6,7},{8,9},{9,10},{10,11},{11... | collective-permute-start | bytes 1544 | tf_op jit(solution)/shard_map/ppermute | solution.py:24
  8.5 38.3 %collective-permute-start = (f32[1,1]{1,0:T(1,128)}, f32[1,1]{1,0:T(1,128)}, u32[]{:S(2)}, u32[]{:S(2)}) collective-permute-start(f32[1,1]{1,0:T(1,128)} %get-tuple-element.393), channel_id=1, source_target_pairs={{0,1},{1,2},{2,3},{3,4},{4,5},{5,6},{6,7},{8,9},{9,10},{10,11},{11... | collective-permute-start | bytes 20 | tf_op jit(solution)/shard_map/ppermute | solution.py:24
  10.8 36.1 %collective-permute-start.3 = (f32[1,1]{1,0:T(1,128)}, f32[1,1]{1,0:T(1,128)}, u32[]{:S(2)}, u32[]{:S(2)}) collective-permute-start(f32[1,1]{1,0:T(1,128)} %get-tuple-element.392), channel_id=1, source_target_pairs={{1,0},{2,1},{3,2},{4,3},{5,4},{6,5},{7,6},{9,8},{10,9},{11,10},{12... | collective-permute-start | bytes 20 | tf_op jit(solution)/shard_map/ppermute | solution.py:27
  32.1 5.7 %copy-start.33 = (s32[1,128]{1,0:T(1,128)S(1)}, s32[1,128]{1,0:T(1,128)}, u32[]{:S(2)}) copy-start(s32[1,128]{1,0:T(1,128)} %param.68) | copy-start | bytes 1540
  48.2 16.3 %copy-start.18 = (f32[128]{0:T(128)}, f32[128]{0:T(128)S(1)}, u32[]{:S(2)}) copy-start(f32[128]{0:T(128)S(1)} %get-tuple-element.390) | copy-start | bytes 1540
  48.2 16.5 %copy-start.23 = (f32[128]{0:T(128)}, f32[128]{0:T(128)S(1)}, u32[]{:S(2)}) copy-start(f32[128]{0:T(128)S(1)} %get-tuple-element.389) | copy-start | bytes 1540
  73.0 12.2 %collective-permute-start.5 = (f32[2,1,8,8,1]{4,3,2,1,0:T(8,128)S(1)}, f32[2,1,8,8,1]{4,3,2,1,0:T(8,128)S(1)}, u32[]{:S(2)}, u32[]{:S(2)}) collective-permute-start(f32[2,1,8,8,1]{4,3,2,1,0:T(8,128)S(1)} %get-tuple-element.379), channel_id=1, source_target_pairs={{1,0},{2,1},{3,2},{4,3},{5,4},{6,5},{7,6},{9,8},{10,9},{11,10},{12... | collective-permute-start | bytes 1544 | tf_op jit(solution)/shard_map/ppermute | solution.py:27
  74.9 10.3 %collective-permute-start.4 = (f32[2,1,8,8,1]{4,3,2,1,0:T(8,128)S(1)}, f32[2,1,8,8,1]{4,3,2,1,0:T(8,128)S(1)}, u32[]{:S(2)}, u32[]{:S(2)}) collective-permute-start(f32[2,1,8,8,1]{4,3,2,1,0:T(8,128)S(1)} %get-tuple-element.378), channel_id=1, source_target_pairs={{0,1},{1,2},{2,3},{3,4},{4,5},{5,6},{6,7},{8,9},{9,10},{10,11},{11... | collective-permute-start | bytes 1544 | tf_op jit(solution)/shard_map/ppermute | solution.py:24
  95.1 12.2 %collective-permute-start.7 = (f32[2,1,8,8,1]{4,3,2,1,0:T(8,128)S(1)}, f32[2,1,8,8,1]{4,3,2,1,0:T(8,128)S(1)}, u32[]{:S(2)}, u32[]{:S(2)}) collective-permute-start(f32[2,1,8,8,1]{4,3,2,1,0:T(8,128)S(1)} %get-tuple-element.377), channel_id=1, source_target_pairs={{1,0},{2,1},{3,2},{4,3},{5,4},{6,5},{7,6},{9,8},{10,9},{11,10},{12... | collective-permute-start | bytes 1544 | tf_op jit(solution)/shard_map/ppermute | solution.py:27
  97.0 10.3 %collective-permute-start.6 = (f32[2,1,8,8,1]{4,3,2,1,0:T(8,128)S(1)}, f32[2,1,8,8,1]{4,3,2,1,0:T(8,128)S(1)}, u32[]{:S(2)}, u32[]{:S(2)}) collective-permute-start(f32[2,1,8,8,1]{4,3,2,1,0:T(8,128)S(1)} %get-tuple-element.376), channel_id=1, source_target_pairs={{0,1},{1,2},{2,3},{3,4},{4,5},{5,6},{6,7},{8,9},{9,10},{10,11},{11... | collective-permute-start | bytes 1544 | tf_op jit(solution)/shard_map/ppermute | solution.py:24
  117.2 12.4 %collective-permute-start.9 = (f32[2,1,8,8,1]{4,3,2,1,0:T(8,128)S(1)}, f32[2,1,8,8,1]{4,3,2,1,0:T(8,128)S(1)}, u32[]{:S(2)}, u32[]{:S(2)}) collective-permute-start(f32[2,1,8,8,1]{4,3,2,1,0:T(8,128)S(1)} %get-tuple-element.375), channel_id=1, source_target_pairs={{1,0},{2,1},{3,2},{4,3},{5,4},{6,5},{7,6},{9,8},{10,9},{11,10},{12... | collective-permute-start | bytes 1544 | tf_op jit(solution)/shard_map/ppermute | solution.py:27
  119.1 10.5 %collective-permute-start.8 = (f32[2,1,8,8,1]{4,3,2,1,0:T(8,128)S(1)}, f32[2,1,8,8,1]{4,3,2,1,0:T(8,128)S(1)}, u32[]{:S(2)}, u32[]{:S(2)}) collective-permute-start(f32[2,1,8,8,1]{4,3,2,1,0:T(8,128)S(1)} %get-tuple-element.374), channel_id=1, source_target_pairs={{0,1},{1,2},{2,3},{3,4},{4,5},{5,6},{6,7},{8,9},{9,10},{10,11},{11... | collective-permute-start | bytes 1544 | tf_op jit(solution)/shard_map/ppermute | solution.py:24
  149.3 12.7 %collective-permute-start.11 = (f32[2,1,8,8,1]{4,3,2,1,0:T(8,128)S(1)}, f32[2,1,8,8,1]{4,3,2,1,0:T(8,128)S(1)}, u32[]{:S(2)}, u32[]{:S(2)}) collective-permute-start(f32[2,1,8,8,1]{4,3,2,1,0:T(8,128)S(1)} %get-tuple-element.373), channel_id=1, source_target_pairs={{1,0},{2,1},{3,2},{4,3},{5,4},{6,5},{7,6},{9,8},{10,9},{11,10},{12... | collective-permute-start | bytes 1544 | tf_op jit(solution)/shard_map/ppermute | solution.py:27
  151.2 10.8 %collective-permute-start.10 = (f32[2,1,8,8,1]{4,3,2,1,0:T(8,128)S(1)}, f32[2,1,8,8,1]{4,3,2,1,0:T(8,128)S(1)}, u32[]{:S(2)}, u32[]{:S(2)}) collective-permute-start(f32[2,1,8,8,1]{4,3,2,1,0:T(8,128)S(1)} %get-tuple-element.372), channel_id=1, source_target_pairs={{0,1},{1,2},{2,3},{3,4},{4,5},{5,6},{6,7},{8,9},{9,10},{10,11},{11... | collective-permute-start | bytes 1544 | tf_op jit(solution)/shard_map/ppermute | solution.py:24
  155.4 6.0 %copy-start.30 = (f32[8,8]{0,1:T(8,128)S(1)}, f32[8,8]{0,1:T(8,128)}, u32[]{:S(2)}) copy-start(f32[8,8]{0,1:T(8,128)} %copy.430) | copy-start | bytes 772
  165.9 12.2 %collective-permute-start.13 = (f32[2,1,8,8,1]{4,3,2,1,0:T(8,128)S(1)}, f32[2,1,8,8,1]{4,3,2,1,0:T(8,128)S(1)}, u32[]{:S(2)}, u32[]{:S(2)}) collective-permute-start(f32[2,1,8,8,1]{4,3,2,1,0:T(8,128)S(1)} %get-tuple-element.371), channel_id=1, source_target_pairs={{1,0},{2,1},{3,2},{4,3},{5,4},{6,5},{7,6},{9,8},{10,9},{11,10},{12... | collective-permute-start | bytes 1544 | tf_op jit(solution)/shard_map/ppermute | solution.py:27
  167.8 10.3 %collective-permute-start.12 = (f32[2,1,8,8,1]{4,3,2,1,0:T(8,128)S(1)}, f32[2,1,8,8,1]{4,3,2,1,0:T(8,128)S(1)}, u32[]{:S(2)}, u32[]{:S(2)}) collective-permute-start(f32[2,1,8,8,1]{4,3,2,1,0:T(8,128)S(1)} %get-tuple-element.370), channel_id=1, source_target_pairs={{0,1},{1,2},{2,3},{3,4},{4,5},{5,6},{6,7},{8,9},{9,10},{10,11},{11... | collective-permute-start | bytes 1544 | tf_op jit(solution)/shard_map/ppermute | solution.py:24
  180.3 12.2 %collective-permute-start.15 = (f32[2,1,8,8,1]{4,3,2,1,0:T(8,128)S(1)}, f32[2,1,8,8,1]{4,3,2,1,0:T(8,128)S(1)}, u32[]{:S(2)}, u32[]{:S(2)}) collective-permute-start(f32[2,1,8,8,1]{4,3,2,1,0:T(8,128)S(1)} %get-tuple-element.369), channel_id=1, source_target_pairs={{1,0},{2,1},{3,2},{4,3},{5,4},{6,5},{7,6},{9,8},{10,9},{11,10},{12... | collective-permute-start | bytes 1544 | tf_op jit(solution)/shard_map/ppermute | solution.py:27
  182.2 10.3 %collective-permute-start.14 = (f32[2,1,8,8,1]{4,3,2,1,0:T(8,128)S(1)}, f32[2,1,8,8,1]{4,3,2,1,0:T(8,128)S(1)}, u32[]{:S(2)}, u32[]{:S(2)}) collective-permute-start(f32[2,1,8,8,1]{4,3,2,1,0:T(8,128)S(1)} %get-tuple-element.368), channel_id=1, source_target_pairs={{0,1},{1,2},{2,3},{3,4},{4,5},{5,6},{6,7},{8,9},{9,10},{10,11},{11... | collective-permute-start | bytes 1544 | tf_op jit(solution)/shard_map/ppermute | solution.py:24
  194.7 12.2 %collective-permute-start.17 = (f32[2,1,8,8,1]{4,3,2,1,0:T(8,128)S(1)}, f32[2,1,8,8,1]{4,3,2,1,0:T(8,128)S(1)}, u32[]{:S(2)}, u32[]{:S(2)}) collective-permute-start(f32[2,1,8,8,1]{4,3,2,1,0:T(8,128)S(1)} %get-tuple-element.367), channel_id=1, source_target_pairs={{1,0},{2,1},{3,2},{4,3},{5,4},{6,5},{7,6},{9,8},{10,9},{11,10},{12... | collective-permute-start | bytes 1544 | tf_op jit(solution)/shard_map/ppermute | solution.py:27
  196.6 10.3 %collective-permute-start.16 = (f32[2,1,8,8,1]{4,3,2,1,0:T(8,128)S(1)}, f32[2,1,8,8,1]{4,3,2,1,0:T(8,128)S(1)}, u32[]{:S(2)}, u32[]{:S(2)}) collective-permute-start(f32[2,1,8,8,1]{4,3,2,1,0:T(8,128)S(1)} %get-tuple-element.366), channel_id=1, source_target_pairs={{0,1},{1,2},{2,3},{3,4},{4,5},{5,6},{6,7},{8,9},{9,10},{10,11},{11... | collective-permute-start | bytes 1544 | tf_op jit(solution)/shard_map/ppermute | solution.py:24
  (29 other events, 32.1 us)
where the time goes:
time: 213 us; the launch traced here: 209 us
  blocking collectives  59.5 us (28%)
  matrix products  56.6 us (27%)
  starting transfers between devices  55.4 us (26%)
  local copies, waits for them, and re-layouts  22.3 us (10%)
  other arithmetic  13.6 us (6%)
    all_gather x8, blocking collectives, wall_partner(): lax.all_gather(wall_face, 'sec', axis=0, tiled=True)  47.8 us
    ppermute x9, starting transfers between devices, padded(): lax.ppermute(lax.slice_in_dim(block, block.shape[dim] - width, None, axis...  36.3 us
    dot_general x21, matrix products, act_along_coordinate(): return jnp.einsum('qc,sabce->sabqe', matrix, grid_values, precision=highest)  22.3 us
    ppermute x9, starting transfers between devices, padded(): lax.ppermute(lax.slice_in_dim(block, 0, width, axis=dim), axis, backward)  19 us
    dot_general x21, matrix products, act_along_coordinate(): return jnp.einsum('qb,sabce->saqce', matrix, grid_values, precision=highest)  18.5 us
    dot_general x21, matrix products, act_along_coordinate(): return jnp.einsum('qa,sabce->sqbce', matrix, grid_values, precision=highest)  15.8 us
    unnamed x71, local copies, waits for them, and re-layouts  9.3 us
    scatter-add x8, local copies, waits for them, and re-layouts, face_terms(): result.at[:, :, :, 0]  7.52 us
  transfers between devices with their start and end apart: 18, of which 0 were waited for; matrix products, arithmetic and copies ran while one was open for 14% of the time, Pallas kernels for 0%

commit v1 on v0

v1 whole, which is shorter than its diff:
```python
import functools

import jax
import jax.numpy as jnp
import ml_dtypes
import numpy as np
from jax import lax
from jax.experimental import pallas as pl
from jax.experimental.pallas import tpu as pltpu
from jax.sharding import PartitionSpec as P

LINE_POINT_TOTAL = 8
FINE = 11
SWEEPS = 4
STEPS = 2
GHOST = STEPS * SWEEPS

time_step = 0.05
relaxation = 0.4
penalty = 30.0

POINTS = LINE_POINT_TOTAL**3
FIELDS = 4
PARAM_ROWS = 8
LANES = 128
HALF = LINE_POINT_TOTAL // 2
MIRROR = FINE // 2
CLASSES = ((0, 0), (0, 1), (1, 0), (1, 1))
CLASS_ROWS = HALF * HALF * LINE_POINT_TOTAL


def round_up(value, unit):
    return -(-value // unit) * unit


PAIR_ROWS = round_up(MIRROR * FINE, 8)
MID_ROWS = round_up(FINE, 8)
SLAB_ROWS = 2 * PAIR_ROWS + MID_ROWS
FINE_C_ROWS = (PAIR_ROWS + MID_ROWS, PAIR_ROWS)
FINE_A_COUNT = (MIRROR + 1, MIRROR)


def class_fine_rows(cls):
    return round_up(FINE_A_COUNT[cls[0]] * FINE_C_ROWS[cls[1]], 16)


def legendre_pair(order, points):
    previous = points * 0.0 + 1.0
    current = points * 1.0
    for level in range(2, order + 1):
        previous, current = (
            current,
            ((2 * level - 1) * points * current - (level - 1) * previous) / level,
        )
    return (current, previous)


def make_tables():
    degree = LINE_POINT_TOTAL - 1
    gll_nodes = -np.cos(np.pi * np.arange(LINE_POINT_TOTAL) / degree)
    for repeat in range(100):
        current, previous = legendre_pair(degree, gll_nodes)
        gll_nodes = gll_nodes - (gll_nodes * current - previous) / (LINE_POINT_TOTAL * current)
    values, lower_values = legendre_pair(degree, gll_nodes)
    weights = 2.0 / (degree * (degree + 1) * values**2)
    spatial_derivative = np.zeros((LINE_POINT_TOTAL, LINE_POINT_TOTAL))
    for row_index in range(LINE_POINT_TOTAL):
        for column_index in range(LINE_POINT_TOTAL):
            if row_index != column_index:
                spatial_derivative[row_index, column_index] = values[row_index] / (
                    values[column_index] * (gll_nodes[row_index] - gll_nodes[column_index])
                )
    spatial_derivative[0, 0] = -degree * (degree + 1) / 4.0
    spatial_derivative[-1, -1] = degree * (degree + 1) / 4.0
    fine_nodes = -np.cos(np.pi * (np.arange(FINE) + 0.75) / (FINE + 0.5))
    for repeat in range(100):
        current, previous = legendre_pair(FINE, fine_nodes)
        slope = FINE * (fine_nodes * current - previous) / (fine_nodes * fine_nodes - 1.0)
        fine_nodes = fine_nodes - current / slope
    current, previous = legendre_pair(FINE, fine_nodes)
    slope = FINE * (fine_nodes * current - previous) / (fine_nodes * fine_nodes - 1.0)
    fine_weights = 2.0 / ((1.0 - fine_nodes * fine_nodes) * slope * slope)
    interpolation = np.ones((FINE, LINE_POINT_TOTAL))
    for column_index in range(LINE_POINT_TOTAL):
        for other_index in range(LINE_POINT_TOTAL):
            if other_index != column_index:
                interpolation[:, column_index] *= (fine_nodes - gll_nodes[other_index]) / (
                    gll_nodes[column_index] - gll_nodes[other_index]
                )
    stiffness_1d = spatial_derivative.T @ (weights[:, None] * spatial_derivative)
    return spatial_derivative, interpolation, stiffness_1d, weights, fine_weights


def parity_parts(matrix, out_rows, sign):
    near = matrix[:out_rows, :HALF]
    far = matrix[:out_rows, ::-1][:, :HALF]
    return (near + sign * far) * 0.5


def fine_matrix(cls, line_a, line_b, line_c):
    count_c = FINE_A_COUNT[cls[1]]
    full = np.einsum("xa,yc,zb->xyzacb", line_a, line_c, line_b)
    full = full.reshape(FINE_A_COUNT[cls[0]], count_c, FINE, CLASS_ROWS)
    slabs = np.zeros((FINE_A_COUNT[cls[0]], FINE_C_ROWS[cls[1]], CLASS_ROWS))
    slabs[:, : MIRROR * FINE] = full[:, :MIRROR].reshape(-1, MIRROR * FINE, CLASS_ROWS)
    if cls[1] == 0:
        slabs[:, PAIR_ROWS : PAIR_ROWS + FINE] = full[:, MIRROR]
    result = np.zeros((class_fine_rows(cls), CLASS_ROWS))
    result[: slabs.shape[0] * slabs.shape[1]] = slabs.reshape(-1, CLASS_ROWS)
    return result


def split_stack(matrix):
    high = matrix.astype(ml_dtypes.bfloat16)
    low = (matrix - high.astype(np.float64)).astype(ml_dtypes.bfloat16)
    return np.concatenate(
        [np.concatenate([high, high], 1), np.concatenate([low, low], 1)], 0
    )


def make_matrices():
    derivative, interpolation, stiffness, weights, fine_weights = make_tables()
    slope = interpolation @ derivative
    even = parity_parts(interpolation, MIRROR + 1, 1.0)
    odd = parity_parts(interpolation, MIRROR, -1.0)
    slope_even = parity_parts(slope, MIRROR + 1, -1.0)
    slope_odd = parity_parts(slope, MIRROR, 1.0)
    plain, steep = (even, odd), (slope_even, slope_odd)
    lifts = []
    for direction in (None, 0, 1, 2):
        for cls in CLASSES:
            line_a = (steep if direction == 0 else plain)[cls[0]]
            line_c = (steep if direction == 2 else plain)[cls[1]]
            line_b = slope if direction == 1 else interpolation
            lifts.append(split_stack(fine_matrix(cls, line_a, line_b, line_c)))
    backs = []
    for cls in CLASSES:
        lines = []
        for parity in cls:
            rows = FINE_A_COUNT[parity]
            lines.append(plain[parity] * fine_weights[:rows, None])
        backs.append(
            split_stack(
                fine_matrix(cls, lines[0], interpolation * fine_weights[:, None], lines[1]).T
            )
        )
    stiff = []
    for cls in CLASSES:
        parts = [
            parity_parts(stiffness, HALF, 1.0 - 2.0 * parity)[:HALF] for parity in cls
        ]
        mass = np.diag(weights[:HALF]) * 0.5
        total = (
            np.einsum("ij,kl,mn->ikmjln", parts[0], mass, np.diag(weights))
            + np.einsum("ij,kl,mn->ikmjln", mass, parts[1], np.diag(weights))
            + np.einsum("ij,kl,mn->ikmjln", mass, mass, stiffness)
        )
        stiff.append(split_stack(total.reshape(CLASS_ROWS, CLASS_ROWS)))
    return lifts, backs, stiff


def pair_of(here, shift, count):
    if count & (count - 1) == 0:
        return here ^ shift
    return (here + shift) % count


class Layout:
    def __init__(self, elements, sections):
        self.elements = elements
        self.sections = sections
        self.main = elements // sections
        self.slot = self.main + 2 * GHOST
        while (self.slot * sections) % LANES:
            self.slot += 1
        self.columns = self.slot * sections
        self.main_rows = POINTS // sections
        self.ghost_groups = elements // (2 * GHOST)
        self.ghost_rows = POINTS // self.ghost_groups
        self.end_groups = elements // GHOST
        self.end_rows = POINTS // self.end_groups
        apart = self.main + GHOST
        self.joint = apart % (2 * GHOST) == GHOST
        self.right_offset = apart if self.joint else GHOST

    def window_pieces(self, source, target, width):
        pieces = []
        done = 0
        while done < width:
            at, to = source + done, target + done
            step = min(width - done, LANES - at % LANES, LANES - to % LANES)
            first = to % LANES
            pieces.append((at // LANES, to // LANES, (to - at) % LANES, first, first + step))
            done += step
        return pieces


def lane_iota(rows):
    return lax.broadcasted_iota(jnp.int32, (rows, LANES), 1)


def in_range(lane, first, last):
    return (lane >= first) & (lane < last)


def turned(value, shift):
    if isinstance(shift, int) and shift % value.shape[-1] == 0:
        return value
    return pltpu.roll(value, shift, axis=1)


def reorder(temperature, velocity, ordered):
    for field in range(FIELDS):
        source = temperature if field == 0 else velocity.at[field - 1]
        for a in range(LINE_POINT_TOTAL):
            for c in range(LINE_POINT_TOTAL):
                base = a * 64 + c
                ordered[field, pl.ds((a * 8 + c) * 8, 8), :] = source[pl.ds(base, 8, stride=8), :]


def pack_main_kernel(layout, scalars, temperature, velocity, params, *rest):
    outs = rest[: layout.sections]
    low_end, high_end, ordered = rest[layout.sections :]
    reorder(temperature, velocity, ordered)
    here = scalars[0]
    elements, main, rows = layout.elements, layout.main, layout.main_rows
    lane = lane_iota(rows)
    for shift in range(layout.sections):
        there = pair_of(here, shift, layout.sections)
        for field in range(FIELDS):
            value = None
            for group in range(layout.sections):
                amount = lax.rem((group - there) * main + elements, elements)
                part = pltpu.roll(ordered[field, pl.ds(group * rows, rows), :], amount, axis=1)
                value = (
                    part
                    if value is None
                    else jnp.where(in_range(lane, group * main, (group + 1) * main), part, value)
                )
            outs[shift][pl.ds(field * rows, rows), :] = value
        outs[shift][pl.ds(FIELDS * rows, PARAM_ROWS), :] = pltpu.roll(
            params[...], lax.rem(elements - there * main, elements), axis=1
        )
    rows = layout.end_rows
    lane = lane_iota(rows)
    for out, first in ((low_end, 0), (high_end, elements - GHOST)):
        for field in range(FIELDS):
            value = None
            for group in range(layout.end_groups):
                part = turned(
                    ordered[field, pl.ds(group * rows, rows), :],
                    (group * GHOST - first) % elements,
                )
                value = (
                    part
                    if value is None
                    else jnp.where(in_range(lane, group * GHOST, (group + 1) * GHOST), part, value)
                )
            out[pl.ds(field * rows, rows), :] = value
        out[pl.ds(FIELDS * rows, PARAM_ROWS), :] = turned(params[...], (-first) % elements)


def pack_ghost_kernel(
    layout, scalars, ordered, params, from_low, from_high, *rest
):
    outs, edge = rest[: layout.sections], rest[layout.sections]
    here = scalars[0]
    elements, main, sections = layout.elements, layout.main, layout.sections
    rows = layout.end_rows
    lane = lane_iota(rows)
    for field in range(FIELDS):
        for group in range(layout.end_groups):
            low = turned(from_low[pl.ds(field * rows, rows), :], (-GHOST - group * GHOST) % elements)
            high = turned(from_high[pl.ds(field * rows, rows), :], (-group * GHOST) % elements)
            edge[field, pl.ds(group * rows, rows), :] = jnp.where(lane < elements // 2, high, low)
    low = turned(from_low[pl.ds(FIELDS * rows, PARAM_ROWS), :], elements - GHOST)
    high = from_high[pl.ds(FIELDS * rows, PARAM_ROWS), :]
    edge_params = jnp.where(lane_iota(PARAM_ROWS) < elements // 2, high, low)
    rows = layout.ghost_rows
    lane = lane_iota(rows)

    def gather(inner, outer, first, last, group, there, mask_lane, value):
        left = jnp.where(first, outer, inner)
        right = jnp.where(last, outer, inner)
        shift_left = lax.rem(2 * GHOST * group + GHOST - main * there + elements, elements)
        at_left = 2 * GHOST * group
        at_right = (2 * GHOST * group + layout.right_offset) % elements
        left_mask = in_range(mask_lane, at_left, at_left + GHOST)
        right_mask = in_range(mask_lane, at_right, at_right + GHOST)
        if layout.joint:
            source_lane = lax.rem(mask_lane - main * there + elements + GHOST, elements)
            both = jnp.where(source_lane < GHOST, left, right)
            part = pltpu.roll(both, shift_left, axis=1)
            return jnp.where(left_mask | right_mask, part, value)
        shift_right = lax.rem(
            2 * GHOST * group + layout.right_offset - main * (there + 1) + 2 * elements, elements
        )
        value = jnp.where(left_mask, pltpu.roll(left, shift_left, axis=1), value)
        return jnp.where(right_mask, pltpu.roll(right, shift_right, axis=1), value)

    for shift in range(sections):
        there = pair_of(here, shift, sections)
        first, last = there == 0, there == sections - 1
        for field in range(FIELDS):
            value = jnp.zeros((rows, LANES), jnp.float32)
            for group in range(layout.ghost_groups):
                span = pl.ds(group * rows, rows)
                value = gather(
                    ordered[field, span, :], edge[field, span, :], first, last, group, there, lane, value
                )
            outs[shift][pl.ds(field * rows, rows), :] = value
        outs[shift][pl.ds(FIELDS * rows, PARAM_ROWS), :] = gather(
            params[...],
            edge_params,
            first,
            last,
            0,
            there,
            lane_iota(PARAM_ROWS),
            jnp.zeros((PARAM_ROWS, LANES), jnp.float32),
        )


def unpack_columns(layout, mains, ghosts, fields, param_value):
    sections, main, slot = layout.sections, layout.main, layout.slot
    tiles = layout.columns // LANES

    def moves(section, group, ghost):
        if not ghost:
            return layout.window_pieces(group * main, section * slot + GHOST, main)
        at_left = 2 * GHOST * group
        at_right = (at_left + layout.right_offset) % layout.elements
        return layout.window_pieces(at_left, section * slot, GHOST) + layout.window_pieces(
            at_right, section * slot + GHOST + main, GHOST
        )

    def fill(sources, rows, first_row, group, ghost, values):
        lane = lane_iota(rows)
        for section in range(sections):
            block = sources[section][pl.ds(first_row, rows), :]
            cache = {}
            for _, tile, shift, first, last in moves(section, group, ghost):
                if shift not in cache:
                    cache[shift] = turned(block, shift)
                mask = in_range(lane, first, last)
                values[tile] = jnp.where(mask, cache[shift], values[tile])
        return values

    def zeros(rows):
        return [jnp.zeros((rows, LANES), jnp.float32) for _ in range(tiles)]

    rows = min(layout.main_rows, layout.ghost_rows)
    for field in range(FIELDS):
        for start in range(0, POINTS, rows):
            group, offset = divmod(start, layout.main_rows)
            values = fill(
                mains, rows, field * layout.main_rows + offset, group, False, zeros(rows)
            )
            group, offset = divmod(start, layout.ghost_rows)
            values = fill(
                ghosts, rows, field * layout.ghost_rows + offset, group, True, values
            )
            for tile in range(tiles):
                fields[field, pl.ds(start, rows), pl.ds(tile * LANES, LANES)] = values[tile]
    values = fill(mains, PARAM_ROWS, FIELDS * layout.main_rows, 0, False, zeros(PARAM_ROWS))
    values = fill(ghosts, PARAM_ROWS, FIELDS * layout.ghost_rows, 0, True, values)
    for tile in range(tiles):
        param_value[:, pl.ds(tile * LANES, LANES)] = values[tile]


def store_split(target, row, half, value):
    high = value.astype(jnp.bfloat16)
    target[pl.ds(row, value.shape[0]), :] = high
    target[pl.ds(half + row, value.shape[0]), :] = (value - high.astype(jnp.float32)).astype(
        jnp.bfloat16
    )


def to_classes(source, pieces):
    for a in range(HALF):
        near = source[pl.ds(a * 64, 64), :]
        far = source[pl.ds((LINE_POINT_TOTAL - 1 - a) * 64, 64), :]
        for parity_a, slab in enumerate((near + far, near - far)):
            lower = slab[: HALF * 8]
            upper = jnp.concatenate(
                [slab[(LINE_POINT_TOTAL - 1 - c) * 8 :][:8] for c in range(HALF)], 0
            )
            for parity_c, part in enumerate((lower + upper, lower - upper)):
                store_split(pieces[2 * parity_a + parity_c], a * HALF * 8, CLASS_ROWS, part)


def multiply(matrix, pieces):
    product = jnp.dot(matrix[...], pieces[...], preferred_element_type=jnp.float32)
    half = product.shape[0] // 2
    return product[:half] + product[half:]


def from_classes(results, a):
    span = pl.ds(a * HALF * 8, HALF * 8)
    ee, eo, oe, oo = [results[index, span, :] for index in range(4)]

    def along_c(even, odd):
        lower, upper = even + odd, even - odd
        return jnp.concatenate(
            [lower] + [upper[c * 8 : c * 8 + 8] for c in reversed(range(HALF))], 0
        )

    return along_c(ee + oe, eo + oo), along_c(ee - oe, eo - oo)


def fine_slabs(fine, q):
    halves = []
    for parity_a in range(2):
        if q >= FINE_A_COUNT[parity_a]:
            break
        even = fine[2 * parity_a][pl.ds(q * FINE_C_ROWS[0], FINE_C_ROWS[0]), :]
        odd = fine[2 * parity_a + 1][pl.ds(q * FINE_C_ROWS[1], FINE_C_ROWS[1]), :]
        halves.append((even[:PAIR_ROWS] + odd, even[:PAIR_ROWS] - odd, even[PAIR_ROWS:]))
    if len(halves) == 1:
        return [halves[0]]
    return [
        tuple(x + y for x, y in zip(*halves)),
        tuple(x - y for x, y in zip(*halves)),
    ]


def main_kernel(layout, tables, *refs):
    weights = tables[3]
    sections, columns = layout.sections, layout.columns
    refs = list(refs)

    def take(count):
        taken, refs[:] = refs[:count], refs[count:]
        return taken

    mains, ghosts = take(sections), take(sections)
    lifts, backs, stiff = take(16), take(4), take(4)
    outs = take(sections)
    fields, param_value = take(2)
    fine = [take(4) for _ in range(3)]
    (lifted, point_pieces, results, keep, gain_rhs, gain_k, gain) = take(7)
    (gain_low, gain_high, gain_wall) = take(3)
    fine_pieces = take(4)
    pieces = [point_pieces.at[index] for index in range(4)]

    unpack_columns(layout, mains, ghosts, fields, param_value)

    params = param_value[...]
    k, metal, partner, has_low, has_high = [params[row : row + 1] for row in range(5)]

    def shifted(value, amount):
        return pltpu.roll(value, amount % columns, axis=1)

    lane = lax.broadcasted_iota(jnp.int32, (1, columns), 1)
    own_slot = lane // layout.slot
    partner_slot = pair_of(own_slot, partner.astype(jnp.int32), sections)
    distance = lax.rem(partner_slot - own_slot + sections, sections)
    coef_low = has_low * (0.5 * penalty) * (k + shifted(k, 1))
    coef_high = has_high * (0.5 * penalty) * (k + shifted(k, -1))
    partner_k, partner_metal = jnp.zeros_like(k), jnp.zeros_like(k)
    for step in range(1, sections):
        chosen = distance == step
        partner_k = jnp.where(chosen, shifted(k, -step * layout.slot), partner_k)
        partner_metal = jnp.where(chosen, shifted(metal, -step * layout.slot), partner_metal)
    coef_wall = jnp.where(metal != partner_metal, (0.5 * penalty) * (k + partner_k), 0.0)
    fluid = 1.0 - metal

    row = lax.broadcasted_iota(jnp.int32, (8, columns), 0)
    weight_b = jnp.zeros((8, columns), jnp.float32)
    stiff_b = jnp.zeros((8, columns), jnp.float32)
    stiff_line = np.diagonal(tables[2])
    for b in range(8):
        weight_b = jnp.where(row == b, float(weights[b]), weight_b)
        stiff_b = jnp.where(row == b, float(stiff_line[b]), stiff_b)
    last = LINE_POINT_TOTAL - 1
    for a in range(LINE_POINT_TOTAL):
        for c in range(LINE_POINT_TOTAL):
            wa, wc = float(weights[a]), float(weights[c])
            mass = weight_b * (wa * wc / time_step)
            diag = mass + k * (
                weight_b * (float(stiff_line[a]) * wc + wa * float(stiff_line[c]))
                + stiff_b * (wa * wc)
            )
            face = None
            if a == 0:
                face_low = coef_low * (weight_b * wc)
                face = face_low
            if a == last:
                face_high = coef_high * (weight_b * wc)
                face = face_high
            if c == 0:
                face_wall = coef_wall * (weight_b * wa)
                face = face_wall if face is None else face + face_wall
            if face is not None:
                diag = diag + face
            factor = relaxation / diag
            span = pl.ds((a * 8 + c) * 8, 8)
            gain[span, :] = factor
            gain_k[span, :] = factor * k
            keep[span, :] = 1.0 - factor * (mass if face is None else mass + face)
            if a == 0:
                gain_low[pl.ds(c * 8, 8), :] = factor * face_low
            if a == last:
                gain_high[pl.ds(c * 8, 8), :] = factor * face_high
            if c == 0:
                gain_wall[pl.ds(a * 8, 8), :] = factor * face_wall

    for direction in range(3):
        to_classes(fields.at[direction + 1], pieces)
        for index in range(4):
            fine[0][index][...] = multiply(lifts[index], pieces[index])
        for q in range(MIRROR + 1):
            for point, slab in zip((q, FINE - 1 - q), fine_slabs(fine[0], q)):
                base = 0
                for part in slab:
                    lifted[direction, point, pl.ds(base, part.shape[0]), :] = part
                    base += part.shape[0]

    iterate = fields.at[0]
    for step_index in range(STEPS):
        to_classes(iterate, pieces)
        for direction in range(3):
            for index, cls in enumerate(CLASSES):
                source = index ^ (2 if direction == 0 else 1 if direction == 2 else 0)
                fine[direction][index][...] = multiply(
                    lifts[4 * (direction + 1) + index], pieces[source]
                )
        pending = [[], [], [], []]
        done = [0, 0, 0, 0]
        for q in range(MIRROR + 1):
            products = None
            for direction in range(3):
                slabs = fine_slabs(fine[direction], q)
                terms = []
                for point, slab in zip((q, FINE - 1 - q), slabs):
                    base = 0
                    parts = []
                    for part in slab:
                        parts.append(
                            part * lifted[direction, point, pl.ds(base, part.shape[0]), :]
                        )
                        base += part.shape[0]
                    terms.append(parts)
                products = (
                    terms
                    if products is None
                    else [[x + y for x, y in zip(s, t)] for s, t in zip(products, terms)]
                )
            if len(products) == 2:
                halves = [
                    [x + y for x, y in zip(*products)],
                    [x - y for x, y in zip(*products)],
                ]
            else:
                halves = products
            for parity_a, (plus, minus, middle) in enumerate(halves):
                pending[2 * parity_a] += [plus + minus, middle]
                pending[2 * parity_a + 1].append(plus - minus)
            for index, cls in enumerate(CLASSES):
                held = sum(part.shape[0] for part in pending[index])
                final = q >= FINE_A_COUNT[cls[0]] - 1
                if pending[index] and (held % 16 == 0 or final):
                    if held % 16:
                        pending[index].append(jnp.zeros((8, columns), jnp.float32))
                        held += 8
                    store_split(
                        fine_pieces[index],
                        done[index],
                        class_fine_rows(cls),
                        jnp.concatenate(pending[index], 0),
                    )
                    done[index] += held
                    pending[index] = []
        for index in range(4):
            results[index] = multiply(backs[index], fine_pieces[index])
        for a in range(HALF):
            for plane, convected in zip((a, last - a), from_classes(results, a)):
                for c in range(LINE_POINT_TOTAL):
                    span = pl.ds((plane * 8 + c) * 8, 8)
                    mass = weight_b * float(weights[plane] * weights[c] / time_step)
                    gain_rhs[span, :] = gain[span, :] * (
                        mass * iterate[span, :] - fluid * convected[c * 8 : c * 8 + 8]
                    )
        for sweep_index in range(SWEEPS):
            if sweep_index > 0:
                to_classes(iterate, pieces)
            for index in range(4):
                results[index] = multiply(stiff[index], pieces[index])
            from_low = gain_low[...] * shifted(iterate[pl.ds(last * 64, 64), :], 1)
            from_high = gain_high[...] * shifted(iterate[pl.ds(0, 64), :], -1)
            wall = jnp.concatenate([iterate[pl.ds(a * 64, 8), :] for a in range(8)], 0)
            far = jnp.zeros_like(wall)
            for step in range(1, sections):
                far = jnp.where(distance == step, shifted(wall, -step * layout.slot), far)
            from_wall = gain_wall[...] * far
            for a in range(HALF):
                for plane, stiffness in zip((a, last - a), from_classes(results, a)):
                    span = pl.ds(plane * 64, 64)
                    value = (
                        keep[span, :] * iterate[span, :]
                        + gain_rhs[span, :]
                        - gain_k[span, :] * stiffness
                    )
                    if plane == 0:
                        value = value + from_low
                    if plane == last:
                        value = value + from_high
                    at_wall = value[:8] + from_wall[plane * 8 : plane * 8 + 8]
                    iterate[span, :] = jnp.concatenate([at_wall, value[8:]], 0)

    rows = layout.main_rows
    lane = lane_iota(rows)
    for section in range(sections):
        value = jnp.zeros((rows, LANES), jnp.float32)
        for group in range(sections):
            for tile, _, shift, first, last_lane in layout.window_pieces(
                section * layout.slot + GHOST, group * layout.main, layout.main
            ):
                block = iterate[pl.ds(group * rows, rows), pl.ds(tile * LANES, LANES)]
                value = jnp.where(in_range(lane, first, last_lane), turned(block, shift), value)
        outs[section][...] = value


def gather_kernel(layout, scalars, *refs):
    chunks, out = refs[: layout.sections], refs[layout.sections]
    here = scalars[0]
    rows, main, elements = layout.main_rows, layout.main, layout.elements
    lane = lane_iota(rows)
    places = [pair_of(here, shift, layout.sections) for shift in range(layout.sections)]
    for group in range(layout.sections):
        value = None
        for shift, there in enumerate(places):
            amount = lax.rem((there - group) * main + elements, elements)
            part = pltpu.roll(chunks[shift][...], amount, axis=1)
            value = (
                part
                if value is None
                else jnp.where(in_range(lane, there * main, (there + 1) * main), part, value)
            )
        for index in range(rows // 8):
            a, c = divmod(group * (rows // 8) + index, LINE_POINT_TOTAL)
            out[pl.ds(a * 64 + c, 8, stride=8), :] = value[index * 8 : index * 8 + 8]


def shape_of(*dims, dtype=jnp.float32):
    return jax.ShapeDtypeStruct(dims, dtype)


def in_vmem(count):
    return [pl.BlockSpec(memory_space=pltpu.VMEM)] * count


SCALAR = pl.BlockSpec(memory_space=pltpu.SMEM)
PARAMS = pltpu.CompilerParams(vmem_limit_bytes=48 * 1024 * 1024)


def body(
    thermal_level_points,
    flow_speed_vector,
    thermal_diffusivity_cell,
    metal_cell_indicator,
    adjoining_patch,
):
    sections = lax.axis_size("sec")
    blocks = lax.axis_size("elem")
    elements = thermal_diffusivity_cell.shape[1]
    layout = Layout(elements, sections)
    here = lax.axis_index("sec").astype(jnp.int32)
    scalars = here[None]
    position = lax.axis_index("elem") * elements + lax.iota(jnp.int32, elements)
    if sections & (sections - 1) == 0:
        relative = adjoining_patch[0] ^ here
    else:
        relative = (adjoining_patch[0] - here) % sections
    params = jnp.stack(
        [
            thermal_diffusivity_cell[0],
            metal_cell_indicator[0].astype(jnp.float32),
            relative.astype(jnp.float32),
            (position > 0).astype(jnp.float32),
            (position < elements * blocks - 1).astype(jnp.float32),
        ]
        + [jnp.zeros((elements,), jnp.float32)] * (PARAM_ROWS - 5),
        0,
    )
    temperature = thermal_level_points.reshape(POINTS, elements)
    velocity = flow_speed_vector.reshape(3, POINTS, elements)

    main_shape = shape_of(FIELDS * layout.main_rows + PARAM_ROWS, elements)
    ghost_shape = shape_of(FIELDS * layout.ghost_rows + PARAM_ROWS, elements)
    end_shape = shape_of(FIELDS * layout.end_rows + PARAM_ROWS, elements)
    packed = pl.pallas_call(
        functools.partial(pack_main_kernel, layout),
        out_shape=[main_shape] * sections + [end_shape] * 2 + [shape_of(FIELDS, POINTS, elements)],
        in_specs=[SCALAR] + in_vmem(3),
        out_specs=in_vmem(sections + 3),
        compiler_params=PARAMS,
        name="pack_main",
    )(scalars, temperature, velocity, params)
    mains, (low_end, high_end, ordered) = packed[:sections], packed[sections:]

    def swap(arrays):
        received = [arrays[0]]
        for shift in range(1, sections):
            pairs = [(i, pair_of(i, shift, sections)) for i in range(sections)]
            received.append(lax.ppermute(arrays[shift], "sec", pairs))
        if sections & (sections - 1):
            received[1:] = received[:0:-1]
        return received

    mains = swap(mains)
    forward = [(i, i + 1) for i in range(blocks - 1)]
    from_low = lax.ppermute(high_end, "elem", forward)
    from_high = lax.ppermute(low_end, "elem", [(i, j) for j, i in forward])
    ghosts = pl.pallas_call(
        functools.partial(pack_ghost_kernel, layout),
        out_shape=[ghost_shape] * sections,
        in_specs=[SCALAR] + in_vmem(4),
        out_specs=in_vmem(sections),
        scratch_shapes=[pltpu.VMEM((FIELDS, POINTS, elements), jnp.float32)],
        compiler_params=PARAMS,
        name="pack_ghost",
    )(scalars, ordered, params, from_low, from_high)
    ghosts = swap(ghosts)

    lifts, backs, stiff = make_matrices()
    columns = layout.columns
    matrices = [jnp.asarray(matrix) for matrix in lifts + backs + stiff]
    fine_rows = [class_fine_rows(cls) for cls in CLASSES]
    f32, bf16 = jnp.float32, jnp.bfloat16
    chunks = pl.pallas_call(
        functools.partial(main_kernel, layout, make_tables()),
        out_shape=[shape_of(layout.main_rows, elements)] * sections,
        in_specs=in_vmem(2 * sections + len(matrices)),
        out_specs=in_vmem(sections),
        scratch_shapes=[
            pltpu.VMEM((FIELDS, POINTS, columns), f32),
            pltpu.VMEM((PARAM_ROWS, columns), f32),
            *[pltpu.VMEM((rows, columns), f32) for _ in range(3) for rows in fine_rows],
            pltpu.VMEM((3, FINE, SLAB_ROWS, columns), f32),
            pltpu.VMEM((4, 2 * CLASS_ROWS, columns), bf16),
            pltpu.VMEM((4, CLASS_ROWS, columns), f32),
            *[pltpu.VMEM((POINTS, columns), f32) for _ in range(4)],
            *[pltpu.VMEM((64, columns), f32) for _ in range(3)],
            *[pltpu.VMEM((2 * rows, columns), bf16) for rows in fine_rows],
        ],
        compiler_params=PARAMS,
        name="march",
    )(*mains, *ghosts, *matrices)
    chunks = swap(chunks)
    result = pl.pallas_call(
        functools.partial(gather_kernel, layout),
        out_shape=shape_of(POINTS, elements),
        in_specs=[SCALAR] + in_vmem(sections),
        out_specs=pl.BlockSpec(memory_space=pltpu.VMEM),
        compiler_params=PARAMS,
        name="unpack",
    )(scalars, *chunks)
    return result.reshape(thermal_level_points.shape)


def solution(mesh):
    return jax.shard_map(
        body,
        mesh=mesh,
        in_specs=(
            P("sec", None, None, None, "elem"),
            P(None, "sec", None, None, None, "elem"),
            P("sec", "elem"),
            P("sec", "elem"),
            P("sec", "elem"),
        ),
        out_specs=P("sec", None, None, None, "elem"),
        check_vma=False,
    )
```

time: 213 us -> 66.3 us (0.31)
  the two profiles are of different devices: /device:TPU:5 before, /device:TPU:0 now
where the time goes in v1:
time: 66.3 us; the launch traced here: 65.8 us
  waiting for transfers between devices  24.8 us (37%)
  Pallas kernels  16.7 us (25%)
  starting transfers between devices  12.5 us (19%)
  local copies, waits for them, and re-layouts  11.6 us (17%)
    ppermute x9, waiting for transfers between devices, swap(): received.append(lax.ppermute(arrays[shift], 'sec', pairs))  19.9 us
    pallas_call x1, Pallas kernels, body(): pl.pallas_call(functools.partial(main_kernel, layout, make_tables()), out...  12.3 us
    unnamed x40, local copies, waits for them, and re-layouts  11.6 us
    ppermute x9, starting transfers between devices, swap(): received.append(lax.ppermute(arrays[shift], 'sec', pairs))  6.3 us
    ppermute x1, starting transfers between devices, body(): from_low = lax.ppermute(high_end, 'elem', forward)  4.87 us
    ppermute x1, waiting for transfers between devices, body(): from_high = lax.ppermute(low_end, 'elem', [(i, j) for j, i in forward])  4.28 us
    pallas_call x1, Pallas kernels, body(): pl.pallas_call(functools.partial(pack_main_kernel, layout), out_shape=[ma...  1.7 us
    pallas_call x1, Pallas kernels, body(): pl.pallas_call(functools.partial(pack_ghost_kernel, layout), out_shape=[g...  1.69 us
  transfers between devices with their start and end apart: 11, of which 6 were waited for; matrix products, arithmetic and copies ran while one was open for 0% of the time, Pallas kernels for 0%

profile of v1, /device:TPU:0, one launch (start us, length us, event | category | flops | bytes accessed | tf_op | source)
XLA Modules:
  0.0 65.8 jit_solution(9984292307597890649)
XLA Ops:
  2.0 1.1 %copy-done = f32[3,1,8,8,8,128]{5,4,3,2,1,0:T(8,128)S(1)} copy-done((f32[3,1,8,8,8,128]{5,4,3,2,1,0:T(8,128)S(1)}, f32[3,1,8,8,8,128]{5,4,3,2,1,0:T(8,128)}, u32[]{:S(2)}) %copy-start) | copy-done | bytes 786456
  3.1 0.9 %copy-done.12 = f32[1,8,8,8,128]{4,3,2,1,0:T(8,128)S(1)} copy-done((f32[1,8,8,8,128]{4,3,2,1,0:T(8,128)S(1)}, f32[1,8,8,8,128]{4,3,2,1,0:T(8,128)}, u32[]{:S(2)}) %copy-start.12) | copy-done | bytes 262168
  4.1 1.7 %pack_main.1 = (f32[520,128]{1,0:T(8,128)S(1)}, f32[520,128]{1,0:T(8,128)S(1)}, f32[520,128]{1,0:T(8,128)S(1)}, f32[520,128]{1,0:T(8,128)S(1)}, f32[136,128]{1,0...) custom-call(s32[1]{0:T(128)} %bitcast.scalars, f32[512,128]{1,0:T(8,128)S(1)} %bitcast.5, ...), custom_call_target="tpu_custom_call" | custom-call | tf_op jit(solution)/shard_map/pack_main/pallas_call | solution.py:692
  5.8 4.9 %collective-permute-start.3 = (f32[136,128]{1,0:T(8,128)S(1)}, f32[136,128]{1,0:T(8,128)S(1)}, u32[]{:S(2)}, u32[]{:S(2)}) collective-permute-start(f32[136,128]{1,0:T(8,128)S(1)} %get-tuple-element.25), channel_id=1, source_target_pairs={{0,1},{1,2},{2,3},{3,4},{4,5},{5,6},{6,7},{8,9},{9,10},{10,11},{11... | collective-permute-start | bytes 208904 | tf_op jit(solution)/shard_map/ppermute | solution.py:713
  10.7 1.3 %collective-permute-start.4 = (f32[136,128]{1,0:T(8,128)S(1)}, f32[136,128]{1,0:T(8,128)S(1)}, u32[]{:S(2)}, u32[]{:S(2)}) collective-permute-start(f32[136,128]{1,0:T(8,128)S(1)} %get-tuple-element.26), channel_id=1, source_target_pairs={{1,0},{2,1},{3,2},{4,3},{5,4},{6,5},{7,6},{9,8},{10,9},{11,10},{12... | collective-permute-start | bytes 208904 | tf_op jit(solution)/shard_map/ppermute | solution.py:714
  12.6 4.3 %collective-permute-done.4.from_high = f32[136,128]{1,0:T(8,128)S(1)} collective-permute-done((f32[136,128]{1,0:T(8,128)S(1)}, f32[136,128]{1,0:T(8,128)S(1)}, u32[]{:S(2)}, u32[]{:S(2)}) %collective-permute-start.4) | collective-permute-done | bytes 69664 | tf_op jit(solution)/shard_map/ppermute | solution.py:714
  16.9 1.7 %pack_ghost.1 = (f32[264,128]{1,0:T(8,128)S(1)}, f32[264,128]{1,0:T(8,128)S(1)}, f32[264,128]{1,0:T(8,128)S(1)}, f32[264,128]{1,0:T(8,128)S(1)}) custom-call(s32[1]{0:T(128)} %bitcast.scalars, f32[4,512,128]{2,1,0:T(8,128)S(1)} %get-tuple-element.24.ordered, f32[8,128]{1,0:T(8,128)S(1)} %stack.5.params, f32[136,128]{1,0:T(8,128)S(1)} %collective-permute-done.3.from_low, ...), custom_call_target="tpu_custom_call" | custom-call | tf_op jit(solution)/shard_map/pack_ghost/pallas_call | solution.py:715
  19.2 1.5 %collective-permute-start.1 = (f32[520,128]{1,0:T(8,128)S(1)}, f32[520,128]{1,0:T(8,128)S(1)}, u32[]{:S(2)}, u32[]{:S(2)}) collective-permute-start(f32[520,128]{1,0:T(8,128)S(1)} %get-tuple-element.22), channel_id=1, source_target_pairs={{0,16},{8,24},{16,0},{24,8},{1,17},{9,25},{17,1},{25,9},{2,18},{10... | collective-permute-start | bytes 798728 | tf_op jit(solution)/shard_map/ppermute | solution.py:706
  20.7 1.4 %collective-permute-start.6 = (f32[264,128]{1,0:T(8,128)S(1)}, f32[264,128]{1,0:T(8,128)S(1)}, u32[]{:S(2)}, u32[]{:S(2)}) collective-permute-start(f32[264,128]{1,0:T(8,128)S(1)} %get-tuple-element.29), channel_id=1, source_target_pairs={{0,16},{8,24},{16,0},{24,8},{1,17},{9,25},{17,1},{25,9},{2,18},{10... | collective-permute-start | bytes 405512 | tf_op jit(solution)/shard_map/ppermute | solution.py:706
  22.7 14.4 %collective-permute-done.6.refs_6_ = f32[264,128]{1,0:T(8,128)S(1)} collective-permute-done((f32[264,128]{1,0:T(8,128)S(1)}, f32[264,128]{1,0:T(8,128)S(1)}, u32[]{:S(2)}, u32[]{:S(2)}) %collective-permute-start.6) | collective-permute-done | bytes 135200 | tf_op jit(solution)/shard_map/ppermute | solution.py:706
  37.0 1.1 %collective-permute-done.7.refs_7_ = f32[264,128]{1,0:T(8,128)S(1)} collective-permute-done((f32[264,128]{1,0:T(8,128)S(1)}, f32[264,128]{1,0:T(8,128)S(1)}, u32[]{:S(2)}, u32[]{:S(2)}) %collective-permute-start.7) | collective-permute-done | bytes 135200 | tf_op jit(solution)/shard_map/ppermute | solution.py:706
  38.3 1.0 %copy-done.7 = bf16[256,576]{1,0:T(8,128)(2,1)S(1)} copy-done((bf16[256,576]{1,0:T(8,128)(2,1)S(1)}, bf16[256,576]{1,0:T(8,128)(2,1)}, u32[]{:S(2)}) %copy-start.7) | copy-done | bytes 294936
  39.2 1.0 %copy-done.8 = bf16[576,256]{1,0:T(8,128)(2,1)S(1)} copy-done((bf16[576,256]{1,0:T(8,128)(2,1)S(1)}, bf16[576,256]{1,0:T(8,128)(2,1)}, u32[]{:S(2)}) %copy-start.8) | copy-done | bytes 294936
  40.2 1.0 %copy-done.9 = bf16[576,256]{1,0:T(8,128)(2,1)S(1)} copy-done((bf16[576,256]{1,0:T(8,128)(2,1)S(1)}, bf16[576,256]{1,0:T(8,128)(2,1)}, u32[]{:S(2)}) %copy-start.9) | copy-done | bytes 294936
  41.2 1.0 %copy-done.10 = bf16[576,256]{1,0:T(8,128)(2,1)S(1)} copy-done((bf16[576,256]{1,0:T(8,128)(2,1)S(1)}, bf16[576,256]{1,0:T(8,128)(2,1)}, u32[]{:S(2)}) %copy-start.10) | copy-done | bytes 294936
  42.1 1.0 %copy-done.11 = bf16[576,256]{1,0:T(8,128)(2,1)S(1)} copy-done((bf16[576,256]{1,0:T(8,128)(2,1)S(1)}, bf16[576,256]{1,0:T(8,128)(2,1)}, u32[]{:S(2)}) %copy-start.11) | copy-done | bytes 294936
  43.1 0.9 %copy-done.14 = bf16[256,256]{1,0:T(8,128)(2,1)S(1)} copy-done((bf16[256,256]{1,0:T(8,128)(2,1)S(1)}, bf16[256,256]{1,0:T(8,128)(2,1)}, u32[]{:S(2)}) %copy-start.14) | copy-done | bytes 131096
  44.0 0.9 %copy-done.15 = bf16[256,256]{1,0:T(8,128)(2,1)S(1)} copy-done((bf16[256,256]{1,0:T(8,128)(2,1)S(1)}, bf16[256,256]{1,0:T(8,128)(2,1)}, u32[]{:S(2)}) %copy-start.15) | copy-done | bytes 131096
  44.9 0.9 %copy-done.16 = bf16[256,256]{1,0:T(8,128)(2,1)S(1)} copy-done((bf16[256,256]{1,0:T(8,128)(2,1)S(1)}, bf16[256,256]{1,0:T(8,128)(2,1)}, u32[]{:S(2)}) %copy-start.16) | copy-done | bytes 131096
  45.8 12.3 %march.1 = (f32[128,128]{1,0:T(8,128)S(1)}, f32[128,128]{1,0:T(8,128)S(1)}, f32[128,128]{1,0:T(8,128)S(1)}, f32[128,128]{1,0:T(8,128)S(1)}) custom-call(f32[520,128]{1,0:T(8,128)S(1)} %get-tuple-element.20.refs_0_, f32[520,128]{1,0:T(8,128)S(1)} %collective-permute-done.refs_1_, f32[520,128]{1,0:T(8,128)S(1)} %collective-permute-done.1.refs_2_, ...), custom_call_target="tpu_custom_call" | custom-call | tf_op jit(solution)/shard_map/march/pallas_call | solution.py:731
  58.9 1.5 %collective-permute-start.9 = (f32[128,128]{1,0:T(8,128)S(1)}, f32[128,128]{1,0:T(8,128)S(1)}, u32[]{:S(2)}, u32[]{:S(2)}) collective-permute-start(f32[128,128]{1,0:T(8,128)S(1)} %get-tuple-element.33), channel_id=1, source_target_pairs={{0,16},{8,24},{16,0},{24,8},{1,17},{9,25},{17,1},{25,9},{2,18},{10... | collective-permute-start | bytes 196616 | tf_op jit(solution)/shard_map/ppermute | solution.py:706
  60.4 2.8 %collective-permute-done.9.refs_2_ = f32[128,128]{1,0:T(8,128)S(1)} collective-permute-done((f32[128,128]{1,0:T(8,128)S(1)}, f32[128,128]{1,0:T(8,128)S(1)}, u32[]{:S(2)}, u32[]{:S(2)}) %collective-permute-start.9) | collective-permute-done | bytes 65568 | tf_op jit(solution)/shard_map/ppermute | solution.py:706
  63.1 1.6 %collective-permute-done.10.refs_3_ = f32[128,128]{1,0:T(8,128)S(1)} collective-permute-done((f32[128,128]{1,0:T(8,128)S(1)}, f32[128,128]{1,0:T(8,128)S(1)}, u32[]{:S(2)}, u32[]{:S(2)}) %collective-permute-start.10) | collective-permute-done | bytes 65568 | tf_op jit(solution)/shard_map/ppermute | solution.py:706
  64.7 1.0 %unpack.1 = f32[512,128]{1,0:T(8,128)} custom-call(s32[1]{0:T(128)} %bitcast.scalars, f32[128,128]{1,0:T(8,128)S(1)} %get-tuple-element.31.refs_0_, f32[128,128]{1,0:T(8,128)S(1)} %collective-permute-done.8.refs_1_, f32[128,128]{1,0:T(8,128)S(1)} %collective-permute-done.9.refs_2_, f32[128,128]{1,0:T(8,128)S(1)} %collective-permute-done.10.refs_3_), custom_call_target="tpu_custom_call" | custom-call | tf_op jit(solution)/shard_map/unpack/pallas_call | solution.py:751
  (48 shorter events, 4.6 us)
Async XLA Ops:
  2.0 1.1 %copy-start = (f32[3,1,8,8,8,128]{5,4,3,2,1,0:T(8,128)S(1)}, f32[3,1,8,8,8,128]{5,4,3,2,1,0:T(8,128)}, u32[]{:S(2)}) copy-start(f32[3,1,8,8,8,128]{5,4,3,2,1,0:T(8,128)} %param.30) | copy-start | bytes 2359300
  4.1 34.1 %copy-start.4 = (bf16[672,256]{1,0:T(8,128)(2,1)S(1)}, bf16[672,256]{1,0:T(8,128)(2,1)}, u32[]{:S(2)}) copy-start(bf16[672,256]{1,0:T(8,128)(2,1)} %constant.74.clone.refs_17_) | copy-start | bytes 1032196
  4.1 34.1 %copy-start.5 = (bf16[672,256]{1,0:T(8,128)(2,1)S(1)}, bf16[672,256]{1,0:T(8,128)(2,1)}, u32[]{:S(2)}) copy-start(bf16[672,256]{1,0:T(8,128)(2,1)} %constant.70.clone.refs_13_) | copy-start | bytes 1032196
  4.1 34.1 %copy-start.6 = (bf16[672,256]{1,0:T(8,128)(2,1)S(1)}, bf16[672,256]{1,0:T(8,128)(2,1)}, u32[]{:S(2)}) copy-start(bf16[672,256]{1,0:T(8,128)(2,1)} %constant.66.clone.refs_9_) | copy-start | bytes 1032196
  4.1 34.1 %copy-start.13 = (bf16[256,256]{1,0:T(8,128)(2,1)S(1)}, bf16[256,256]{1,0:T(8,128)(2,1)}, u32[]{:S(2)}) copy-start(bf16[256,256]{1,0:T(8,128)(2,1)} %constant.88.clone.refs_31_) | copy-start | bytes 393220
  5.8 6.8 %collective-permute-start.3 = (f32[136,128]{1,0:T(8,128)S(1)}, f32[136,128]{1,0:T(8,128)S(1)}, u32[]{:S(2)}, u32[]{:S(2)}) collective-permute-start(f32[136,128]{1,0:T(8,128)S(1)} %get-tuple-element.25), channel_id=1, source_target_pairs={{0,1},{1,2},{2,3},{3,4},{4,5},{5,6},{6,7},{8,9},{9,10},{10,11},{11... | collective-permute-start | bytes 208904 | tf_op jit(solution)/shard_map/ppermute | solution.py:713
  10.7 6.2 %collective-permute-start.4 = (f32[136,128]{1,0:T(8,128)S(1)}, f32[136,128]{1,0:T(8,128)S(1)}, u32[]{:S(2)}, u32[]{:S(2)}) collective-permute-start(f32[136,128]{1,0:T(8,128)S(1)} %get-tuple-element.26), channel_id=1, source_target_pairs={{1,0},{2,1},{3,2},{4,3},{5,4},{6,5},{7,6},{9,8},{10,9},{11,10},{12... | collective-permute-start | bytes 208904 | tf_op jit(solution)/shard_map/ppermute | solution.py:714
  16.9 21.3 %copy-start.1 = (bf16[736,256]{1,0:T(8,128)(2,1)S(1)}, bf16[736,256]{1,0:T(8,128)(2,1)}, u32[]{:S(2)}) copy-start(bf16[736,256]{1,0:T(8,128)(2,1)} %constant.71.clone.refs_14_) | copy-start | bytes 1130500
  16.9 21.3 %copy-start.2 = (bf16[736,256]{1,0:T(8,128)(2,1)S(1)}, bf16[736,256]{1,0:T(8,128)(2,1)}, u32[]{:S(2)}) copy-start(bf16[736,256]{1,0:T(8,128)(2,1)} %constant.67.clone.refs_10_) | copy-start | bytes 1130500
  16.9 21.4 %copy-start.3 = (bf16[672,256]{1,0:T(8,128)(2,1)S(1)}, bf16[672,256]{1,0:T(8,128)(2,1)}, u32[]{:S(2)}) copy-start(bf16[672,256]{1,0:T(8,128)(2,1)} %constant.78.clone.refs_21_) | copy-start | bytes 1032196
  18.6 3.5 %collective-permute-start.5 = (f32[264,128]{1,0:T(8,128)S(1)}, f32[264,128]{1,0:T(8,128)S(1)}, u32[]{:S(2)}, u32[]{:S(2)}) collective-permute-start(f32[264,128]{1,0:T(8,128)S(1)} %get-tuple-element.28), channel_id=1, source_target_pairs={{0,8},{8,0},{16,24},{24,16},{1,9},{9,1},{17,25},{25,17},{2,10},{10... | collective-permute-start | bytes 405512 | tf_op jit(solution)/shard_map/ppermute | solution.py:706
  18.7 19.5 %collective-permute-start = (f32[520,128]{1,0:T(8,128)S(1)}, f32[520,128]{1,0:T(8,128)S(1)}, u32[]{:S(2)}, u32[]{:S(2)}) collective-permute-start(f32[520,128]{1,0:T(8,128)S(1)} %get-tuple-element.21), channel_id=1, source_target_pairs={{0,8},{8,0},{16,24},{24,16},{1,9},{9,1},{17,25},{25,17},{2,10},{10... | collective-permute-start | bytes 798728 | tf_op jit(solution)/shard_map/ppermute | solution.py:706
  19.2 19.0 %collective-permute-start.1 = (f32[520,128]{1,0:T(8,128)S(1)}, f32[520,128]{1,0:T(8,128)S(1)}, u32[]{:S(2)}, u32[]{:S(2)}) collective-permute-start(f32[520,128]{1,0:T(8,128)S(1)} %get-tuple-element.22), channel_id=1, source_target_pairs={{0,16},{8,24},{16,0},{24,8},{1,17},{9,25},{17,1},{25,9},{2,18},{10... | collective-permute-start | bytes 798728 | tf_op jit(solution)/shard_map/ppermute | solution.py:706
  20.7 17.5 %collective-permute-start.2 = (f32[520,128]{1,0:T(8,128)S(1)}, f32[520,128]{1,0:T(8,128)S(1)}, u32[]{:S(2)}, u32[]{:S(2)}) collective-permute-start(f32[520,128]{1,0:T(8,128)S(1)} %get-tuple-element.23), channel_id=1, source_target_pairs={{0,24},{8,16},{16,8},{24,0},{1,25},{9,17},{17,9},{25,1},{2,26},{10... | collective-permute-start | bytes 798728 | tf_op jit(solution)/shard_map/ppermute | solution.py:706
  20.7 16.4 %collective-permute-start.6 = (f32[264,128]{1,0:T(8,128)S(1)}, f32[264,128]{1,0:T(8,128)S(1)}, u32[]{:S(2)}, u32[]{:S(2)}) collective-permute-start(f32[264,128]{1,0:T(8,128)S(1)} %get-tuple-element.29), channel_id=1, source_target_pairs={{0,16},{8,24},{16,0},{24,8},{1,17},{9,25},{17,1},{25,9},{2,18},{10... | collective-permute-start | bytes 405512 | tf_op jit(solution)/shard_map/ppermute | solution.py:706
  22.1 16.1 %collective-permute-start.7 = (f32[264,128]{1,0:T(8,128)S(1)}, f32[264,128]{1,0:T(8,128)S(1)}, u32[]{:S(2)}, u32[]{:S(2)}) collective-permute-start(f32[264,128]{1,0:T(8,128)S(1)} %get-tuple-element.30), channel_id=1, source_target_pairs={{0,24},{8,16},{16,8},{24,0},{1,25},{9,17},{17,9},{25,1},{2,26},{10... | collective-permute-start | bytes 405512 | tf_op jit(solution)/shard_map/ppermute | solution.py:706
  38.3 1.0 %copy-start.7 = (bf16[256,576]{1,0:T(8,128)(2,1)S(1)}, bf16[256,576]{1,0:T(8,128)(2,1)}, u32[]{:S(2)}) copy-start(bf16[256,576]{1,0:T(8,128)(2,1)} %constant.84.clone.refs_27_) | copy-start | bytes 884740
  39.2 1.0 %copy-start.8 = (bf16[576,256]{1,0:T(8,128)(2,1)S(1)}, bf16[576,256]{1,0:T(8,128)(2,1)}, u32[]{:S(2)}) copy-start(bf16[576,256]{1,0:T(8,128)(2,1)} %constant.80.clone.refs_23_) | copy-start | bytes 884740
  40.2 1.0 %copy-start.9 = (bf16[576,256]{1,0:T(8,128)(2,1)S(1)}, bf16[576,256]{1,0:T(8,128)(2,1)}, u32[]{:S(2)}) copy-start(bf16[576,256]{1,0:T(8,128)(2,1)} %constant.76.clone.refs_19_) | copy-start | bytes 884740
  41.2 1.0 %copy-start.10 = (bf16[576,256]{1,0:T(8,128)(2,1)S(1)}, bf16[576,256]{1,0:T(8,128)(2,1)}, u32[]{:S(2)}) copy-start(bf16[576,256]{1,0:T(8,128)(2,1)} %constant.72.clone.refs_15_) | copy-start | bytes 884740
  42.1 1.0 %copy-start.11 = (bf16[576,256]{1,0:T(8,128)(2,1)S(1)}, bf16[576,256]{1,0:T(8,128)(2,1)}, u32[]{:S(2)}) copy-start(bf16[576,256]{1,0:T(8,128)(2,1)} %constant.68.clone.refs_11_) | copy-start | bytes 884740
  58.1 2.2 %collective-permute-start.8 = (f32[128,128]{1,0:T(8,128)S(1)}, f32[128,128]{1,0:T(8,128)S(1)}, u32[]{:S(2)}, u32[]{:S(2)}) collective-permute-start(f32[128,128]{1,0:T(8,128)S(1)} %get-tuple-element.32), channel_id=1, source_target_pairs={{0,8},{8,0},{16,24},{24,16},{1,9},{9,1},{17,25},{25,17},{2,10},{10... | collective-permute-start | bytes 196616 | tf_op jit(solution)/shard_map/ppermute | solution.py:706
  58.9 4.3 %collective-permute-start.9 = (f32[128,128]{1,0:T(8,128)S(1)}, f32[128,128]{1,0:T(8,128)S(1)}, u32[]{:S(2)}, u32[]{:S(2)}) collective-permute-start(f32[128,128]{1,0:T(8,128)S(1)} %get-tuple-element.33), channel_id=1, source_target_pairs={{0,16},{8,24},{16,0},{24,8},{1,17},{9,25},{17,1},{25,9},{2,18},{10... | collective-permute-start | bytes 196616 | tf_op jit(solution)/shard_map/ppermute | solution.py:706
  60.4 4.4 %collective-permute-start.10 = (f32[128,128]{1,0:T(8,128)S(1)}, f32[128,128]{1,0:T(8,128)S(1)}, u32[]{:S(2)}, u32[]{:S(2)}) collective-permute-start(f32[128,128]{1,0:T(8,128)S(1)} %get-tuple-element.34), channel_id=1, source_target_pairs={{0,24},{8,16},{16,8},{24,0},{1,25},{9,17},{17,9},{25,1},{2,26},{10... | collective-permute-start | bytes 196616 | tf_op jit(solution)/shard_map/ppermute | solution.py:706
  (7 other events, 5.6 us)

commit v2 on v1

--- a/solution.py
+++ b/solution.py
@@ -21,6 +21,7 @@
 
 POINTS = LINE_POINT_TOTAL**3
 FIELDS = 4
+PARTS = ((0, 1), (2, 3))
 PARAM_ROWS = 8
 LANES = 128
 HALF = LINE_POINT_TOTAL // 2
@@ -159,29 +160,25 @@
     return lifts, backs, stiff
 
 
-def pair_of(here, shift, count):
-    if count & (count - 1) == 0:
-        return here ^ shift
-    return (here + shift) % count
-
-
 class Layout:
     def __init__(self, elements, sections):
+        assert sections & (sections - 1) == 0 and elements == LANES
         self.elements = elements
         self.sections = sections
         self.main = elements // sections
-        self.slot = self.main + 2 * GHOST
-        while (self.slot * sections) % LANES:
-            self.slot += 1
+        self.unit = int(np.gcd(self.main, 2 * GHOST))
+        assert self.unit in (GHOST, 2 * GHOST)
+        self.slot = round_up(self.main + 2 * GHOST, max(self.unit, LANES // sections))
         self.columns = self.slot * sections
+        self.tiles = self.columns // LANES
         self.main_rows = POINTS // sections
-        self.ghost_groups = elements // (2 * GHOST)
-        self.ghost_rows = POINTS // self.ghost_groups
-        self.end_groups = elements // GHOST
-        self.end_rows = POINTS // self.end_groups
-        apart = self.main + GHOST
-        self.joint = apart % (2 * GHOST) == GHOST
-        self.right_offset = apart if self.joint else GHOST
+        self.units = elements // self.unit
+        self.unit_rows = POINTS // self.units
+        self.window_units = (self.main + 2 * GHOST) // self.unit
+        self.region_units = (elements // 2 + 2 * GHOST) // self.unit
+        self.half = sections // 2
+        self.slot_units = self.slot // self.unit
+        self.end_rows = POINTS // (elements // GHOST)
 
     def window_pieces(self, source, target, width):
         pieces = []
@@ -206,165 +203,176 @@
 def turned(value, shift):
     if isinstance(shift, int) and shift % value.shape[-1] == 0:
         return value
-    return pltpu.roll(value, shift, axis=1)
-
-
-def reorder(temperature, velocity, ordered):
+    return pltpu.roll(value, shift % LANES if isinstance(shift, int) else shift, axis=1)
+
+
+def exchange_groups(blocks, width):
+    blocks = list(blocks)
+    count = len(blocks)
+    lane = lane_iota(next(block for block in blocks if block is not None).shape[0])
+    step = 1
+    while step < count:
+        keep = (lane & (step * width)) == 0
+        for index in range(count):
+            if index & step:
+                continue
+            low, high = blocks[index], blocks[index | step]
+            if low is None and high is None:
+                continue
+            zero = jnp.zeros(lane.shape, jnp.float32)
+            up = zero if low is None else turned(low, -step * width)
+            down = zero if high is None else turned(high, step * width)
+            blocks[index] = jnp.where(keep, zero if low is None else low, down)
+            blocks[index | step] = jnp.where(keep, up, zero if high is None else high)
+        step *= 2
+    return blocks
+
+
+def pack_kernel(layout, blocks, scalars, *refs):
+    inputs = refs[:5]
+    outs, ends = refs[5 : 5 + 2 * len(PARTS)], refs[5 + 2 * len(PARTS) : 7 + 2 * len(PARTS)]
+    held = refs[7 + 2 * len(PARTS) : 12 + 2 * len(PARTS)]
+    packed, arrived = refs[12 + 2 * len(PARTS) :]
+    temperature, velocity, conductivity, metal, patch = held
+    elements, main, sections = layout.elements, layout.main, layout.sections
+    unit, units, rows = layout.unit, layout.units, layout.unit_rows
+    here, block = scalars[0], scalars[1]
+    copies = [
+        pltpu.make_async_copy(inputs[0], temperature, arrived.at[0]),
+        *[
+            pltpu.make_async_copy(inputs[1].at[d], velocity.at[d], arrived.at[1 + d])
+            for d in range(3)
+        ],
+        *[
+            pltpu.make_async_copy(inputs[i], held[i], arrived.at[2 + i]) for i in range(2, 5)
+        ],
+    ]
+    for copy in copies:
+        copy.start()
     for field in range(FIELDS):
+        copies[field].wait()
         source = temperature if field == 0 else velocity.at[field - 1]
-        for a in range(LINE_POINT_TOTAL):
-            for c in range(LINE_POINT_TOTAL):
-                base = a * 64 + c
-                ordered[field, pl.ds((a * 8 + c) * 8, 8), :] = source[pl.ds(base, 8, stride=8), :]
-
-
-def pack_main_kernel(layout, scalars, temperature, velocity, params, *rest):
-    outs = rest[: layout.sections]
-    low_end, high_end, ordered = rest[layout.sections :]
-    reorder(temperature, velocity, ordered)
-    here = scalars[0]
-    elements, main, rows = layout.elements, layout.main, layout.main_rows
-    lane = lane_iota(rows)
-    for shift in range(layout.sections):
-        there = pair_of(here, shift, layout.sections)
-        for field in range(FIELDS):
-            value = None
-            for group in range(layout.sections):
-                amount = lax.rem((group - there) * main + elements, elements)
-                part = pltpu.roll(ordered[field, pl.ds(group * rows, rows), :], amount, axis=1)
-                value = (
-                    part
-                    if value is None
-                    else jnp.where(in_range(lane, group * main, (group + 1) * main), part, value)
+        groups = []
+        for group in range(units):
+            parts = []
+            for index in range(group * rows // 8, (group + 1) * rows // 8):
+                a, c = divmod(index, LINE_POINT_TOTAL)
+                parts.append(source[pl.ds(a * 64 + c, 8, stride=8), :])
+            groups.append(pltpu.roll(jnp.concatenate(parts, 0), GHOST, axis=1))
+        for index, value in enumerate(exchange_groups(groups, unit)):
+            packed[field, index] = value
+    for copy in copies[FIELDS:]:
+        copy.wait()
+    position = block * elements + lax.broadcasted_iota(jnp.int32, (1, elements), 1)
+    zero = jnp.zeros((1, elements), jnp.float32)
+    params = jnp.concatenate(
+        [
+            conductivity[...],
+            metal[...].astype(jnp.float32),
+            (patch[...] ^ here).astype(jnp.float32),
+            jnp.where(position > 0, 1.0, 0.0),
+            jnp.where(position < elements * blocks - 1, 1.0, 0.0),
+        ]
+        + [zero] * (PARAM_ROWS - 5),
+        0,
+    )
+    region = here // layout.half
+    for part, part_fields in enumerate(PARTS):
+        for side, there in enumerate((region, 1 - region)):
+            out = outs[2 * part + side]
+            row = 0
+            for field in part_fields:
+                for index in range(layout.region_units):
+                    place = lax.rem(there * (units // 2) + index, units)
+                    out[pl.ds(row, rows), :] = packed[field, place]
+                    row += rows
+            if part == 0:
+                out[pl.ds(row, PARAM_ROWS), :] = pltpu.roll(
+                    params, lax.rem(elements + GHOST - there * (elements // 2), elements), axis=1
                 )
-            outs[shift][pl.ds(field * rows, rows), :] = value
-        outs[shift][pl.ds(FIELDS * rows, PARAM_ROWS), :] = pltpu.roll(
-            params[...], lax.rem(elements - there * main, elements), axis=1
-        )
-    rows = layout.end_rows
-    lane = lane_iota(rows)
-    for out, first in ((low_end, 0), (high_end, elements - GHOST)):
-        for field in range(FIELDS):
-            value = None
-            for group in range(layout.end_groups):
-                part = turned(
-                    ordered[field, pl.ds(group * rows, rows), :],
-                    (group * GHOST - first) % elements,
-                )
-                value = (
-                    part
-                    if value is None
-                    else jnp.where(in_range(lane, group * GHOST, (group + 1) * GHOST), part, value)
-                )
-            out[pl.ds(field * rows, rows), :] = value
-        out[pl.ds(FIELDS * rows, PARAM_ROWS), :] = turned(params[...], (-first) % elements)
-
-
-def pack_ghost_kernel(
-    layout, scalars, ordered, params, from_low, from_high, *rest
-):
-    outs, edge = rest[: layout.sections], rest[layout.sections]
-    here = scalars[0]
-    elements, main, sections = layout.elements, layout.main, layout.sections
-    rows = layout.end_rows
-    lane = lane_iota(rows)
+    swapped = here >= sections // 2
+    lane = lane_iota(layout.end_rows)
+    row = 0
     for field in range(FIELDS):
-        for group in range(layout.end_groups):
-            low = turned(from_low[pl.ds(field * rows, rows), :], (-GHOST - group * GHOST) % elements)
-            high = turned(from_high[pl.ds(field * rows, rows), :], (-group * GHOST) % elements)
-            edge[field, pl.ds(group * rows, rows), :] = jnp.where(lane < elements // 2, high, low)
-    low = turned(from_low[pl.ds(FIELDS * rows, PARAM_ROWS), :], elements - GHOST)
-    high = from_high[pl.ds(FIELDS * rows, PARAM_ROWS), :]
-    edge_params = jnp.where(lane_iota(PARAM_ROWS) < elements // 2, high, low)
-    rows = layout.ghost_rows
-    lane = lane_iota(rows)
-
-    def gather(inner, outer, first, last, group, there, mask_lane, value):
-        left = jnp.where(first, outer, inner)
-        right = jnp.where(last, outer, inner)
-        shift_left = lax.rem(2 * GHOST * group + GHOST - main * there + elements, elements)
-        at_left = 2 * GHOST * group
-        at_right = (2 * GHOST * group + layout.right_offset) % elements
-        left_mask = in_range(mask_lane, at_left, at_left + GHOST)
-        right_mask = in_range(mask_lane, at_right, at_right + GHOST)
-        if layout.joint:
-            source_lane = lax.rem(mask_lane - main * there + elements + GHOST, elements)
-            both = jnp.where(source_lane < GHOST, left, right)
-            part = pltpu.roll(both, shift_left, axis=1)
-            return jnp.where(left_mask | right_mask, part, value)
-        shift_right = lax.rem(
-            2 * GHOST * group + layout.right_offset - main * (there + 1) + 2 * elements, elements
-        )
-        value = jnp.where(left_mask, pltpu.roll(left, shift_left, axis=1), value)
-        return jnp.where(right_mask, pltpu.roll(right, shift_right, axis=1), value)
-
-    for shift in range(sections):
-        there = pair_of(here, shift, sections)
-        first, last = there == 0, there == sections - 1
-        for field in range(FIELDS):
-            value = jnp.zeros((rows, LANES), jnp.float32)
-            for group in range(layout.ghost_groups):
-                span = pl.ds(group * rows, rows)
-                value = gather(
-                    ordered[field, span, :], edge[field, span, :], first, last, group, there, lane, value
-                )
-            outs[shift][pl.ds(field * rows, rows), :] = value
-        outs[shift][pl.ds(FIELDS * rows, PARAM_ROWS), :] = gather(
-            params[...],
-            edge_params,
-            first,
-            last,
+        if unit == GHOST:
+            high, low = packed[field, 0], packed[field, 1]
+        else:
+            upper, lower = packed[field, 0, : rows // 2], packed[field, 0, rows // 2 :]
+            keep = (lane & GHOST) == 0
+            high = jnp.where(keep, upper, turned(lower, GHOST))
+            low = jnp.where(keep, turned(upper, -GHOST), lower)
+        ends[0][pl.ds(row, layout.end_rows), :] = jnp.where(swapped, low, high)
+        ends[1][pl.ds(row, layout.end_rows), :] = jnp.where(swapped, high, low)
+        row += layout.end_rows
+    high = turned(params, GHOST)
+    ends[0][pl.ds(row, PARAM_ROWS), :] = jnp.where(swapped, params, high)
+    ends[1][pl.ds(row, PARAM_ROWS), :] = jnp.where(swapped, high, params)
+
+
+def unpack_columns(layout, here, chunks, ends, fields, param_value):
+    sections, unit, rows = layout.sections, layout.unit, layout.unit_rows
+    end_rows = layout.end_rows
+    within = lax.rem(here, layout.half)
+    first_row = within * (layout.main // unit * rows)
+    at_first, at_last = here == 0, here == sections - 1
+    per_tile = LANES // unit
+    end_lane = lane_iota(end_rows)
+
+    def unit_block(field, section, index):
+        part, place = next(
+            (part, inside.index(field)) for part, inside in enumerate(PARTS) if field in inside
+        )
+        base = (place * layout.region_units + index) * rows
+        block = chunks[part][section][pl.ds(pl.multiple_of(first_row + base, 8), rows), :]
+        if index not in (0, layout.window_units - 1):
+            return block
+        replace = at_first if index == 0 else at_last
+        end = ends[section][pl.ds(field * end_rows, end_rows), :]
+        if unit == GHOST:
+            return jnp.where(replace, end, block)
+        if index == 0:
+            parts = [end, turned(end, -GHOST)]
+            mask = (end_lane & GHOST) == 0
+        else:
+            parts = [turned(end, GHOST), end]
+            mask = (end_lane & GHOST) != 0
+        mask = mask & replace
+        return jnp.concatenate(
+            [
+                jnp.where(mask, part, block[i * end_rows : (i + 1) * end_rows])
+                for i, part in enumerate(parts)
+            ],
             0,
-            there,
-            lane_iota(PARAM_ROWS),
-            jnp.zeros((PARAM_ROWS, LANES), jnp.float32),
-        )
-
-
-def unpack_columns(layout, mains, ghosts, fields, param_value):
-    sections, main, slot = layout.sections, layout.main, layout.slot
-    tiles = layout.columns // LANES
-
-    def moves(section, group, ghost):
-        if not ghost:
-            return layout.window_pieces(group * main, section * slot + GHOST, main)
-        at_left = 2 * GHOST * group
-        at_right = (at_left + layout.right_offset) % layout.elements
-        return layout.window_pieces(at_left, section * slot, GHOST) + layout.window_pieces(
-            at_right, section * slot + GHOST + main, GHOST
-        )
-
-    def fill(sources, rows, first_row, group, ghost, values):
-        lane = lane_iota(rows)
-        for section in range(sections):
-            block = sources[section][pl.ds(first_row, rows), :]
-            cache = {}
-            for _, tile, shift, first, last in moves(section, group, ghost):
-                if shift not in cache:
-                    cache[shift] = turned(block, shift)
-                mask = in_range(lane, first, last)
-                values[tile] = jnp.where(mask, cache[shift], values[tile])
-        return values
-
-    def zeros(rows):
-        return [jnp.zeros((rows, LANES), jnp.float32) for _ in range(tiles)]
-
-    rows = min(layout.main_rows, layout.ghost_rows)
+        )
+
     for field in range(FIELDS):
-        for start in range(0, POINTS, rows):
-            group, offset = divmod(start, layout.main_rows)
-            values = fill(
-                mains, rows, field * layout.main_rows + offset, group, False, zeros(rows)
-            )
-            group, offset = divmod(start, layout.ghost_rows)
-            values = fill(
-                ghosts, rows, field * layout.ghost_rows + offset, group, True, values
-            )
-            for tile in range(tiles):
-                fields[field, pl.ds(start, rows), pl.ds(tile * LANES, LANES)] = values[tile]
-    values = fill(mains, PARAM_ROWS, FIELDS * layout.main_rows, 0, False, zeros(PARAM_ROWS))
-    values = fill(ghosts, PARAM_ROWS, FIELDS * layout.ghost_rows, 0, True, values)
-    for tile in range(tiles):
+        for tile in range(layout.tiles):
+            blocks = []
+            for place in range(per_tile):
+                section, index = divmod(tile * per_tile + place, layout.slot_units)
+                inside = index < layout.window_units
+                blocks.append(unit_block(field, section, index) if inside else None)
+            for group, value in enumerate(exchange_groups(blocks, unit)):
+                fields[field, pl.ds(group * rows, rows), pl.ds(tile * LANES, LANES)] = value
+
+    lane = lane_iota(PARAM_ROWS)
+    values = [jnp.zeros((PARAM_ROWS, LANES), jnp.float32) for _ in range(layout.tiles)]
+    for section in range(sections):
+        block = chunks[0][section][
+            pl.ds(len(PARTS[0]) * layout.region_units * rows, PARAM_ROWS), :
+        ]
+        block = pltpu.roll(block, lax.rem(LANES - within * layout.main, LANES), axis=1)
+        end = ends[section][pl.ds(FIELDS * end_rows, PARAM_ROWS), :]
+        after = GHOST + layout.main
+        block = jnp.where(at_first & (lane < GHOST), end, block)
+        block = jnp.where(
+            at_last & in_range(lane, after, after + GHOST), turned(end, after), block
+        )
+        for _, tile, shift, first, last in layout.window_pieces(
+            0, section * layout.slot, after + GHOST
+        ):
+            values[tile] = jnp.where(in_range(lane, first, last), turned(block, shift), values[tile])
+    for tile in range(layout.tiles):
         param_value[:, pl.ds(tile * LANES, LANES)] = values[tile]
 
 
@@ -424,26 +432,44 @@
     ]
 
 
-def main_kernel(layout, tables, *refs):
+def main_kernel(layout, tables, scalars, *refs):
     weights = tables[3]
     sections, columns = layout.sections, layout.columns
+    here = scalars[0]
     refs = list(refs)
 
     def take(count):
         taken, refs[:] = refs[:count], refs[count:]
         return taken
 
-    mains, ghosts = take(sections), take(sections)
-    lifts, backs, stiff = take(16), take(4), take(4)
+    chunks, ends = [take(sections) for _ in PARTS], take(sections)
+    stored = take(2)
     outs = take(sections)
     fields, param_value = take(2)
     fine = [take(4) for _ in range(3)]
     (lifted, point_pieces, results, keep, gain_rhs, gain_k, gain) = take(7)
     (gain_low, gain_high, gain_wall) = take(3)
     fine_pieces = take(4)
+    matrices = take(2)
+    (arrived,) = take(1)
     pieces = [point_pieces.at[index] for index in range(4)]
-
-    unpack_columns(layout, mains, ghosts, fields, param_value)
+    heights = [2 * class_fine_rows(cls) for cls in CLASSES]
+    starts = np.concatenate([[0], np.cumsum(heights * 4 + [2 * CLASS_ROWS] * 4)]).tolist()
+    tall = [matrices[0].at[pl.ds(i, j - i)] for i, j in zip(starts[:-1], starts[1:])]
+    lifts, stiff = tall[:16], tall[16:]
+    wide = np.concatenate([[0], np.cumsum([round_up(h, LANES) for h in heights])]).tolist()
+    backs = [matrices[1].at[:, pl.ds(i, h)] for i, h in zip(wide, heights)]
+    copies = [
+        pltpu.make_async_copy(
+            stored[0].at[pl.ds(i, j - i)], matrices[0].at[pl.ds(i, j - i)], arrived.at[index]
+        )
+        for index, (i, j) in enumerate(zip(starts[0:17:4], starts[4:21:4]))
+    ]
+    copies.append(pltpu.make_async_copy(stored[1], matrices[1], arrived.at[5]))
+    for copy in copies:
+        copy.start()
+
+    unpack_columns(layout, here, chunks, ends, fields, param_value)
 
     params = param_value[...]
     k, metal, partner, has_low, has_high = [params[row : row + 1] for row in range(5)]
@@ -453,7 +479,7 @@
 
     lane = lax.broadcasted_iota(jnp.int32, (1, columns), 1)
     own_slot = lane // layout.slot
-    partner_slot = pair_of(own_slot, partner.astype(jnp.int32), sections)
+    partner_slot = own_slot ^ partner.astype(jnp.int32)
     distance = lax.rem(partner_slot - own_slot + sections, sections)
     coef_low = has_low * (0.5 * penalty) * (k + shifted(k, 1))
     coef_high = has_high * (0.5 * penalty) * (k + shifted(k, -1))
@@ -507,6 +533,8 @@
 
     for direction in range(3):
         to_classes(fields.at[direction + 1], pieces)
+        if direction == 0:
+            copies[0].wait()
         for index in range(4):
             fine[0][index][...] = multiply(lifts[index], pieces[index])
         for q in range(MIRROR + 1):
@@ -516,6 +544,8 @@
                     lifted[direction, point, pl.ds(base, part.shape[0]), :] = part
                     base += part.shape[0]
 
+    for copy in copies[1:]:
+        copy.wait()
     iterate = fields.at[0]
     for step_index in range(STEPS):
         to_classes(iterate, pieces)
@@ -626,7 +656,7 @@
     here = scalars[0]
     rows, main, elements = layout.main_rows, layout.main, layout.elements
     lane = lane_iota(rows)
-    places = [pair_of(here, shift, layout.sections) for shift in range(layout.sections)]
+    places = [here ^ shift for shift in range(layout.sections)]
     for group in range(layout.sections):
         value = None
         for shift, there in enumerate(places):
@@ -650,6 +680,14 @@
     return [pl.BlockSpec(memory_space=pltpu.VMEM)] * count
 
 
+def in_hbm(count):
+    return [pl.BlockSpec(memory_space=pltpu.HBM)] * count
+
+
+def kept_in_hbm(array):
+    return pltpu.with_memory_space_constraint(array, pltpu.HBM)
+
+
 SCALAR = pl.BlockSpec(memory_space=pltpu.SMEM)
 PARAMS = pltpu.CompilerParams(vmem_limit_bytes=48 * 1024 * 1024)
 
@@ -665,73 +703,92 @@
     blocks = lax.axis_size("elem")
     elements = thermal_diffusivity_cell.shape[1]
     layout = Layout(elements, sections)
-    here = lax.axis_index("sec").astype(jnp.int32)
-    scalars = here[None]
-    position = lax.axis_index("elem") * elements + lax.iota(jnp.int32, elements)
-    if sections & (sections - 1) == 0:
-        relative = adjoining_patch[0] ^ here
-    else:
-        relative = (adjoining_patch[0] - here) % sections
-    params = jnp.stack(
-        [
-            thermal_diffusivity_cell[0],
-            metal_cell_indicator[0].astype(jnp.float32),
-            relative.astype(jnp.float32),
-            (position > 0).astype(jnp.float32),
-            (position < elements * blocks - 1).astype(jnp.float32),
-        ]
-        + [jnp.zeros((elements,), jnp.float32)] * (PARAM_ROWS - 5),
-        0,
-    )
-    temperature = thermal_level_points.reshape(POINTS, elements)
-    velocity = flow_speed_vector.reshape(3, POINTS, elements)
-
-    main_shape = shape_of(FIELDS * layout.main_rows + PARAM_ROWS, elements)
-    ghost_shape = shape_of(FIELDS * layout.ghost_rows + PARAM_ROWS, elements)
+    scalars = jnp.stack([lax.axis_index("sec"), lax.axis_index("elem")]).astype(jnp.int32)
+    f32, bf16 = jnp.float32, jnp.bfloat16
+    dma = pltpu.SemaphoreType.DMA
+
+    chunk_shapes = [
+        shape_of(
+            len(part) * layout.region_units * layout.unit_rows
+            + (PARAM_ROWS if index == 0 else 0),
+            elements,
+        )
+        for index, part in enumerate(PARTS)
+        for _ in range(2)
+    ]
     end_shape = shape_of(FIELDS * layout.end_rows + PARAM_ROWS, elements)
     packed = pl.pallas_call(
-        functools.partial(pack_main_kernel, layout),
-        out_shape=[main_shape] * sections + [end_shape] * 2 + [shape_of(FIELDS, POINTS, elements)],
-        in_specs=[SCALAR] + in_vmem(3),
-        out_specs=in_vmem(sections + 3),
+        functools.partial(pack_kernel, layout, blocks),
+        out_shape=chunk_shapes + [end_shape] * 2,
+        in_specs=[SCALAR] + in_hbm(5),
+        out_specs=in_vmem(len(chunk_shapes) + 2),
+        scratch_shapes=[
+            pltpu.VMEM((POINTS, elements), f32),
+            pltpu.VMEM((3, POINTS, elements), f32),
+            pltpu.VMEM((1, elements), f32),
+            pltpu.VMEM((1, elements), jnp.int32),
+            pltpu.VMEM((1, elements), jnp.int32),
+            pltpu.VMEM((FIELDS, layout.units, layout.unit_rows, elements), f32),
+            dma((7,)),
+        ],
         compiler_params=PARAMS,
-        name="pack_main",
-    )(scalars, temperature, velocity, params)
-    mains, (low_end, high_end, ordered) = packed[:sections], packed[sections:]
-
-    def swap(arrays):
-        received = [arrays[0]]
-        for shift in range(1, sections):
-            pairs = [(i, pair_of(i, shift, sections)) for i in range(sections)]
-            received.append(lax.ppermute(arrays[shift], "sec", pairs))
-        if sections & (sections - 1):
-            received[1:] = received[:0:-1]
-        return received
-
-    mains = swap(mains)
-    forward = [(i, i + 1) for i in range(blocks - 1)]
-    from_low = lax.ppermute(high_end, "elem", forward)
-    from_high = lax.ppermute(low_end, "elem", [(i, j) for j, i in forward])
-    ghosts = pl.pallas_call(
-        functools.partial(pack_ghost_kernel, layout),
-        out_shape=[ghost_shape] * sections,
-        in_specs=[SCALAR] + in_vmem(4),
-        out_specs=in_vmem(sections),
-        scratch_shapes=[pltpu.VMEM((FIELDS, POINTS, elements), jnp.float32)],
-        compiler_params=PARAMS,
-        name="pack_ghost",
-    )(scalars, ordered, params, from_low, from_high)
-    ghosts = swap(ghosts)
-
+        name="pack",
+    )(
+        scalars,
+        *[
+            kept_in_hbm(x)
+            for x in (
+                thermal_level_points.reshape(POINTS, elements),
+                flow_speed_vector.reshape(3, POINTS, elements),
+                thermal_diffusivity_cell,
+                metal_cell_indicator,
+                adjoining_patch,
+            )
+        ],
+    )
+    end_pair = packed[-2:]
+
+    def across(array, mask):
+        return lax.ppermute(array, "sec", [(i, i ^ mask) for i in range(sections)])
+
+    chunks = [
+        {0: packed[2 * part], layout.half: across(packed[2 * part + 1], layout.half)}
+        for part in range(len(PARTS))
+    ]
+    ends = []
+    for source in range(sections):
+        mirrored = sections - 1 - source
+        pairs = [(source * blocks + i, i + 1) for i in range(blocks - 1)]
+        pairs += [
+            (mirrored * blocks + i + 1, (sections - 1) * blocks + i) for i in range(blocks - 1)
+        ]
+        ends.append(
+            lax.ppermute(end_pair[0 if source < sections // 2 else 1], ("sec", "elem"), pairs)
+        )
+    first, ends = lax.optimization_barrier((chunks[0][layout.half], ends))
+    chunks[0][layout.half] = first
+    for chunk in chunks:
+        bit = layout.half // 2
+        while bit:
+            for mask in sorted(chunk):
+                chunk[mask | bit] = across(chunk[mask], bit)
+            bit //= 2
+    chunks = [chunk[mask] for chunk in chunks for mask in range(sections)]
     lifts, backs, stiff = make_matrices()
     columns = layout.columns
-    matrices = [jnp.asarray(matrix) for matrix in lifts + backs + stiff]
+    wide = [
+        np.pad(matrix, ((0, 0), (0, round_up(matrix.shape[1], LANES) - matrix.shape[1])))
+        for matrix in backs
+    ]
+    matrices = [
+        jnp.asarray(np.concatenate(lifts + stiff, 0)),
+        jnp.asarray(np.concatenate(wide, 1)),
+    ]
     fine_rows = [class_fine_rows(cls) for cls in CLASSES]
-    f32, bf16 = jnp.float32, jnp.bfloat16
-    chunks = pl.pallas_call(
+    results = pl.pallas_call(
         functools.partial(main_kernel, layout, make_tables()),
         out_shape=[shape_of(layout.main_rows, elements)] * sections,
-        in_specs=in_vmem(2 * sections + len(matrices)),
+        in_specs=[SCALAR] + in_vmem(len(chunks) + sections) + in_hbm(len(matrices)),
         out_specs=in_vmem(sections),
         scratch_shapes=[
             pltpu.VMEM((FIELDS, POINTS, columns), f32),
@@ -743,11 +800,13 @@
             *[pltpu.VMEM((POINTS, columns), f32) for _ in range(4)],
             *[pltpu.VMEM((64, columns), f32) for _ in range(3)],
             *[pltpu.VMEM((2 * rows, columns), bf16) for rows in fine_rows],
+            *[pltpu.VMEM(matrix.shape, bf16) for matrix in matrices],
+            dma((6,)),
         ],
         compiler_params=PARAMS,
         name="march",
-    )(*mains, *ghosts, *matrices)
-    chunks = swap(chunks)
+    )(scalars, *chunks, *ends, *[kept_in_hbm(matrix) for matrix in matrices])
+    results = [results[0]] + [across(results[mask], mask) for mask in range(1, sections)]
     result = pl.pallas_call(
         functools.partial(gather_kernel, layout),
         out_shape=shape_of(POINTS, elements),
@@ -755,7 +814,7 @@
         out_specs=pl.BlockSpec(memory_space=pltpu.VMEM),
         compiler_params=PARAMS,
         name="unpack",
-    )(scalars, *chunks)
+    )(scalars, *results)
     return result.reshape(thermal_level_points.shape)
 
 

time: 66.3 us -> 48.1 us (0.73)
  local copies, waits for them, and re-layouts: 11.6 us -> 0 us
  waiting for transfers between devices: 24.8 us -> 14.4 us
  Pallas kernels: 16.7 us -> 19 us
  starting transfers between devices: 12.5 us -> 14.3 us
    unnamed x40 -> x0, local copies, waits for them, and re-layouts: 11.6 us -> none
    ppermute x11 -> x13, waiting for transfers between devices: 24.8 us -> 14.4 us  [the longest x9 13.9 us: across(): return lax.ppermute(array, 'sec', [(i, i ^ mask) for i in range(sections)])]
    ppermute x11 -> x13, starting transfers between devices: 12.5 us -> 14.3 us  [the longest x9 7.84 us: across(): return lax.ppermute(array, 'sec', [(i, i ^ mask) for i in range(sections)])]
    pallas_call x1, Pallas kernels: 12.3 us -> 14.1 us  [body(): pl.pallas_call(functools.partial(main_kernel, layout, make_tables()), out...]
    pallas_call x2 -> x1, Pallas kernels: 3.39 us -> 3.29 us  [body(): pl.pallas_call(functools.partial(pack_kernel, layout, blocks), out_shape=...]
  transfers between devices with their start and end apart: 11 -> 13, of which waited for: 6 -> 6; matrix products, arithmetic and copies ran while one was open for 0% -> 0% of each run, Pallas kernels for 0% -> 0%
where the time goes in v2:
time: 48.1 us; the launch traced here: 47.9 us
  Pallas kernels  19 us (40%)
  waiting for transfers between devices  14.4 us (30%)
  starting transfers between devices  14.3 us (30%)
    pallas_call x1, Pallas kernels, body(): pl.pallas_call(functools.partial(main_kernel, layout, make_tables()), out...  14.1 us
    ppermute x9, waiting for transfers between devices, across(): return lax.ppermute(array, 'sec', [(i, i ^ mask) for i in range(sections)])  13.9 us
    ppermute x9, starting transfers between devices, across(): return lax.ppermute(array, 'sec', [(i, i ^ mask) for i in range(sections)])  7.84 us
    ppermute x4, starting transfers between devices, body(): lax.ppermute(end_pair[0 if source < sections // 2 else 1], ('sec', 'elem'...  6.49 us
    pallas_call x1, Pallas kernels, body(): pl.pallas_call(functools.partial(pack_kernel, layout, blocks), out_shape=...  3.29 us
    pallas_call x1, Pallas kernels, body(): pl.pallas_call(functools.partial(gather_kernel, layout), out_shape=shape_...  1.59 us
  transfers between devices with their start and end apart: 13, of which 6 were waited for; matrix products, arithmetic and copies ran while one was open for 0% of the time, Pallas kernels for 0%

profile of v2, /device:TPU:0, one launch (start us, length us, event | category | flops | bytes accessed | tf_op | source)
XLA Modules:
  0.0 47.9 jit_solution(2447695552715248289)
XLA Ops:
  0.0 0.1 pad_add_fusion.scalars
  0.1 3.3 %pack.1 = (f32[648,128]{1,0:T(8,128)S(1)}, f32[648,128]{1,0:T(8,128)S(1)}, f32[640,128]{1,0:T(8,128)S(1)}, f32[640,128]{1,0:T(8,128)S(1)}, f32[136,128]{1,0:T(8,128)S(1)}, /*index=5*/f32[136,128]{1,0:T(8,128)S(1)}) custom-call(s32[2]{0:T(128)S(1)} %pad_add_fusion.scalars, f32[512,128]{1,0:T(8,128)} %bitcast.6, f32[3,512,128]{2,1,0:T(8,128)} %bitcast.5, ...), custom_call_target="tpu_custom_call" | custom-call | tf_op jit(solution)/shard_map/pack/pallas_call | solution.py:720
  3.4 3.0 %collective-permute-start.1 = (f32[648,128]{1,0:T(8,128)S(1)}, f32[648,128]{1,0:T(8,128)S(1)}, u32[]{:S(2)}, u32[]{:S(2)}) collective-permute-start(f32[648,128]{1,0:T(8,128)S(1)} %get-tuple-element.21), channel_id=1, source_target_pairs={{0,16},{8,24},{16,0},{24,8},{1,17},{9,25},{17,1},{25,9},{2,18},{10... | collective-permute-start | bytes 995336 | tf_op jit(solution)/shard_map/ppermute | solution.py:752
  6.4 0.1 collective-permute-start.8
  6.5 0.7 %collective-permute-start.3 = (f32[136,128]{1,0:T(8,128)S(1)}, f32[136,128]{1,0:T(8,128)S(1)}, u32[]{:S(2)}, u32[]{:S(2)}) collective-permute-start(f32[136,128]{1,0:T(8,128)S(1)} %get-tuple-element.22), channel_id=1, source_target_pairs={{8,1},{9,2},{10,3},{11,4},{12,5},{13,6},{14,7},{17,24},{18,25},{19... | collective-permute-start | bytes 208904 | tf_op jit(solution)/shard_map/ppermute | solution.py:766
  7.1 4.5 %collective-permute-start.2 = (f32[136,128]{1,0:T(8,128)S(1)}, f32[136,128]{1,0:T(8,128)S(1)}, u32[]{:S(2)}, u32[]{:S(2)}) collective-permute-start(f32[136,128]{1,0:T(8,128)S(1)} %get-tuple-element.22), channel_id=1, source_target_pairs={{0,1},{1,2},{2,3},{3,4},{4,5},{5,6},{6,7},{25,24},{26,25},{27,26},... | collective-permute-start | bytes 208904 | tf_op jit(solution)/shard_map/ppermute | solution.py:766
  11.6 0.7 %collective-permute-start.5 = (f32[136,128]{1,0:T(8,128)S(1)}, f32[136,128]{1,0:T(8,128)S(1)}, u32[]{:S(2)}, u32[]{:S(2)}) collective-permute-start(f32[136,128]{1,0:T(8,128)S(1)} %get-tuple-element.23), channel_id=1, source_target_pairs={{24,1},{25,2},{26,3},{27,4},{28,5},{29,6},{30,7},{1,24},{2,25},{3,... | collective-permute-start | bytes 208904 | tf_op jit(solution)/shard_map/ppermute | solution.py:766
  12.3 0.0 collective-permute-done.3.refs_9_
  12.3 0.7 %collective-permute-start.4 = (f32[136,128]{1,0:T(8,128)S(1)}, f32[136,128]{1,0:T(8,128)S(1)}, u32[]{:S(2)}, u32[]{:S(2)}) collective-permute-start(f32[136,128]{1,0:T(8,128)S(1)} %get-tuple-element.23), channel_id=1, source_target_pairs={{16,1},{17,2},{18,3},{19,4},{20,5},{21,6},{22,7},{9,24},{10,25},{1... | collective-permute-start | bytes 208904 | tf_op jit(solution)/shard_map/ppermute | solution.py:766
  13.0 0.6 %collective-permute-done.2.refs_8_ = f32[136,128]{1,0:T(8,128)S(1)} collective-permute-done((f32[136,128]{1,0:T(8,128)S(1)}, f32[136,128]{1,0:T(8,128)S(1)}, u32[]{:S(2)}, u32[]{:S(2)}) %collective-permute-start.2) | collective-permute-done | bytes 69664 | tf_op jit(solution)/shard_map/ppermute | solution.py:766
  13.6 0.0 collective-permute-start
  13.6 0.0 collective-permute-done.5.refs_11_
  13.6 0.0 collective-permute-done.4.refs_10_
  13.6 1.4 %collective-permute-done.1.refs_2_ = f32[648,128]{1,0:T(8,128)S(1)} collective-permute-done((f32[648,128]{1,0:T(8,128)S(1)}, f32[648,128]{1,0:T(8,128)S(1)}, u32[]{:S(2)}, u32[]{:S(2)}) %collective-permute-start.1) | collective-permute-done | bytes 331808 | tf_op jit(solution)/shard_map/ppermute | solution.py:752
  15.0 0.0 collective-permute-start.6
  15.0 0.5 %collective-permute-start.7 = (f32[640,128]{1,0:T(8,128)S(1)}, f32[640,128]{1,0:T(8,128)S(1)}, u32[]{:S(2)}, u32[]{:S(2)}) collective-permute-start(f32[640,128]{1,0:T(8,128)S(1)} %get-tuple-element.25.refs_4_), channel_id=1, source_target_pairs={{0,8},{8,0},{16,24},{24,16},{1,9},{9,1},{17,25},{25,17},{2,10},{10... | collective-permute-start | bytes 983048 | tf_op jit(solution)/shard_map/ppermute | solution.py:752
  15.5 6.5 %collective-permute-done.8.refs_6_ = f32[640,128]{1,0:T(8,128)S(1)} collective-permute-done((f32[640,128]{1,0:T(8,128)S(1)}, f32[640,128]{1,0:T(8,128)S(1)}, u32[]{:S(2)}, u32[]{:S(2)}) %collective-permute-start.8) | collective-permute-done | bytes 327712 | tf_op jit(solution)/shard_map/ppermute | solution.py:752
  22.0 1.6 %collective-permute-done.9.refs_7_ = f32[640,128]{1,0:T(8,128)S(1)} collective-permute-done((f32[640,128]{1,0:T(8,128)S(1)}, f32[640,128]{1,0:T(8,128)S(1)}, u32[]{:S(2)}, u32[]{:S(2)}) %collective-permute-start.9) | collective-permute-done | bytes 327712 | tf_op jit(solution)/shard_map/ppermute | solution.py:752
  23.6 14.1 %march.1 = (f32[128,128]{1,0:T(8,128)S(1)}, f32[128,128]{1,0:T(8,128)S(1)}, f32[128,128]{1,0:T(8,128)S(1)}, f32[128,128]{1,0:T(8,128)S(1)}) custom-call(s32[2]{0:T(128)S(1)} %pad_add_fusion.scalars, f32[648,128]{1,0:T(8,128)S(1)} %get-tuple-element.20.refs_0_, f32[648,128]{1,0:T(8,128)S(1)} %collective-permute-done.refs_1_, ...), custom_call_target="tpu_custom_call" | custom-call | tf_op jit(solution)/shard_map/march/pallas_call | solution.py:788
  37.7 0.2 collective-permute-start.10
  37.9 4.0 %collective-permute-start.11 = (f32[128,128]{1,0:T(8,128)S(1)}, f32[128,128]{1,0:T(8,128)S(1)}, u32[]{:S(2)}, u32[]{:S(2)}) collective-permute-start(f32[128,128]{1,0:T(8,128)S(1)} %get-tuple-element.33), channel_id=1, source_target_pairs={{0,16},{8,24},{16,0},{24,8},{1,17},{9,25},{17,1},{25,9},{2,18},{10... | collective-permute-start | bytes 196616 | tf_op jit(solution)/shard_map/ppermute | solution.py:752
  41.9 2.4 %collective-permute-done.11.refs_2_ = f32[128,128]{1,0:T(8,128)S(1)} collective-permute-done((f32[128,128]{1,0:T(8,128)S(1)}, f32[128,128]{1,0:T(8,128)S(1)}, u32[]{:S(2)}, u32[]{:S(2)}) %collective-permute-start.11) | collective-permute-done | bytes 65568 | tf_op jit(solution)/shard_map/ppermute | solution.py:752
  44.3 2.0 %collective-permute-done.12.refs_3_ = f32[128,128]{1,0:T(8,128)S(1)} collective-permute-done((f32[128,128]{1,0:T(8,128)S(1)}, f32[128,128]{1,0:T(8,128)S(1)}, u32[]{:S(2)}, u32[]{:S(2)}) %collective-permute-start.12) | collective-permute-done | bytes 65568 | tf_op jit(solution)/shard_map/ppermute | solution.py:752
  46.3 1.6 %unpack.1 = f32[512,128]{1,0:T(8,128)} custom-call(s32[2]{0:T(128)S(1)} %pad_add_fusion.scalars, f32[128,128]{1,0:T(8,128)S(1)} %get-tuple-element.31.refs_0_, f32[128,128]{1,0:T(8,128)S(1)} %collective-permute-done.10.refs_1_, f32[128,128]{1,0:T(8,128)S(1)} %collective-permute-done.11.refs_2_, f32[128,128]{1,0:T(8,128)S(1)} %collective-permute-done.12.refs_3_), custom_call_target="tpu_custom_call" | custom-call | tf_op jit(solution)/shard_map/unpack/pallas_call | solution.py:810
  (6 shorter events, 0.0 us)
Async XLA Ops:
  3.4 11.6 %collective-permute-start.1 = (f32[648,128]{1,0:T(8,128)S(1)}, f32[648,128]{1,0:T(8,128)S(1)}, u32[]{:S(2)}, u32[]{:S(2)}) collective-permute-start(f32[648,128]{1,0:T(8,128)S(1)} %get-tuple-element.21), channel_id=1, source_target_pairs={{0,16},{8,24},{16,0},{24,8},{1,17},{9,25},{17,1},{25,9},{2,18},{10... | collective-permute-start | bytes 995336 | tf_op jit(solution)/shard_map/ppermute | solution.py:752
  6.4 15.6 %collective-permute-start.8 = (f32[640,128]{1,0:T(8,128)S(1)}, f32[640,128]{1,0:T(8,128)S(1)}, u32[]{:S(2)}, u32[]{:S(2)}) collective-permute-start(f32[640,128]{1,0:T(8,128)S(1)} %get-tuple-element.26), channel_id=1, source_target_pairs={{0,16},{8,24},{16,0},{24,8},{1,17},{9,25},{17,1},{25,9},{2,18},{10... | collective-permute-start | bytes 983048 | tf_op jit(solution)/shard_map/ppermute | solution.py:752
  6.5 5.9 %collective-permute-start.3 = (f32[136,128]{1,0:T(8,128)S(1)}, f32[136,128]{1,0:T(8,128)S(1)}, u32[]{:S(2)}, u32[]{:S(2)}) collective-permute-start(f32[136,128]{1,0:T(8,128)S(1)} %get-tuple-element.22), channel_id=1, source_target_pairs={{8,1},{9,2},{10,3},{11,4},{12,5},{13,6},{14,7},{17,24},{18,25},{19... | collective-permute-start | bytes 208904 | tf_op jit(solution)/shard_map/ppermute | solution.py:766
  7.1 6.4 %collective-permute-start.2 = (f32[136,128]{1,0:T(8,128)S(1)}, f32[136,128]{1,0:T(8,128)S(1)}, u32[]{:S(2)}, u32[]{:S(2)}) collective-permute-start(f32[136,128]{1,0:T(8,128)S(1)} %get-tuple-element.22), channel_id=1, source_target_pairs={{0,1},{1,2},{2,3},{3,4},{4,5},{5,6},{6,7},{25,24},{26,25},{27,26},... | collective-permute-start | bytes 208904 | tf_op jit(solution)/shard_map/ppermute | solution.py:766
  11.6 1.9 %collective-permute-start.5 = (f32[136,128]{1,0:T(8,128)S(1)}, f32[136,128]{1,0:T(8,128)S(1)}, u32[]{:S(2)}, u32[]{:S(2)}) collective-permute-start(f32[136,128]{1,0:T(8,128)S(1)} %get-tuple-element.23), channel_id=1, source_target_pairs={{24,1},{25,2},{26,3},{27,4},{28,5},{29,6},{30,7},{1,24},{2,25},{3,... | collective-permute-start | bytes 208904 | tf_op jit(solution)/shard_map/ppermute | solution.py:766
  12.3 1.2 %collective-permute-start.4 = (f32[136,128]{1,0:T(8,128)S(1)}, f32[136,128]{1,0:T(8,128)S(1)}, u32[]{:S(2)}, u32[]{:S(2)}) collective-permute-start(f32[136,128]{1,0:T(8,128)S(1)} %get-tuple-element.23), channel_id=1, source_target_pairs={{16,1},{17,2},{18,3},{19,4},{20,5},{21,6},{22,7},{9,24},{10,25},{1... | collective-permute-start | bytes 208904 | tf_op jit(solution)/shard_map/ppermute | solution.py:766
  13.6 8.4 %collective-permute-start = (f32[648,128]{1,0:T(8,128)S(1)}, f32[648,128]{1,0:T(8,128)S(1)}, u32[]{:S(2)}, u32[]{:S(2)}) collective-permute-start(f32[648,128]{1,0:T(8,128)S(1)} %get-tuple-element.20.refs_0_), channel_id=1, source_target_pairs={{0,8},{8,0},{16,24},{24,16},{1,9},{9,1},{17,25},{25,17},{2,10},{10... | collective-permute-start | bytes 995336 | tf_op jit(solution)/shard_map/ppermute | solution.py:752
  15.0 8.6 %collective-permute-start.6 = (f32[648,128]{1,0:T(8,128)S(1)}, f32[648,128]{1,0:T(8,128)S(1)}, u32[]{:S(2)}, u32[]{:S(2)}) collective-permute-start(f32[648,128]{1,0:T(8,128)S(1)} %collective-permute-done.1.refs_2_), channel_id=1, source_target_pairs={{0,8},{8,0},{16,24},{24,16},{1,9},{9,1},{17,25},{25,17},{2,10},{10... | collective-permute-start | bytes 995336 | tf_op jit(solution)/shard_map/ppermute | solution.py:752
  15.0 7.0 %collective-permute-start.7 = (f32[640,128]{1,0:T(8,128)S(1)}, f32[640,128]{1,0:T(8,128)S(1)}, u32[]{:S(2)}, u32[]{:S(2)}) collective-permute-start(f32[640,128]{1,0:T(8,128)S(1)} %get-tuple-element.25.refs_4_), channel_id=1, source_target_pairs={{0,8},{8,0},{16,24},{24,16},{1,9},{9,1},{17,25},{25,17},{2,10},{10... | collective-permute-start | bytes 983048 | tf_op jit(solution)/shard_map/ppermute | solution.py:752
  22.0 1.6 %collective-permute-start.9 = (f32[640,128]{1,0:T(8,128)S(1)}, f32[640,128]{1,0:T(8,128)S(1)}, u32[]{:S(2)}, u32[]{:S(2)}) collective-permute-start(f32[640,128]{1,0:T(8,128)S(1)} %collective-permute-done.8.refs_6_), channel_id=1, source_target_pairs={{0,8},{8,0},{16,24},{24,16},{1,9},{9,1},{17,25},{25,17},{2,10},{10... | collective-permute-start | bytes 983048 | tf_op jit(solution)/shard_map/ppermute | solution.py:752
  37.7 4.2 %collective-permute-start.10 = (f32[128,128]{1,0:T(8,128)S(1)}, f32[128,128]{1,0:T(8,128)S(1)}, u32[]{:S(2)}, u32[]{:S(2)}) collective-permute-start(f32[128,128]{1,0:T(8,128)S(1)} %get-tuple-element.32), channel_id=1, source_target_pairs={{0,8},{8,0},{16,24},{24,16},{1,9},{9,1},{17,25},{25,17},{2,10},{10... | collective-permute-start | bytes 196616 | tf_op jit(solution)/shard_map/ppermute | solution.py:752
  37.9 6.4 %collective-permute-start.11 = (f32[128,128]{1,0:T(8,128)S(1)}, f32[128,128]{1,0:T(8,128)S(1)}, u32[]{:S(2)}, u32[]{:S(2)}) collective-permute-start(f32[128,128]{1,0:T(8,128)S(1)} %get-tuple-element.33), channel_id=1, source_target_pairs={{0,16},{8,24},{16,0},{24,8},{1,17},{9,25},{17,1},{25,9},{2,18},{10... | collective-permute-start | bytes 196616 | tf_op jit(solution)/shard_map/ppermute | solution.py:752
  41.9 4.4 %collective-permute-start.12 = (f32[128,128]{1,0:T(8,128)S(1)}, f32[128,128]{1,0:T(8,128)S(1)}, u32[]{:S(2)}, u32[]{:S(2)}) collective-permute-start(f32[128,128]{1,0:T(8,128)S(1)} %get-tuple-element.34), channel_id=1, source_target_pairs={{0,24},{8,16},{16,8},{24,0},{1,25},{9,17},{17,9},{25,1},{2,26},{10... | collective-permute-start | bytes 196616 | tf_op jit(solution)/shard_map/ppermute | solution.py:752

commit v3 on v2

v3 whole, which is shorter than its diff:
```python
import functools

import jax
import jax.numpy as jnp
import ml_dtypes
import numpy as np
from jax import lax
from jax.experimental import pallas as pl
from jax.experimental.pallas import tpu as pltpu
from jax.sharding import PartitionSpec as P

LINE_POINT_TOTAL = 8
FINE = 11
SWEEPS = 4
STEPS = 2
GHOST = STEPS * SWEEPS

time_step = 0.05
relaxation = 0.4
penalty = 30.0

POINTS = LINE_POINT_TOTAL**3
FIELDS = 4
PARTS = ((0,), (1, 2, 3))
PARAM_ROWS = 8
LANES = 128
HALF = LINE_POINT_TOTAL // 2
MIRROR = FINE // 2
CLASSES = ((0, 0), (0, 1), (1, 0), (1, 1))
CLASS_ROWS = HALF * HALF * LINE_POINT_TOTAL


def round_up(value, unit):
    return -(-value // unit) * unit


PAIR_ROWS = round_up(MIRROR * FINE, 8)
MID_ROWS = round_up(FINE, 8)
SLAB_ROWS = 2 * PAIR_ROWS + MID_ROWS
FINE_C_ROWS = (PAIR_ROWS + MID_ROWS, PAIR_ROWS)
FINE_A_COUNT = (MIRROR + 1, MIRROR)


def class_fine_rows(cls):
    return round_up(FINE_A_COUNT[cls[0]] * FINE_C_ROWS[cls[1]], 16)


def legendre_pair(order, points):
    previous = points * 0.0 + 1.0
    current = points * 1.0
    for level in range(2, order + 1):
        previous, current = (
            current,
            ((2 * level - 1) * points * current - (level - 1) * previous) / level,
        )
    return (current, previous)


def make_tables():
    degree = LINE_POINT_TOTAL - 1
    gll_nodes = -np.cos(np.pi * np.arange(LINE_POINT_TOTAL) / degree)
    for repeat in range(100):
        current, previous = legendre_pair(degree, gll_nodes)
        gll_nodes = gll_nodes - (gll_nodes * current - previous) / (LINE_POINT_TOTAL * current)
    values, lower_values = legendre_pair(degree, gll_nodes)
    weights = 2.0 / (degree * (degree + 1) * values**2)
    spatial_derivative = np.zeros((LINE_POINT_TOTAL, LINE_POINT_TOTAL))
    for row_index in range(LINE_POINT_TOTAL):
        for column_index in range(LINE_POINT_TOTAL):
            if row_index != column_index:
                spatial_derivative[row_index, column_index] = values[row_index] / (
                    values[column_index] * (gll_nodes[row_index] - gll_nodes[column_index])
                )
    spatial_derivative[0, 0] = -degree * (degree + 1) / 4.0
    spatial_derivative[-1, -1] = degree * (degree + 1) / 4.0
    fine_nodes = -np.cos(np.pi * (np.arange(FINE) + 0.75) / (FINE + 0.5))
    for repeat in range(100):
        current, previous = legendre_pair(FINE, fine_nodes)
        slope = FINE * (fine_nodes * current - previous) / (fine_nodes * fine_nodes - 1.0)
        fine_nodes = fine_nodes - current / slope
    current, previous = legendre_pair(FINE, fine_nodes)
    slope = FINE * (fine_nodes * current - previous) / (fine_nodes * fine_nodes - 1.0)
    fine_weights = 2.0 / ((1.0 - fine_nodes * fine_nodes) * slope * slope)
    interpolation = np.ones((FINE, LINE_POINT_TOTAL))
    for column_index in range(LINE_POINT_TOTAL):
        for other_index in range(LINE_POINT_TOTAL):
            if other_index != column_index:
                interpolation[:, column_index] *= (fine_nodes - gll_nodes[other_index]) / (
                    gll_nodes[column_index] - gll_nodes[other_index]
                )
    stiffness_1d = spatial_derivative.T @ (weights[:, None] * spatial_derivative)
    return spatial_derivative, interpolation, stiffness_1d, weights, fine_weights


def parity_parts(matrix, out_rows, sign):
    near = matrix[:out_rows, :HALF]
    far = matrix[:out_rows, ::-1][:, :HALF]
    return (near + sign * far) * 0.5


def fine_matrix(cls, line_a, line_b, line_c):
    count_c = FINE_A_COUNT[cls[1]]
    full = np.einsum("xa,yc,zb->xyzacb", line_a, line_c, line_b)
    full = full.reshape(FINE_A_COUNT[cls[0]], count_c, FINE, CLASS_ROWS)
    slabs = np.zeros((FINE_A_COUNT[cls[0]], FINE_C_ROWS[cls[1]], CLASS_ROWS))
    slabs[:, : MIRROR * FINE] = full[:, :MIRROR].reshape(-1, MIRROR * FINE, CLASS_ROWS)
    if cls[1] == 0:
        slabs[:, PAIR_ROWS : PAIR_ROWS + FINE] = full[:, MIRROR]
    result = np.zeros((class_fine_rows(cls), CLASS_ROWS))
    result[: slabs.shape[0] * slabs.shape[1]] = slabs.reshape(-1, CLASS_ROWS)
    return result


def split_stack(matrix):
    high = matrix.astype(ml_dtypes.bfloat16)
    low = (matrix - high.astype(np.float64)).astype(ml_dtypes.bfloat16)
    return np.concatenate(
        [np.concatenate([high, high], 1), np.concatenate([low, low], 1)], 0
    )


def make_matrices():
    derivative, interpolation, stiffness, weights, fine_weights = make_tables()
    slope = interpolation @ derivative
    even = parity_parts(interpolation, MIRROR + 1, 1.0)
    odd = parity_parts(interpolation, MIRROR, -1.0)
    slope_even = parity_parts(slope, MIRROR + 1, -1.0)
    slope_odd = parity_parts(slope, MIRROR, 1.0)
    plain, steep = (even, odd), (slope_even, slope_odd)
    lifts = []
    for direction in (None, 0, 1, 2):
        for cls in CLASSES:
            line_a = (steep if direction == 0 else plain)[cls[0]]
            line_c = (steep if direction == 2 else plain)[cls[1]]
            line_b = slope if direction == 1 else interpolation
            lifts.append(split_stack(fine_matrix(cls, line_a, line_b, line_c)))
    backs = []
    for cls in CLASSES:
        lines = []
        for parity in cls:
            rows = FINE_A_COUNT[parity]
            lines.append(plain[parity] * fine_weights[:rows, None])
        backs.append(
            split_stack(
                fine_matrix(cls, lines[0], interpolation * fine_weights[:, None], lines[1]).T
            )
        )
    stiff = []
    for cls in CLASSES:
        parts = [
            parity_parts(stiffness, HALF, 1.0 - 2.0 * parity)[:HALF] for parity in cls
        ]
        mass = np.diag(weights[:HALF]) * 0.5
        total = (
            np.einsum("ij,kl,mn->ikmjln", parts[0], mass, np.diag(weights))
            + np.einsum("ij,kl,mn->ikmjln", mass, parts[1], np.diag(weights))
            + np.einsum("ij,kl,mn->ikmjln", mass, mass, stiffness)
        )
        stiff.append(split_stack(total.reshape(CLASS_ROWS, CLASS_ROWS)))
    return lifts, backs, stiff


class Layout:
    def __init__(self, elements, sections):
        assert sections & (sections - 1) == 0 and elements == LANES
        self.elements = elements
        self.sections = sections
        self.main = elements // sections
        self.unit = int(np.gcd(self.main, 2 * GHOST))
        assert self.unit in (GHOST, 2 * GHOST)
        self.slot = round_up(self.main + 2 * GHOST, max(self.unit, LANES // sections))
        self.columns = self.slot * sections
        self.tiles = self.columns // LANES
        self.main_rows = POINTS // sections
        self.units = elements // self.unit
        self.unit_rows = POINTS // self.units
        self.window_units = (self.main + 2 * GHOST) // self.unit
        self.slot_units = self.slot // self.unit
        self.end_rows = POINTS // (elements // GHOST)
        self.half = sections // 2
        self.whole_units = elements // 2 // self.unit
        self.tip_row = self.whole_units * self.unit_rows
        self.chunk_rows = self.tip_row + self.end_rows
        self.tips_rows = FIELDS * self.end_rows + PARAM_ROWS

    def window_pieces(self, source, target, width):
        pieces = []
        done = 0
        while done < width:
            at, to = source + done, target + done
            step = min(width - done, LANES - at % LANES, LANES - to % LANES)
            first = to % LANES
            pieces.append((at // LANES, to // LANES, (to - at) % LANES, first, first + step))
            done += step
        return pieces


def lane_iota(rows):
    return lax.broadcasted_iota(jnp.int32, (rows, LANES), 1)


def in_range(lane, first, last):
    return (lane >= first) & (lane < last)


def turned(value, shift):
    if isinstance(shift, int) and shift % value.shape[-1] == 0:
        return value
    return pltpu.roll(value, shift % LANES if isinstance(shift, int) else shift, axis=1)


def exchange_groups(blocks, width):
    blocks = list(blocks)
    count = len(blocks)
    lane = lane_iota(next(block for block in blocks if block is not None).shape[0])
    step = 1
    while step < count:
        keep = (lane & (step * width)) == 0
        for index in range(count):
            if index & step:
                continue
            low, high = blocks[index], blocks[index | step]
            if low is None and high is None:
                continue
            zero = jnp.zeros(lane.shape, jnp.float32)
            up = zero if low is None else turned(low, -step * width)
            down = zero if high is None else turned(high, step * width)
            blocks[index] = jnp.where(keep, zero if low is None else low, down)
            blocks[index | step] = jnp.where(keep, up, zero if high is None else high)
        step *= 2
    return blocks


def pack_field(layout, here, source, own, other, base, packed):
    unit, units, rows = layout.unit, layout.units, layout.unit_rows
    groups = []
    for group in range(units):
        parts = []
        for index in range(group * rows // 8, (group + 1) * rows // 8):
            a, c = divmod(index, LINE_POINT_TOTAL)
            parts.append(source[pl.ds(a * 64 + c, 8, stride=8), :])
        groups.append(pltpu.roll(jnp.concatenate(parts, 0), GHOST, axis=1))
    blocks = exchange_groups(groups, unit)
    for index, value in enumerate(blocks):
        packed[index] = value
    if unit == GHOST:
        high, low = blocks[0], blocks[1]
    else:
        upper, lower = blocks[0][: rows // 2], blocks[0][rows // 2 :]
        keep = (lane_iota(layout.end_rows) & GHOST) == 0
        high = jnp.where(keep, upper, turned(lower, GHOST))
        low = jnp.where(keep, turned(upper, -GHOST), lower)
    region = here // layout.half
    for out, there in ((own, region), (other, 1 - region)):
        first = jnp.where(there == 0, 2 * GHOST // unit, layout.whole_units)
        for index in range(layout.whole_units):
            out[pl.ds(base + index * rows, rows), :] = packed[first + index]
        out[pl.ds(base + layout.tip_row, layout.end_rows), :] = jnp.where(there == 0, low, high)
    return high, low


def pack_kernel(layout, blocks, scalars, *refs):
    inputs, outs, tips = refs[:5], refs[5 : 5 + 2 * len(PARTS)], refs[5 + 2 * len(PARTS)]
    *held, packed, arrived = refs[6 + 2 * len(PARTS) :]
    elements = layout.elements
    here, block = scalars[0], scalars[1]
    pairs = list(zip(inputs, held))
    pairs = pairs[:1] + [(x.at[d], y.at[d]) for x, y in pairs[1:2] for d in range(3)] + pairs[2:]
    copies = [
        pltpu.make_async_copy(source, target, arrived.at[index])
        for index, (source, target) in enumerate(pairs)
    ]
    for copy in copies:
        copy.start()
    rows = layout.end_rows
    for part, fields in enumerate(PARTS):
        for place, field in enumerate(fields):
            copies[field].wait()
            ends = pack_field(
                layout,
                here,
                pairs[field][1],
                outs[2 * part],
                outs[2 * part + 1],
                place * layout.chunk_rows,
                packed,
            )
            for index, end in enumerate(ends):
                tips[pl.ds(index * layout.tips_rows + field * rows, rows), :] = end
    for copy in copies[FIELDS:]:
        copy.wait()
    conductivity, metal, patch = held[2:]
    position = block * elements + lax.broadcasted_iota(jnp.int32, (1, elements), 1)
    zero = jnp.zeros((1, elements), jnp.float32)
    params = jnp.concatenate(
        [
            conductivity[...],
            metal[...].astype(jnp.float32),
            (patch[...] ^ here).astype(jnp.float32),
            jnp.where(position > 0, 1.0, 0.0),
            jnp.where(position < elements * blocks - 1, 1.0, 0.0),
        ]
        + [zero] * (PARAM_ROWS - 5),
        0,
    )
    region = here // layout.half
    for out, there in zip(outs[:2], (region, 1 - region)):
        out[pl.ds(len(PARTS[0]) * layout.chunk_rows, PARAM_ROWS), :] = pltpu.roll(
            params, lax.rem(elements + GHOST - there * (elements // 2), elements), axis=1
        )
    for index, param in enumerate((turned(params, GHOST), params)):
        tips[pl.ds((index + 1) * layout.tips_rows - PARAM_ROWS, PARAM_ROWS), :] = param


def join_kernel(layout, scalars, own, received, early, late):
    here = scalars[0]
    rows = layout.tips_rows
    is_even = lax.rem(here, 2) == 0
    lower = here < layout.half
    own_high, own_low = own[:rows, :], own[rows:, :]
    other_high, other_low = received[:rows, :], received[rows:, :]
    high = [jnp.where(is_even, own_high, other_high), jnp.where(is_even, other_high, own_high)]
    low = [jnp.where(is_even, other_low, own_low), jnp.where(is_even, own_low, other_low)]
    for index in range(2):
        early[pl.ds(index * rows, rows), :] = jnp.where(lower, high[index], low[index])
        late[pl.ds(index * rows, rows), :] = jnp.where(lower, low[index], high[index])


def tip_slice(layout, tips, section, first, rows):
    return tips[section // 2][pl.ds(section % 2 * layout.tips_rows + first, rows), :]


def unpack_field(layout, here, field, chunks, base, tips, target):
    sections, unit, rows = layout.sections, layout.unit, layout.unit_rows
    end_rows = layout.end_rows
    region, within = here // layout.half, lax.rem(here, layout.half)
    skipped = jnp.where(region == 0, 2 * GHOST // unit, 0)
    at_first, at_last = here == 0, here == sections - 1
    per_tile = LANES // unit
    final = layout.window_units - 1

    def merged(left, right):
        keep = (lane_iota(end_rows) & GHOST) == 0
        return jnp.concatenate(
            [
                jnp.where(keep, left, turned(right, GHOST)),
                jnp.where(keep, turned(left, -GHOST), right),
            ],
            0,
        )

    def unit_block(section, index):
        place = jnp.clip(
            within * (layout.main // unit) + index - skipped, 0, layout.whole_units - 1
        )
        block = chunks[section][pl.ds(pl.multiple_of(base + place * rows, 8), rows), :]
        inner = chunks[section][pl.ds(base + layout.tip_row, end_rows), :]
        outer = tip_slice(layout, tips, section, field * end_rows, end_rows)
        if unit == GHOST:
            if index == 0:
                block = jnp.where(at_first, outer, block)
            if index == 1:
                block = jnp.where(at_first, inner, block)
            if index == final - 1:
                block = jnp.where(at_last, inner, block)
            if index == final:
                block = jnp.where(at_last, outer, block)
            return block
        if index == 0:
            block = jnp.where(at_first, merged(outer, inner), block)
        if index == final:
            block = jnp.where(at_last, merged(inner, outer), block)
        return block

    for tile in range(layout.tiles):
        blocks = []
        for place in range(per_tile):
            section, index = divmod(tile * per_tile + place, layout.slot_units)
            blocks.append(unit_block(section, index) if index <= final else None)
        for group, value in enumerate(exchange_groups(blocks, unit)):
            target[pl.ds(group * rows, rows), pl.ds(tile * LANES, LANES)] = value


def unpack_params(layout, here, chunks, tips):
    sections = layout.sections
    within = lax.rem(here, layout.half)
    at_first, at_last = here == 0, here == sections - 1
    lane = lane_iota(PARAM_ROWS)
    after = GHOST + layout.main
    values = [jnp.zeros((PARAM_ROWS, LANES), jnp.float32) for _ in range(layout.tiles)]
    for section in range(sections):
        block = pltpu.roll(
            chunks[section][pl.ds(len(PARTS[0]) * layout.chunk_rows, PARAM_ROWS), :],
            lax.rem(LANES - within * layout.main, LANES),
            axis=1,
        )
        end = tip_slice(layout, tips, section, FIELDS * layout.end_rows, PARAM_ROWS)
        block = jnp.where(at_first & (lane < GHOST), end, block)
        block = jnp.where(
            at_last & in_range(lane, after, after + GHOST), turned(end, after), block
        )
        for _, tile, shift, first, last in layout.window_pieces(
            0, section * layout.slot, after + GHOST
        ):
            values[tile] = jnp.where(in_range(lane, first, last), turned(block, shift), values[tile])
    return jnp.concatenate(values, 1)


def store_split(target, row, half, value):
    high = value.astype(jnp.bfloat16)
    target[pl.ds(row, value.shape[0]), :] = high
    target[pl.ds(half + row, value.shape[0]), :] = (value - high.astype(jnp.float32)).astype(
        jnp.bfloat16
    )


def to_classes(source, pieces):
    for a in range(HALF):
        near = source[pl.ds(a * 64, 64), :]
        far = source[pl.ds((LINE_POINT_TOTAL - 1 - a) * 64, 64), :]
        for parity_a, slab in enumerate((near + far, near - far)):
            lower = slab[: HALF * 8]
            upper = jnp.concatenate(
                [slab[(LINE_POINT_TOTAL - 1 - c) * 8 :][:8] for c in range(HALF)], 0
            )
            for parity_c, part in enumerate((lower + upper, lower - upper)):
                store_split(pieces[2 * parity_a + parity_c], a * HALF * 8, CLASS_ROWS, part)


def multiply(matrix, pieces):
    product = jnp.dot(matrix[...], pieces[...], preferred_element_type=jnp.float32)
    half = product.shape[0] // 2
    return product[:half] + product[half:]


def from_classes(results, a):
    span = pl.ds(a * HALF * 8, HALF * 8)
    ee, eo, oe, oo = [results[index, span, :] for index in range(4)]

    def along_c(even, odd):
        lower, upper = even + odd, even - odd
        return jnp.concatenate(
            [lower] + [upper[c * 8 : c * 8 + 8] for c in reversed(range(HALF))], 0
        )

    return along_c(ee + oe, eo + oo), along_c(ee - oe, eo - oo)


def fine_slabs(fine, q):
    halves = []
    for parity_a in range(2):
        if q >= FINE_A_COUNT[parity_a]:
            break
        even = fine[2 * parity_a][pl.ds(q * FINE_C_ROWS[0], FINE_C_ROWS[0]), :]
        odd = fine[2 * parity_a + 1][pl.ds(q * FINE_C_ROWS[1], FINE_C_ROWS[1]), :]
        halves.append((even[:PAIR_ROWS] + odd, even[:PAIR_ROWS] - odd, even[PAIR_ROWS:]))
    if len(halves) == 1:
        return [halves[0]]
    return [
        tuple(x + y for x, y in zip(*halves)),
        tuple(x - y for x, y in zip(*halves)),
    ]


HEIGHTS = [2 * class_fine_rows(cls) for cls in CLASSES]
TALL = np.concatenate([[0], np.cumsum(HEIGHTS * 4 + [2 * CLASS_ROWS] * 4)]).tolist()
WIDE = np.concatenate([[0], np.cumsum([round_up(rows, LANES) for rows in HEIGHTS])]).tolist()


def lift_matrix(tall, direction, index):
    at = 4 * direction + index
    return tall.at[pl.ds(TALL[at], TALL[at + 1] - TALL[at])]


def shifted(value, amount):
    return pltpu.roll(value, amount % value.shape[1], axis=1)


def column_weights(line, columns):
    row = lax.broadcasted_iota(jnp.int32, (LINE_POINT_TOTAL, columns), 0)
    value = jnp.zeros((LINE_POINT_TOTAL, columns), jnp.float32)
    for b in range(LINE_POINT_TOTAL):
        value = jnp.where(row == b, float(line[b]), value)
    return value


def wall_distance(layout, params):
    lane = lax.broadcasted_iota(jnp.int32, (1, layout.columns), 1)
    own_slot = lane // layout.slot
    partner_slot = own_slot ^ params[2:3].astype(jnp.int32)
    return lax.rem(partner_slot - own_slot + layout.sections, layout.sections)


def store_slabs(fine, target):
    for q in range(MIRROR + 1):
        for point, slab in zip((q, FINE - 1 - q), fine_slabs(fine, q)):
            base = 0
            for part in slab:
                target[point, pl.ds(base, part.shape[0]), :] = part
                base += part.shape[0]


def gradients(tall, pieces, fine):
    for direction in range(3):
        for index in range(4):
            source = index ^ (2 if direction == 0 else 1 if direction == 2 else 0)
            fine[direction][index][...] = multiply(
                lift_matrix(tall, direction + 1, index), pieces[source]
            )


def start_kernel(layout, tables, scalars, *refs):
    sections, columns = layout.sections, layout.columns
    here = scalars[0]
    refs = list(refs)

    def take(count):
        taken, refs[:] = refs[:count], refs[count:]
        return taken

    chunks, tips, stored = take(sections), take(sections // 2), take(2)
    (iterate, param_value, keep, gain_k, gain, gain_low, gain_high, gain_wall) = take(8)
    slopes, (tall, wide) = take(3), take(2)
    fine, pieces, (arrived,) = take(4), take(4), take(1)
    copies = [
        pltpu.make_async_copy(
            stored[0].at[pl.ds(i, j - i)], tall.at[pl.ds(i, j - i)], arrived.at[index]
        )
        for index, (i, j) in enumerate(zip(TALL[0:17:4], TALL[4:21:4]))
    ]
    copies.append(pltpu.make_async_copy(stored[1], wide, arrived.at[5]))
    for index in (1, 2, 3, 0, 4, 5):
        copies[index].start()

    unpack_field(layout, here, 0, chunks, 0, tips, iterate)
    params = unpack_params(layout, here, chunks, tips)
    param_value[...] = params
    to_classes(iterate, pieces)
    for direction in range(3):
        copies[direction + 1].wait()
        for index in range(4):
            source = index ^ (2 if direction == 0 else 1 if direction == 2 else 0)
            fine[index][...] = multiply(lift_matrix(tall, direction + 1, index), pieces[source])
        store_slabs(fine, slopes[direction])

    weights, stiff_line = tables[3], np.diagonal(tables[2])
    k, metal, _, has_low, has_high = [params[row : row + 1] for row in range(5)]
    distance = wall_distance(layout, params)
    coef_low = has_low * (0.5 * penalty) * (k + shifted(k, 1))
    coef_high = has_high * (0.5 * penalty) * (k + shifted(k, -1))
    partner_k, partner_metal = jnp.zeros_like(k), jnp.zeros_like(k)
    for step in range(1, sections):
        chosen = distance == step
        partner_k = jnp.where(chosen, shifted(k, -step * layout.slot), partner_k)
        partner_metal = jnp.where(chosen, shifted(metal, -step * layout.slot), partner_metal)
    coef_wall = jnp.where(metal != partner_metal, (0.5 * penalty) * (k + partner_k), 0.0)
    weight_b = column_weights(weights, columns)
    stiff_b = column_weights(stiff_line, columns)
    last = LINE_POINT_TOTAL - 1
    for a in range(LINE_POINT_TOTAL):
        for c in range(LINE_POINT_TOTAL):
            wa, wc = float(weights[a]), float(weights[c])
            mass = weight_b * (wa * wc / time_step)
            diag = mass + k * (
                weight_b * (float(stiff_line[a]) * wc + wa * float(stiff_line[c]))
                + stiff_b * (wa * wc)
            )
            face = None
            if a == 0:
                face_low = coef_low * (weight_b * wc)
                face = face_low
            if a == last:
                face_high = coef_high * (weight_b * wc)
                face = face_high
            if c == 0:
                face_wall = coef_wall * (weight_b * wa)
                face = face_wall if face is None else face + face_wall
            if face is not None:
                diag = diag + face
            factor = relaxation / diag
            span = pl.ds((a * 8 + c) * 8, 8)
            gain[span, :] = factor
            gain_k[span, :] = factor * k
            keep[span, :] = 1.0 - factor * (mass if face is None else mass + face)
            if a == 0:
                gain_low[pl.ds(c * 8, 8), :] = factor * face_low
            if a == last:
                gain_high[pl.ds(c * 8, 8), :] = factor * face_high
            if c == 0:
                gain_wall[pl.ds(a * 8, 8), :] = factor * face_wall
    for index in (0, 4, 5):
        copies[index].wait()


def point_slabs(source, q):
    slabs = []
    for point in (q, FINE - 1 - q)[: 1 if q == MIRROR else 2]:
        slabs.append(
            [
                source[point, pl.ds(0, PAIR_ROWS), :],
                source[point, pl.ds(PAIR_ROWS, PAIR_ROWS), :],
                source[point, pl.ds(2 * PAIR_ROWS, MID_ROWS), :],
            ]
        )
    return slabs


def add_products(total, slabs, others):
    terms = [[x * y for x, y in zip(s, t)] for s, t in zip(slabs, others)]
    if total is None:
        return terms
    return [[x + y for x, y in zip(s, t)] for s, t in zip(total, terms)]


def project(layout, products_of, wide, fine_pieces, results):
    pending = [[], [], [], []]
    done = [0, 0, 0, 0]
    for q in range(MIRROR + 1):
        products = products_of(q)
        halves = products
        if len(products) == 2:
            halves = [
                [x + y for x, y in zip(*products)],
                [x - y for x, y in zip(*products)],
            ]
        for parity_a, (plus, minus, middle) in enumerate(halves):
            pending[2 * parity_a] += [plus + minus, middle]
            pending[2 * parity_a + 1].append(plus - minus)
        for index, cls in enumerate(CLASSES):
            held = sum(part.shape[0] for part in pending[index])
            final = q >= FINE_A_COUNT[cls[0]] - 1
            if pending[index] and (held % 16 == 0 or final):
                if held % 16:
                    pending[index].append(jnp.zeros((8, layout.columns), jnp.float32))
                    held += 8
                store_split(
                    fine_pieces[index],
                    done[index],
                    class_fine_rows(cls),
                    jnp.concatenate(pending[index], 0),
                )
                done[index] += held
                pending[index] = []
    for index in range(4):
        back = wide.at[:, pl.ds(WIDE[index], HEIGHTS[index])]
        results[index] = multiply(back, fine_pieces[index])


def march_kernel(layout, tables, scalars, *refs):
    weights = tables[3]
    sections, columns = layout.sections, layout.columns
    refs = list(refs)

    def take(count):
        taken, refs[:] = refs[:count], refs[count:]
        return taken

    chunks, tips = [take(sections) for _ in PARTS], take(sections // 2)
    (initial, param_value, keep, gain_k, gain, gain_low, gain_high, gain_wall) = take(8)
    slopes, (tall, wide) = take(3), take(2)
    outs = take(sections)
    (iterate, held, results, gain_rhs) = take(4)
    lifted = take(3)
    fine, pieces, fine_pieces = [take(4) for _ in range(3)], take(4), take(4)

    for d in range(3):
        part = next(index for index, inside in enumerate(PARTS) if 1 + d in inside)
        base = PARTS[part].index(1 + d) * layout.chunk_rows
        unpack_field(layout, scalars[0], 1 + d, chunks[part], base, tips, held)
        to_classes(held, pieces)
        for index in range(4):
            fine[0][index][...] = multiply(lift_matrix(tall, 0, index), pieces[index])
        store_slabs(fine[0], lifted[d])
    params = param_value[...]
    distance = wall_distance(layout, params)
    fluid = 1.0 - params[1:2]
    weight_b = column_weights(weights, columns)
    last = LINE_POINT_TOTAL - 1

    def first_products(q):
        total = None
        for slope, velocity in zip(slopes, lifted):
            total = add_products(total, point_slabs(slope, q), point_slabs(velocity, q))
        return total

    def later_products(q):
        total = None
        for slope, velocity in zip(fine, lifted):
            total = add_products(total, fine_slabs(slope, q), point_slabs(velocity, q))
        return total

    for step_index in range(STEPS):
        current = initial if step_index == 0 else iterate
        if step_index == 0:
            project(layout, first_products, wide, fine_pieces, results)
        else:
            to_classes(current, pieces)
            gradients(tall, pieces, fine)
            project(layout, later_products, wide, fine_pieces, results)
        for a in range(HALF):
            for plane, convected in zip((a, last - a), from_classes(results, a)):
                for c in range(LINE_POINT_TOTAL):
                    span = pl.ds((plane * 8 + c) * 8, 8)
                    mass = weight_b * float(weights[plane] * weights[c] / time_step)
                    gain_rhs[span, :] = gain[span, :] * (
                        mass * current[span, :] - fluid * convected[c * 8 : c * 8 + 8]
                    )
        for sweep_index in range(SWEEPS):
            current = initial if step_index == 0 and sweep_index == 0 else iterate
            if step_index == 0 or sweep_index > 0:
                to_classes(current, pieces)
            for index in range(4):
                stiff = tall.at[pl.ds(TALL[16 + index], 2 * CLASS_ROWS)]
                results[index] = multiply(stiff, pieces[index])
            from_low = gain_low[...] * shifted(current[pl.ds(last * 64, 64), :], 1)
            from_high = gain_high[...] * shifted(current[pl.ds(0, 64), :], -1)
            wall = jnp.concatenate([current[pl.ds(a * 64, 8), :] for a in range(8)], 0)
            far = jnp.zeros_like(wall)
            for step in range(1, sections):
                far = jnp.where(distance == step, shifted(wall, -step * layout.slot), far)
            from_wall = gain_wall[...] * far
            for a in range(HALF):
                for plane, stiffness in zip((a, last - a), from_classes(results, a)):
                    span = pl.ds(plane * 64, 64)
                    value = (
                        keep[span, :] * current[span, :]
                        + gain_rhs[span, :]
                        - gain_k[span, :] * stiffness
                    )
                    if plane == 0:
                        value = value + from_low
                    if plane == last:
                        value = value + from_high
                    at_wall = value[:8] + from_wall[plane * 8 : plane * 8 + 8]
                    iterate[span, :] = jnp.concatenate([at_wall, value[8:]], 0)

    rows = layout.main_rows
    lane = lane_iota(rows)
    for section in range(sections):
        value = jnp.zeros((rows, LANES), jnp.float32)
        for group in range(sections):
            for tile, _, shift, first, last_lane in layout.window_pieces(
                section * layout.slot + GHOST, group * layout.main, layout.main
            ):
                block = iterate[pl.ds(group * rows, rows), pl.ds(tile * LANES, LANES)]
                value = jnp.where(in_range(lane, first, last_lane), turned(block, shift), value)
        outs[section][...] = value


def gather_kernel(layout, scalars, *refs):
    chunks, (out, held, sent) = refs[: layout.sections], refs[layout.sections :]
    here = scalars[0]
    rows, main, elements = layout.main_rows, layout.main, layout.elements
    lane = lane_iota(rows)
    places = [here ^ shift for shift in range(layout.sections)]
    copies = []
    for group in range(layout.sections):
        value = None
        for shift, there in enumerate(places):
            amount = lax.rem((there - group) * main + elements, elements)
            part = pltpu.roll(chunks[shift][...], amount, axis=1)
            value = (
                part
                if value is None
                else jnp.where(in_range(lane, there * main, (there + 1) * main), part, value)
            )
        for index in range(rows // 8):
            a, c = divmod(group * (rows // 8) + index, LINE_POINT_TOTAL)
            held[pl.ds(a * 64 + c, 8, stride=8), :] = value[index * 8 : index * 8 + 8]
        planes = (group + 1) * rows // 64
        if planes > group * rows // 64:
            span = pl.ds((planes - max(1, rows // 64)) * 64, max(64, rows))
            copy = pltpu.make_async_copy(held.at[span], out.at[span], sent.at[group])
            copy.start()
            copies.append(copy)
    for copy in copies:
        copy.wait()


def shape_of(*dims, dtype=jnp.float32):
    return jax.ShapeDtypeStruct(dims, dtype)


def in_vmem(count):
    return [pl.BlockSpec(memory_space=pltpu.VMEM)] * count


def in_hbm(count):
    return [pl.BlockSpec(memory_space=pltpu.HBM)] * count


def kept_in_hbm(array):
    return pltpu.with_memory_space_constraint(array, pltpu.HBM)


FLOPS_BUSY = 1e8


SCALAR = pl.BlockSpec(memory_space=pltpu.SMEM)
PARAMS = pltpu.CompilerParams(vmem_limit_bytes=24 * 1024 * 1024)


def body(
    thermal_level_points,
    flow_speed_vector,
    thermal_diffusivity_cell,
    metal_cell_indicator,
    adjoining_patch,
):
    sections = lax.axis_size("sec")
    blocks = lax.axis_size("elem")
    elements = thermal_diffusivity_cell.shape[1]
    layout = Layout(elements, sections)
    scalars = jnp.stack([lax.axis_index("sec"), lax.axis_index("elem")]).astype(jnp.int32)
    f32, bf16 = jnp.float32, jnp.bfloat16
    dma = pltpu.SemaphoreType.DMA

    columns = layout.columns

    def call(kernel, name, out_shape, arrays, hbm=(), scratch=(), out_specs=None, busy=1.0):
        results = pl.pallas_call(
            kernel,
            out_shape=out_shape,
            in_specs=[SCALAR] + in_vmem(len(arrays)) + in_hbm(len(hbm)),
            out_specs=in_vmem(len(out_shape)) if out_specs is None else out_specs,
            scratch_shapes=list(scratch),
            compiler_params=PARAMS,
            cost_estimate=pl.CostEstimate(
                flops=int(busy * FLOPS_BUSY), bytes_accessed=0, transcendentals=0
            ),
            name=name,
        )(scalars, *arrays, *[kept_in_hbm(array) for array in hbm])
        return list(results)

    chunk_shapes = [
        shape_of(len(fields) * layout.chunk_rows + extra, elements)
        for fields, extra in zip(PARTS, (PARAM_ROWS, 0))
        for _ in range(2)
    ]
    *packed, tips = call(
        functools.partial(pack_kernel, layout, blocks),
        "pack",
        chunk_shapes + [shape_of(2 * layout.tips_rows, elements)],
        [],
        hbm=[
            thermal_level_points.reshape(POINTS, elements),
            flow_speed_vector.reshape(3, POINTS, elements),
            thermal_diffusivity_cell,
            metal_cell_indicator,
            adjoining_patch,
        ],
        scratch=[
            pltpu.VMEM((POINTS, elements), f32),
            pltpu.VMEM((3, POINTS, elements), f32),
            pltpu.VMEM((1, elements), f32),
            pltpu.VMEM((1, elements), jnp.int32),
            pltpu.VMEM((1, elements), jnp.int32),
            pltpu.VMEM((layout.units, layout.unit_rows, elements), f32),
            dma((7,)),
        ],
        busy=3.3,
    )

    def across(array, mask):
        return lax.ppermute(array, "sec", [(i, i ^ mask) for i in range(sections)])

    chunks = [
        {0: packed[2 * part], layout.half: across(packed[2 * part + 1], layout.half)}
        for part in range(len(PARTS))
    ]
    early, late = call(
        functools.partial(join_kernel, layout),
        "join",
        [shape_of(2 * layout.tips_rows, elements)] * 2,
        [tips, across(tips, 1)],
        busy=0.6,
    )
    tips = []
    for step in range(sections // 2):
        mirrored = sections // 2 - 1 - step
        up, down = 2 * step + 1, 2 * mirrored + 1
        pairs = [(up * blocks + i, i + 1) for i in range(blocks - 1)]
        pairs += [
            (down * blocks + i + 1, (sections - 1) * blocks + i) for i in range(blocks - 1)
        ]
        tips.append(
            lax.ppermute(early if step < sections // 4 else late, ("sec", "elem"), pairs)
        )
    def spread(chunk, after):
        chunk[layout.half], after = lax.optimization_barrier((chunk[layout.half], after))
        bit = layout.half // 2
        while bit:
            for mask in sorted(chunk):
                chunk[mask | bit] = across(chunk[mask], bit)
            bit //= 2
        return [chunk[mask] for mask in range(sections)], after

    chunks[0], tips = spread(chunks[0], tips)

    lifts, backs, stiff = make_matrices()
    tall = jnp.asarray(np.concatenate(lifts + stiff, 0))
    wide = jnp.asarray(
        np.concatenate(
            [
                np.pad(back, ((0, 0), (0, round_up(back.shape[1], LANES) - back.shape[1])))
                for back in backs
            ],
            1,
        )
    )
    tables = make_tables()
    fine_rows = [class_fine_rows(cls) for cls in CLASSES]
    points = shape_of(POINTS, columns)
    fine_field = shape_of(FINE, SLAB_ROWS, columns)
    face = shape_of(64, columns)
    fine_scratch = [pltpu.VMEM((rows, columns), f32) for rows in fine_rows]
    piece_scratch = [pltpu.VMEM((2 * CLASS_ROWS, columns), bf16) for _ in CLASSES]
    started = call(
        functools.partial(start_kernel, layout, tables),
        "start",
        [points, shape_of(PARAM_ROWS, columns)]
        + [points] * 3
        + [face] * 3
        + [fine_field] * 3
        + [shape_of(*tall.shape, dtype=bf16), shape_of(*wide.shape, dtype=bf16)],
        chunks[0] + tips,
        hbm=[tall, wide],
        scratch=fine_scratch + piece_scratch + [dma((6,))],
        busy=25.0,
    )
    factors, slopes, (tall, wide) = started[:8], started[8:11], started[11:]
    chunks[1], factors[1] = spread(chunks[1], factors[1])
    results = call(
        functools.partial(march_kernel, layout, tables),
        "march",
        [shape_of(layout.main_rows, elements)] * sections,
        chunks[0] + chunks[1] + tips + factors + slopes + [tall, wide],
        scratch=[
            pltpu.VMEM((POINTS, columns), f32),
            pltpu.VMEM((POINTS, columns), f32),
            pltpu.VMEM((4, CLASS_ROWS, columns), f32),
            pltpu.VMEM((POINTS, columns), f32),
            *[pltpu.VMEM((FINE, SLAB_ROWS, columns), f32) for _ in range(3)],
            *(fine_scratch * 3),
            *piece_scratch,
            *[pltpu.VMEM((2 * rows, columns), bf16) for rows in fine_rows],
        ],
        busy=8.9,
    )
    results = [results[0]] + [across(results[mask], mask) for mask in range(1, sections)]
    (result,) = call(
        functools.partial(gather_kernel, layout),
        "unpack",
        [shape_of(POINTS, elements)],
        list(results),
        scratch=[pltpu.VMEM((POINTS, elements), f32), dma((sections,))],
        out_specs=in_hbm(1),
        busy=1.5,
    )
    return result.reshape(thermal_level_points.shape)


def solution(mesh):
    return jax.shard_map(
        body,
        mesh=mesh,
        in_specs=(
            P("sec", None, None, None, "elem"),
            P(None, "sec", None, None, None, "elem"),
            P("sec", "elem"),
            P("sec", "elem"),
            P("sec", "elem"),
        ),
        out_specs=P("sec", None, None, None, "elem"),
        check_vma=False,
    )
```

time: 48.1 us -> 42.8 us (0.89)
  waiting for transfers between devices: 14.4 us -> 6.86 us
  Pallas kernels: 19 us -> 20.2 us
  starting transfers between devices: 14.3 us -> 15.4 us
    ppermute x9 -> x10, waiting for transfers between devices: 13.9 us -> 6.86 us  [across(): return lax.ppermute(array, 'sec', [(i, i ^ mask) for i in range(sections)])]
    ppermute x9 -> x10, starting transfers between devices: 7.84 us -> 14 us  [across(): return lax.ppermute(array, 'sec', [(i, i ^ mask) for i in range(sections)])]
    ppermute x4 -> x2, starting transfers between devices: 6.49 us -> 1.34 us  [body(): lax.ppermute(early if step < sections // 4 else late, ('sec', 'elem'), pa...]
    pallas_call x3 -> x5, Pallas kernels: 19 us -> 20.2 us  [call(): pl.pallas_call(kernel, out_shape=out_shape, in_specs=[SCALAR] + in_vmem(l...]
    ppermute x4 -> x2, waiting for transfers between devices: 0.57 us -> 0.01 us  [body(): lax.ppermute(early if step < sections // 4 else late, ('sec', 'elem'), pa...]
  transfers between devices with their start and end apart: 13 -> 12, of which waited for: 6 -> 6; matrix products, arithmetic and copies ran while one was open for 0% -> 0% of each run, Pallas kernels for 0% -> 12%
where the time goes in v3:
time: 42.8 us; the launch traced here: 42.6 us
  Pallas kernels  20.2 us (47%)
  starting transfers between devices  15.4 us (36%)
  waiting for transfers between devices  6.86 us (16%)
    pallas_call x5, Pallas kernels, call(): pl.pallas_call(kernel, out_shape=out_shape, in_specs=[SCALAR] + in_vmem(l...  20.2 us
    ppermute x10, starting transfers between devices, across(): return lax.ppermute(array, 'sec', [(i, i ^ mask) for i in range(sections)])  14 us
    ppermute x10, waiting for transfers between devices, across(): return lax.ppermute(array, 'sec', [(i, i ^ mask) for i in range(sections)])  6.86 us
    ppermute x2, starting transfers between devices, body(): lax.ppermute(early if step < sections // 4 else late, ('sec', 'elem'), pa...  1.34 us
  transfers between devices with their start and end apart: 12, of which 6 were waited for; matrix products, arithmetic and copies ran while one was open for 0% of the time, Pallas kernels for 12%

profile of v3, /device:TPU:0, one launch (start us, length us, event | category | flops | bytes accessed | tf_op | source)
XLA Modules:
  0.0 42.6 jit_solution(15851630658405970414)
XLA Ops:
  0.0 0.1 pad_add_fusion.scalars
  0.1 3.4 %pack.1 = (f32[296,128]{1,0:T(8,128)S(1)}, f32[296,128]{1,0:T(8,128)S(1)}, f32[864,128]{1,0:T(8,128)S(1)}, f32[864,128]{1,0:T(8,128)S(1)}, f32[272,128]{1,0:T(8,128)S(1)}) custom-call(s32[2]{0:T(128)S(1)} %pad_add_fusion.scalars, f32[512,128]{1,0:T(8,128)} %bitcast.6, f32[3,512,128]{2,1,0:T(8,128)} %bitcast.5, f32[1,128]{1,0:T(1,128)} %refs_2_.1, ...), custom_call_target="tpu_custom_call" | custom-call | flops 330000000 | tf_op jit(solution)/shard_map/pack/pallas_call | solution.py:821
  3.4 0.5 %collective-permute-start.2 = (f32[272,128]{1,0:T(8,128)S(1)}, f32[272,128]{1,0:T(8,128)S(1)}, u32[]{:S(2)}, u32[]{:S(2)}) collective-permute-start(f32[272,128]{1,0:T(8,128)S(1)} %get-tuple-element.36.own), channel_id=1, source_target_pairs={{0,8},{8,0},{16,24},{24,16},{1,9},{9,1},{17,25},{25,17},{2,10},{10... | collective-permute-start | bytes 417800 | tf_op jit(solution)/shard_map/ppermute | solution.py:865
  4.0 2.6 %collective-permute-start.1 = (f32[296,128]{1,0:T(8,128)S(1)}, f32[296,128]{1,0:T(8,128)S(1)}, u32[]{:S(2)}, u32[]{:S(2)}) collective-permute-start(f32[296,128]{1,0:T(8,128)S(1)} %get-tuple-element.35), channel_id=1, source_target_pairs={{0,16},{8,24},{16,0},{24,8},{1,17},{9,25},{17,1},{25,9},{2,18},{10... | collective-permute-start | bytes 454664 | tf_op jit(solution)/shard_map/ppermute | solution.py:865
  6.5 0.6 %join.1 = (f32[272,128]{1,0:T(8,128)S(1)}, f32[272,128]{1,0:T(8,128)S(1)}) custom-call(s32[2]{0:T(128)S(1)} %pad_add_fusion.scalars, f32[272,128]{1,0:T(8,128)S(1)} %get-tuple-element.36.own, f32[272,128]{1,0:T(8,128)S(1)} %collective-permute-done.2.received), custom_call_target="tpu_custom_call" | custom-call | flops 60000000 | tf_op jit(solution)/shard_map/join/pallas_call | solution.py:821
  7.1 0.7 %collective-permute-start.3 = (f32[272,128]{1,0:T(8,128)S(1)}, f32[272,128]{1,0:T(8,128)S(1)}, u32[]{:S(2)}, u32[]{:S(2)}) collective-permute-start(f32[272,128]{1,0:T(8,128)S(1)} %get-tuple-element.37), channel_id=1, source_target_pairs={{8,1},{9,2},{10,3},{11,4},{12,5},{13,6},{14,7},{25,24},{26,25},{27... | collective-permute-start | bytes 417800 | tf_op jit(solution)/shard_map/ppermute | solution.py:887
  7.8 0.7 %collective-permute-start.4 = (f32[272,128]{1,0:T(8,128)S(1)}, f32[272,128]{1,0:T(8,128)S(1)}, u32[]{:S(2)}, u32[]{:S(2)}) collective-permute-start(f32[272,128]{1,0:T(8,128)S(1)} %get-tuple-element.38), channel_id=1, source_target_pairs={{24,1},{25,2},{26,3},{27,4},{28,5},{29,6},{30,7},{9,24},{10,25},{1... | collective-permute-start | bytes 417800 | tf_op jit(solution)/shard_map/ppermute | solution.py:887
  8.5 1.3 %collective-permute-start.7 = (f32[864,128]{1,0:T(8,128)S(1)}, f32[864,128]{1,0:T(8,128)S(1)}, u32[]{:S(2)}, u32[]{:S(2)}) collective-permute-start(f32[864,128]{1,0:T(8,128)S(1)} %get-tuple-element.41), channel_id=1, source_target_pairs={{0,16},{8,24},{16,0},{24,8},{1,17},{9,25},{17,1},{25,9},{2,18},{10... | collective-permute-start | bytes 1327112 | tf_op jit(solution)/shard_map/ppermute | solution.py:865
  9.8 3.4 %collective-permute-start = (f32[296,128]{1,0:T(8,128)S(1)}, f32[296,128]{1,0:T(8,128)S(1)}, u32[]{:S(2)}, u32[]{:S(2)}) collective-permute-start(f32[296,128]{1,0:T(8,128)S(1)} %get-tuple-element.34.refs_0_), channel_id=1, source_target_pairs={{0,8},{8,0},{16,24},{24,16},{1,9},{9,1},{17,25},{25,17},{2,10},{10... | collective-permute-start | bytes 454664 | tf_op jit(solution)/shard_map/ppermute | solution.py:865
  13.2 0.0 collective-permute-done.1.refs_2_
  13.2 0.1 collective-permute-start.5
  13.3 0.5 %collective-permute-start.6 = (f32[864,128]{1,0:T(8,128)S(1)}, f32[864,128]{1,0:T(8,128)S(1)}, u32[]{:S(2)}, u32[]{:S(2)}) collective-permute-start(f32[864,128]{1,0:T(8,128)S(1)} %get-tuple-element.40.refs_4_), channel_id=1, source_target_pairs={{0,8},{8,0},{16,24},{24,16},{1,9},{9,1},{17,25},{25,17},{2,10},{10... | collective-permute-start | bytes 1327112 | tf_op jit(solution)/shard_map/ppermute | solution.py:865
  13.8 0.4 collective-permute-done.refs_1_
  14.2 0.4 %collective-permute-done.5.refs_3_ = f32[296,128]{1,0:T(8,128)S(1)} collective-permute-done((f32[296,128]{1,0:T(8,128)S(1)}, f32[296,128]{1,0:T(8,128)S(1)}, u32[]{:S(2)}, u32[]{:S(2)}) %collective-permute-start.5) | collective-permute-done | bytes 151584 | tf_op jit(solution)/shard_map/ppermute | solution.py:865
  14.7 4.4 %start.1 = (f32[512,256]{1,0:T(8,128)S(1)}, f32[8,256]{1,0:T(8,128)S(1)}, f32[512,256]{1,0:T(8,128)S(1)}, f32[512,256]{1,0:T(8,128)S(1)}, f32[512,256]{1,0:T(8,1...) custom-call(s32[2]{0:T(128)S(1)} %pad_add_fusion.scalars, ...), custom_call_target="tpu_custom_call" | custom-call | flops 2500000000 | tf_op jit(solution)/shard_map/start/pallas_call | solution.py:821
  19.1 0.2 collective-permute-done.7.refs_6_
  19.4 3.5 %collective-permute-start.8 = (f32[864,128]{1,0:T(8,128)S(1)}, f32[864,128]{1,0:T(8,128)S(1)}, u32[]{:S(2)}, u32[]{:S(2)}) collective-permute-start(f32[864,128]{1,0:T(8,128)S(1)} %collective-permute-done.7.refs_6_), channel_id=1, source_target_pairs={{0,8},{8,0},{16,24},{24,16},{1,9},{9,1},{17,25},{25,17},{2,10},{10... | collective-permute-start | bytes 1327112 | tf_op jit(solution)/shard_map/ppermute | solution.py:865
  22.9 1.4 %collective-permute-done.8.refs_7_ = f32[864,128]{1,0:T(8,128)S(1)} collective-permute-done((f32[864,128]{1,0:T(8,128)S(1)}, f32[864,128]{1,0:T(8,128)S(1)}, u32[]{:S(2)}, u32[]{:S(2)}) %collective-permute-start.8) | collective-permute-done | bytes 442400 | tf_op jit(solution)/shard_map/ppermute | solution.py:865
  24.3 10.3 %march.1 = (f32[128,128]{1,0:T(8,128)S(1)}, f32[128,128]{1,0:T(8,128)S(1)}, f32[128,128]{1,0:T(8,128)S(1)}, f32[128,128]{1,0:T(8,128)S(1)}) custom-call(s32[2]{0:T(128)S(1)} %pad_add_fusion.scalars, f32[296,128]{1,0:T(8,128)S(1)} %get-tuple-element.34.refs_0_, f32[296,128]{1,0:T(8,128)S(1)} %collective-permute-done.refs_1_, ...), custom_call_target="tpu_custom_call" | custom-call | flops 890000000 | tf_op jit(solution)/shard_map/march/pallas_call | solution.py:821
  34.6 0.4 %collective-permute-start.9 = (f32[128,128]{1,0:T(8,128)S(1)}, f32[128,128]{1,0:T(8,128)S(1)}, u32[]{:S(2)}, u32[]{:S(2)}) collective-permute-start(f32[128,128]{1,0:T(8,128)S(1)} %get-tuple-element.60), channel_id=1, source_target_pairs={{0,8},{8,0},{16,24},{24,16},{1,9},{9,1},{17,25},{25,17},{2,10},{10... | collective-permute-start | bytes 196616 | tf_op jit(solution)/shard_map/ppermute | solution.py:865
  35.0 1.7 %collective-permute-start.10 = (f32[128,128]{1,0:T(8,128)S(1)}, f32[128,128]{1,0:T(8,128)S(1)}, u32[]{:S(2)}, u32[]{:S(2)}) collective-permute-start(f32[128,128]{1,0:T(8,128)S(1)} %get-tuple-element.61), channel_id=1, source_target_pairs={{0,16},{8,24},{16,0},{24,8},{1,17},{9,25},{17,1},{25,9},{2,18},{10... | collective-permute-start | bytes 196616 | tf_op jit(solution)/shard_map/ppermute | solution.py:865
  36.7 2.6 %collective-permute-done.10.refs_2_ = f32[128,128]{1,0:T(8,128)S(1)} collective-permute-done((f32[128,128]{1,0:T(8,128)S(1)}, f32[128,128]{1,0:T(8,128)S(1)}, u32[]{:S(2)}, u32[]{:S(2)}) %collective-permute-start.10) | collective-permute-done | bytes 65568 | tf_op jit(solution)/shard_map/ppermute | solution.py:865
  39.3 1.7 %collective-permute-done.11.refs_3_ = f32[128,128]{1,0:T(8,128)S(1)} collective-permute-done((f32[128,128]{1,0:T(8,128)S(1)}, f32[128,128]{1,0:T(8,128)S(1)}, u32[]{:S(2)}, u32[]{:S(2)}) %collective-permute-start.11) | collective-permute-done | bytes 65568 | tf_op jit(solution)/shard_map/ppermute | solution.py:865
  41.0 1.6 %unpack.1 = f32[512,128]{1,0:T(8,128)} custom-call(s32[2]{0:T(128)S(1)} %pad_add_fusion.scalars, f32[128,128]{1,0:T(8,128)S(1)} %get-tuple-element.59.refs_0_, f32[128,128]{1,0:T(8,128)S(1)} %collective-permute-done.9.refs_1_, f32[128,128]{1,0:T(8,128)S(1)} %collective-permute-done.10.refs_2_, f32[128,128]{1,0:T(8,128)S(1)} %collective-permute-done.11.refs_3_), custom_call_target="tpu_custom_call" | custom-call | flops 150000000 | tf_op jit(solution)/shard_map/unpack/pallas_call | solution.py:821
  (6 shorter events, 0.0 us)
Async XLA Ops:
  3.4 3.1 %collective-permute-start.2 = (f32[272,128]{1,0:T(8,128)S(1)}, f32[272,128]{1,0:T(8,128)S(1)}, u32[]{:S(2)}, u32[]{:S(2)}) collective-permute-start(f32[272,128]{1,0:T(8,128)S(1)} %get-tuple-element.36.own), channel_id=1, source_target_pairs={{0,8},{8,0},{16,24},{24,16},{1,9},{9,1},{17,25},{25,17},{2,10},{10... | collective-permute-start | bytes 417800 | tf_op jit(solution)/shard_map/ppermute | solution.py:865
  4.0 9.2 %collective-permute-start.1 = (f32[296,128]{1,0:T(8,128)S(1)}, f32[296,128]{1,0:T(8,128)S(1)}, u32[]{:S(2)}, u32[]{:S(2)}) collective-permute-start(f32[296,128]{1,0:T(8,128)S(1)} %get-tuple-element.35), channel_id=1, source_target_pairs={{0,16},{8,24},{16,0},{24,8},{1,17},{9,25},{17,1},{25,9},{2,18},{10... | collective-permute-start | bytes 454664 | tf_op jit(solution)/shard_map/ppermute | solution.py:865
  7.1 6.1 %collective-permute-start.3 = (f32[272,128]{1,0:T(8,128)S(1)}, f32[272,128]{1,0:T(8,128)S(1)}, u32[]{:S(2)}, u32[]{:S(2)}) collective-permute-start(f32[272,128]{1,0:T(8,128)S(1)} %get-tuple-element.37), channel_id=1, source_target_pairs={{8,1},{9,2},{10,3},{11,4},{12,5},{13,6},{14,7},{25,24},{26,25},{27... | collective-permute-start | bytes 417800 | tf_op jit(solution)/shard_map/ppermute | solution.py:887
  7.8 5.4 %collective-permute-start.4 = (f32[272,128]{1,0:T(8,128)S(1)}, f32[272,128]{1,0:T(8,128)S(1)}, u32[]{:S(2)}, u32[]{:S(2)}) collective-permute-start(f32[272,128]{1,0:T(8,128)S(1)} %get-tuple-element.38), channel_id=1, source_target_pairs={{24,1},{25,2},{26,3},{27,4},{28,5},{29,6},{30,7},{9,24},{10,25},{1... | collective-permute-start | bytes 417800 | tf_op jit(solution)/shard_map/ppermute | solution.py:887
  8.5 10.9 %collective-permute-start.7 = (f32[864,128]{1,0:T(8,128)S(1)}, f32[864,128]{1,0:T(8,128)S(1)}, u32[]{:S(2)}, u32[]{:S(2)}) collective-permute-start(f32[864,128]{1,0:T(8,128)S(1)} %get-tuple-element.41), channel_id=1, source_target_pairs={{0,16},{8,24},{16,0},{24,8},{1,17},{9,25},{17,1},{25,9},{2,18},{10... | collective-permute-start | bytes 1327112 | tf_op jit(solution)/shard_map/ppermute | solution.py:865
  9.8 4.4 %collective-permute-start = (f32[296,128]{1,0:T(8,128)S(1)}, f32[296,128]{1,0:T(8,128)S(1)}, u32[]{:S(2)}, u32[]{:S(2)}) collective-permute-start(f32[296,128]{1,0:T(8,128)S(1)} %get-tuple-element.34.refs_0_), channel_id=1, source_target_pairs={{0,8},{8,0},{16,24},{24,16},{1,9},{9,1},{17,25},{25,17},{2,10},{10... | collective-permute-start | bytes 454664 | tf_op jit(solution)/shard_map/ppermute | solution.py:865
  13.2 1.4 %collective-permute-start.5 = (f32[296,128]{1,0:T(8,128)S(1)}, f32[296,128]{1,0:T(8,128)S(1)}, u32[]{:S(2)}, u32[]{:S(2)}) collective-permute-start(f32[296,128]{1,0:T(8,128)S(1)} %collective-permute-done.1.refs_2_), channel_id=1, source_target_pairs={{0,8},{8,0},{16,24},{24,16},{1,9},{9,1},{17,25},{25,17},{2,10},{10... | collective-permute-start | bytes 454664 | tf_op jit(solution)/shard_map/ppermute | solution.py:865
  13.3 9.6 %collective-permute-start.6 = (f32[864,128]{1,0:T(8,128)S(1)}, f32[864,128]{1,0:T(8,128)S(1)}, u32[]{:S(2)}, u32[]{:S(2)}) collective-permute-start(f32[864,128]{1,0:T(8,128)S(1)} %get-tuple-element.40.refs_4_), channel_id=1, source_target_pairs={{0,8},{8,0},{16,24},{24,16},{1,9},{9,1},{17,25},{25,17},{2,10},{10... | collective-permute-start | bytes 1327112 | tf_op jit(solution)/shard_map/ppermute | solution.py:865
  19.4 5.0 %collective-permute-start.8 = (f32[864,128]{1,0:T(8,128)S(1)}, f32[864,128]{1,0:T(8,128)S(1)}, u32[]{:S(2)}, u32[]{:S(2)}) collective-permute-start(f32[864,128]{1,0:T(8,128)S(1)} %collective-permute-done.7.refs_6_), channel_id=1, source_target_pairs={{0,8},{8,0},{16,24},{24,16},{1,9},{9,1},{17,25},{25,17},{2,10},{10... | collective-permute-start | bytes 1327112 | tf_op jit(solution)/shard_map/ppermute | solution.py:865
  34.6 2.1 %collective-permute-start.9 = (f32[128,128]{1,0:T(8,128)S(1)}, f32[128,128]{1,0:T(8,128)S(1)}, u32[]{:S(2)}, u32[]{:S(2)}) collective-permute-start(f32[128,128]{1,0:T(8,128)S(1)} %get-tuple-element.60), channel_id=1, source_target_pairs={{0,8},{8,0},{16,24},{24,16},{1,9},{9,1},{17,25},{25,17},{2,10},{10... | collective-permute-start | bytes 196616 | tf_op jit(solution)/shard_map/ppermute | solution.py:865
  35.0 4.3 %collective-permute-start.10 = (f32[128,128]{1,0:T(8,128)S(1)}, f32[128,128]{1,0:T(8,128)S(1)}, u32[]{:S(2)}, u32[]{:S(2)}) collective-permute-start(f32[128,128]{1,0:T(8,128)S(1)} %get-tuple-element.61), channel_id=1, source_target_pairs={{0,16},{8,24},{16,0},{24,8},{1,17},{9,25},{17,1},{25,9},{2,18},{10... | collective-permute-start | bytes 196616 | tf_op jit(solution)/shard_map/ppermute | solution.py:865
  36.7 4.3 %collective-permute-start.11 = (f32[128,128]{1,0:T(8,128)S(1)}, f32[128,128]{1,0:T(8,128)S(1)}, u32[]{:S(2)}, u32[]{:S(2)}) collective-permute-start(f32[128,128]{1,0:T(8,128)S(1)} %get-tuple-element.62), channel_id=1, source_target_pairs={{0,24},{8,16},{16,8},{24,0},{1,25},{9,17},{17,9},{25,1},{2,26},{10... | collective-permute-start | bytes 196616 | tf_op jit(solution)/shard_map/ppermute | solution.py:865

commit v4 on v3

--- a/solution.py
+++ b/solution.py
@@ -209,26 +209,23 @@
     return pltpu.roll(value, shift % LANES if isinstance(shift, int) else shift, axis=1)
 
 
-def exchange_groups(blocks, width):
-    blocks = list(blocks)
+def exchange_groups(blocks, width, offset=0):
     count = len(blocks)
-    lane = lane_iota(next(block for block in blocks if block is not None).shape[0])
+    rows = next(block for block in blocks if block is not None).shape[0]
+    lane = lane_iota(rows)
+    zero = jnp.zeros((rows, LANES), jnp.float32)
+    held = [
+        zero if block is None else turned(block, index * width + offset)
+        for index, block in enumerate(blocks)
+    ]
     step = 1
     while step < count:
-        keep = (lane & (step * width)) == 0
-        for index in range(count):
-            if index & step:
-                continue
-            low, high = blocks[index], blocks[index | step]
-            if low is None and high is None:
-                continue
-            zero = jnp.zeros(lane.shape, jnp.float32)
-            up = zero if low is None else turned(low, -step * width)
-            down = zero if high is None else turned(high, step * width)
-            blocks[index] = jnp.where(keep, zero if low is None else low, down)
-            blocks[index | step] = jnp.where(keep, up, zero if high is None else high)
+        stay = (lane & (step * width)) == 0
+        held = [
+            jnp.where(stay, held[index], held[(index + step) % count]) for index in range(count)
+        ]
         step *= 2
-    return blocks
+    return [turned(held[-index % count], -index * width) for index in range(count)]
 
 
 def pack_field(layout, here, source, own, other, base, packed):
@@ -239,8 +236,8 @@
         for index in range(group * rows // 8, (group + 1) * rows // 8):
             a, c = divmod(index, LINE_POINT_TOTAL)
             parts.append(source[pl.ds(a * 64 + c, 8, stride=8), :])
-        groups.append(pltpu.roll(jnp.concatenate(parts, 0), GHOST, axis=1))
-    blocks = exchange_groups(groups, unit)
+        groups.append(jnp.concatenate(parts, 0))
+    blocks = exchange_groups(groups, unit, GHOST)
     for index, value in enumerate(blocks):
         packed[index] = value
     if unit == GHOST:
@@ -518,31 +515,11 @@
         taken, refs[:] = refs[:count], refs[count:]
         return taken
 
-    chunks, tips, stored = take(sections), take(sections // 2), take(2)
+    chunks, tips = take(sections), take(sections // 2)
     (iterate, param_value, keep, gain_k, gain, gain_low, gain_high, gain_wall) = take(8)
-    slopes, (tall, wide) = take(3), take(2)
-    fine, pieces, (arrived,) = take(4), take(4), take(1)
-    copies = [
-        pltpu.make_async_copy(
-            stored[0].at[pl.ds(i, j - i)], tall.at[pl.ds(i, j - i)], arrived.at[index]
-        )
-        for index, (i, j) in enumerate(zip(TALL[0:17:4], TALL[4:21:4]))
-    ]
-    copies.append(pltpu.make_async_copy(stored[1], wide, arrived.at[5]))
-    for index in (1, 2, 3, 0, 4, 5):
-        copies[index].start()
-
     unpack_field(layout, here, 0, chunks, 0, tips, iterate)
     params = unpack_params(layout, here, chunks, tips)
     param_value[...] = params
-    to_classes(iterate, pieces)
-    for direction in range(3):
-        copies[direction + 1].wait()
-        for index in range(4):
-            source = index ^ (2 if direction == 0 else 1 if direction == 2 else 0)
-            fine[index][...] = multiply(lift_matrix(tall, direction + 1, index), pieces[source])
-        store_slabs(fine, slopes[direction])
-
     weights, stiff_line = tables[3], np.diagonal(tables[2])
     k, metal, _, has_low, has_high = [params[row : row + 1] for row in range(5)]
     distance = wall_distance(layout, params)
@@ -588,8 +565,15 @@
                 gain_high[pl.ds(c * 8, 8), :] = factor * face_high
             if c == 0:
                 gain_wall[pl.ds(a * 8, 8), :] = factor * face_wall
-    for index in (0, 4, 5):
-        copies[index].wait()
+
+
+def slope_kernel(layout, scalars, *refs):
+    (iterate, tall), slopes = refs[:2], refs[2:5]
+    fine, pieces = [refs[5 + 4 * d : 9 + 4 * d] for d in range(3)], refs[17:21]
+    to_classes(iterate, pieces)
+    gradients(tall, pieces, fine)
+    for direction in range(3):
+        store_slabs(fine[direction], slopes[direction])
 
 
 def point_slabs(source, q):
@@ -752,18 +736,18 @@
     here = scalars[0]
     rows, main, elements = layout.main_rows, layout.main, layout.elements
     lane = lane_iota(rows)
-    places = [here ^ shift for shift in range(layout.sections)]
+    sections = layout.sections
+    held_chunks = [
+        pltpu.roll(chunks[shift][...], lax.rem((here ^ shift) * main, elements), axis=1)
+        for shift in range(sections)
+    ]
     copies = []
-    for group in range(layout.sections):
-        value = None
-        for shift, there in enumerate(places):
-            amount = lax.rem((there - group) * main + elements, elements)
-            part = pltpu.roll(chunks[shift][...], amount, axis=1)
-            value = (
-                part
-                if value is None
-                else jnp.where(in_range(lane, there * main, (there + 1) * main), part, value)
-            )
+    for group in range(sections):
+        wanted = (lane // main + (sections - group)) % sections ^ here
+        value = held_chunks[0]
+        for shift in range(1, sections):
+            value = jnp.where(wanted == shift, held_chunks[shift], value)
+        value = turned(value, -group * main)
         for index in range(rows // 8):
             a, c = divmod(group * (rows // 8) + index, LINE_POINT_TOTAL)
             held[pl.ds(a * 64 + c, 8, stride=8), :] = value[index * 8 : index * 8 + 8]
@@ -920,16 +904,20 @@
         "start",
         [points, shape_of(PARAM_ROWS, columns)]
         + [points] * 3
-        + [face] * 3
-        + [fine_field] * 3
-        + [shape_of(*tall.shape, dtype=bf16), shape_of(*wide.shape, dtype=bf16)],
+        + [face] * 3,
         chunks[0] + tips,
-        hbm=[tall, wide],
-        scratch=fine_scratch + piece_scratch + [dma((6,))],
-        busy=25.0,
-    )
-    factors, slopes, (tall, wide) = started[:8], started[8:11], started[11:]
-    chunks[1], factors[1] = spread(chunks[1], factors[1])
+        busy=15.0,
+    )
+    factors = started
+    slopes = call(
+        functools.partial(slope_kernel, layout),
+        "slope",
+        [fine_field] * 3,
+        [factors[0], tall],
+        scratch=fine_scratch * 3 + piece_scratch,
+        busy=15.0,
+    )
+    chunks[1], slopes[0] = spread(chunks[1], slopes[0])
     results = call(
         functools.partial(march_kernel, layout, tables),
         "march",

time: 42.8 us -> 41.6 us (0.972)
  Pallas kernels: 20.2 us -> 18.1 us
  waiting for transfers between devices: 6.86 us -> 8.05 us
    pallas_call x5 -> x6, Pallas kernels: 20.2 us -> 18.1 us  [call(): pl.pallas_call(kernel, out_shape=out_shape, in_specs=[SCALAR] + in_vmem(l...]
    ppermute x10, waiting for transfers between devices: 6.86 us -> 8.05 us  [across(): return lax.ppermute(array, 'sec', [(i, i ^ mask) for i in range(sections)])]
  transfers between devices with their start and end apart: 12 -> 12, of which waited for: 6 -> 6; matrix products, arithmetic and copies ran while one was open for 0% -> 0% of each run, Pallas kernels for 12% -> 9%
where the time goes in v4:
time: 41.6 us; the launch traced here: 41.5 us
  Pallas kernels  18.1 us (44%)
  starting transfers between devices  15.2 us (37%)
  waiting for transfers between devices  8.05 us (19%)
    pallas_call x6, Pallas kernels, call(): pl.pallas_call(kernel, out_shape=out_shape, in_specs=[SCALAR] + in_vmem(l...  18.1 us
    ppermute x10, starting transfers between devices, across(): return lax.ppermute(array, 'sec', [(i, i ^ mask) for i in range(sections)])  13.9 us
    ppermute x10, waiting for transfers between devices, across(): return lax.ppermute(array, 'sec', [(i, i ^ mask) for i in range(sections)])  8.05 us
    ppermute x2, starting transfers between devices, body(): lax.ppermute(early if step < sections // 4 else late, ('sec', 'elem'), pa...  1.34 us
  transfers between devices with their start and end apart: 12, of which 6 were waited for; matrix products, arithmetic and copies ran while one was open for 0% of the time, Pallas kernels for 9%

profile of v4, /device:TPU:0, one launch (start us, length us, event | category | flops | bytes accessed | tf_op | source)
XLA Modules:
  0.0 41.5 jit_solution(17829179918047190393)
XLA Ops:
  0.1 3.1 %pack.1 = (f32[296,128]{1,0:T(8,128)S(1)}, f32[296,128]{1,0:T(8,128)S(1)}, f32[864,128]{1,0:T(8,128)S(1)}, f32[864,128]{1,0:T(8,128)S(1)}, f32[272,128]{1,0:T(8,128)S(1)}) custom-call(s32[2]{0:T(128)S(1)} %pad_add_fusion.scalars, f32[512,128]{1,0:T(8,128)} %bitcast.6, f32[3,512,128]{2,1,0:T(8,128)} %bitcast.5, f32[1,128]{1,0:T(1,128)} %refs_2_.1, ...), custom_call_target="tpu_custom_call" | custom-call | flops 330000000 | tf_op jit(solution)/shard_map/pack/pallas_call | solution.py:805
  3.1 0.5 %collective-permute-start.2 = (f32[272,128]{1,0:T(8,128)S(1)}, f32[272,128]{1,0:T(8,128)S(1)}, u32[]{:S(2)}, u32[]{:S(2)}) collective-permute-start(f32[272,128]{1,0:T(8,128)S(1)} %get-tuple-element.34.own), channel_id=1, source_target_pairs={{0,8},{8,0},{16,24},{24,16},{1,9},{9,1},{17,25},{25,17},{2,10},{10... | collective-permute-start | bytes 417800 | tf_op jit(solution)/shard_map/ppermute | solution.py:849
  3.7 2.6 %collective-permute-start.1 = (f32[296,128]{1,0:T(8,128)S(1)}, f32[296,128]{1,0:T(8,128)S(1)}, u32[]{:S(2)}, u32[]{:S(2)}) collective-permute-start(f32[296,128]{1,0:T(8,128)S(1)} %get-tuple-element.33), channel_id=1, source_target_pairs={{0,16},{8,24},{16,0},{24,8},{1,17},{9,25},{17,1},{25,9},{2,18},{10... | collective-permute-start | bytes 454664 | tf_op jit(solution)/shard_map/ppermute | solution.py:849
  6.2 0.6 %join.1 = (f32[272,128]{1,0:T(8,128)S(1)}, f32[272,128]{1,0:T(8,128)S(1)}) custom-call(s32[2]{0:T(128)S(1)} %pad_add_fusion.scalars, f32[272,128]{1,0:T(8,128)S(1)} %get-tuple-element.34.own, f32[272,128]{1,0:T(8,128)S(1)} %collective-permute-done.2.received), custom_call_target="tpu_custom_call" | custom-call | flops 60000000 | tf_op jit(solution)/shard_map/join/pallas_call | solution.py:805
  6.8 0.7 %collective-permute-start.3 = (f32[272,128]{1,0:T(8,128)S(1)}, f32[272,128]{1,0:T(8,128)S(1)}, u32[]{:S(2)}, u32[]{:S(2)}) collective-permute-start(f32[272,128]{1,0:T(8,128)S(1)} %get-tuple-element.35), channel_id=1, source_target_pairs={{8,1},{9,2},{10,3},{11,4},{12,5},{13,6},{14,7},{25,24},{26,25},{27... | collective-permute-start | bytes 417800 | tf_op jit(solution)/shard_map/ppermute | solution.py:871
  7.5 0.7 %collective-permute-start.4 = (f32[272,128]{1,0:T(8,128)S(1)}, f32[272,128]{1,0:T(8,128)S(1)}, u32[]{:S(2)}, u32[]{:S(2)}) collective-permute-start(f32[272,128]{1,0:T(8,128)S(1)} %get-tuple-element.36), channel_id=1, source_target_pairs={{24,1},{25,2},{26,3},{27,4},{28,5},{29,6},{30,7},{9,24},{10,25},{1... | collective-permute-start | bytes 417800 | tf_op jit(solution)/shard_map/ppermute | solution.py:871
  8.2 1.3 %collective-permute-start.7 = (f32[864,128]{1,0:T(8,128)S(1)}, f32[864,128]{1,0:T(8,128)S(1)}, u32[]{:S(2)}, u32[]{:S(2)}) collective-permute-start(f32[864,128]{1,0:T(8,128)S(1)} %get-tuple-element.39), channel_id=1, source_target_pairs={{0,16},{8,24},{16,0},{24,8},{1,17},{9,25},{17,1},{25,9},{2,18},{10... | collective-permute-start | bytes 1327112 | tf_op jit(solution)/shard_map/ppermute | solution.py:849
  9.5 3.4 %collective-permute-start = (f32[296,128]{1,0:T(8,128)S(1)}, f32[296,128]{1,0:T(8,128)S(1)}, u32[]{:S(2)}, u32[]{:S(2)}) collective-permute-start(f32[296,128]{1,0:T(8,128)S(1)} %get-tuple-element.32.refs_0_), channel_id=1, source_target_pairs={{0,8},{8,0},{16,24},{24,16},{1,9},{9,1},{17,25},{25,17},{2,10},{10... | collective-permute-start | bytes 454664 | tf_op jit(solution)/shard_map/ppermute | solution.py:849
  12.9 0.1 collective-permute-start.5
  13.0 0.5 %collective-permute-start.6 = (f32[864,128]{1,0:T(8,128)S(1)}, f32[864,128]{1,0:T(8,128)S(1)}, u32[]{:S(2)}, u32[]{:S(2)}) collective-permute-start(f32[864,128]{1,0:T(8,128)S(1)} %get-tuple-element.38.refs_4_), channel_id=1, source_target_pairs={{0,8},{8,0},{16,24},{24,16},{1,9},{9,1},{17,25},{25,17},{2,10},{10... | collective-permute-start | bytes 1327112 | tf_op jit(solution)/shard_map/ppermute | solution.py:849
  13.5 0.4 %collective-permute-done.refs_1_ = f32[296,128]{1,0:T(8,128)S(1)} collective-permute-done((f32[296,128]{1,0:T(8,128)S(1)}, f32[296,128]{1,0:T(8,128)S(1)}, u32[]{:S(2)}, u32[]{:S(2)}) %collective-permute-start) | collective-permute-done | bytes 151584 | tf_op jit(solution)/shard_map/ppermute | solution.py:849
  13.9 0.4 %collective-permute-done.5.refs_3_ = f32[296,128]{1,0:T(8,128)S(1)} collective-permute-done((f32[296,128]{1,0:T(8,128)S(1)}, f32[296,128]{1,0:T(8,128)S(1)}, u32[]{:S(2)}, u32[]{:S(2)}) %collective-permute-start.5) | collective-permute-done | bytes 151584 | tf_op jit(solution)/shard_map/ppermute | solution.py:849
  14.4 1.1 %start.1 = (f32[512,256]{1,0:T(8,128)S(1)}, f32[8,256]{1,0:T(8,128)S(1)}, f32[512,256]{1,0:T(8,128)S(1)}, f32[512,256]{1,0:T(8,128)S(1)}, f32[512,256]{1,0:T(8,1...) custom-call(s32[2]{0:T(128)S(1)} %pad_add_fusion.scalars, ...), custom_call_target="tpu_custom_call" | custom-call | flops 1500000000 | tf_op jit(solution)/shard_map/start/pallas_call | solution.py:805
  15.5 1.9 %slope.1 = (f32[11,128,256]{2,1,0:T(8,128)S(1)}, f32[11,128,256]{2,1,0:T(8,128)S(1)}, f32[11,128,256]{2,1,0:T(8,128)S(1)}) custom-call(s32[2]{0:T(128)S(1)} %pad_add_fusion.scalars, f32[512,256]{1,0:T(8,128)S(1)} %get-tuple-element.42.refs_0_.refs_10_, bf16[12416,256]{1,0:T(8,128)(2,1)S(1)} %copy-done), custom_call_target="tpu_custom_call" | custom-call | flops 1500000000 | tf_op jit(solution)/shard_map/slope/pallas_call | solution.py:805
  17.4 1.6 %collective-permute-done.7.refs_6_ = f32[864,128]{1,0:T(8,128)S(1)} collective-permute-done((f32[864,128]{1,0:T(8,128)S(1)}, f32[864,128]{1,0:T(8,128)S(1)}, u32[]{:S(2)}, u32[]{:S(2)}) %collective-permute-start.7) | collective-permute-done | bytes 442400 | tf_op jit(solution)/shard_map/ppermute | solution.py:849
  19.1 3.5 %collective-permute-start.8 = (f32[864,128]{1,0:T(8,128)S(1)}, f32[864,128]{1,0:T(8,128)S(1)}, u32[]{:S(2)}, u32[]{:S(2)}) collective-permute-start(f32[864,128]{1,0:T(8,128)S(1)} %collective-permute-done.7.refs_6_), channel_id=1, source_target_pairs={{0,8},{8,0},{16,24},{24,16},{1,9},{9,1},{17,25},{25,17},{2,10},{10... | collective-permute-start | bytes 1327112 | tf_op jit(solution)/shard_map/ppermute | solution.py:849
  22.6 1.4 %collective-permute-done.8.refs_7_ = f32[864,128]{1,0:T(8,128)S(1)} collective-permute-done((f32[864,128]{1,0:T(8,128)S(1)}, f32[864,128]{1,0:T(8,128)S(1)}, u32[]{:S(2)}, u32[]{:S(2)}) %collective-permute-start.8) | collective-permute-done | bytes 442400 | tf_op jit(solution)/shard_map/ppermute | solution.py:849
  24.0 9.9 %march.1 = (f32[128,128]{1,0:T(8,128)S(1)}, f32[128,128]{1,0:T(8,128)S(1)}, f32[128,128]{1,0:T(8,128)S(1)}, f32[128,128]{1,0:T(8,128)S(1)}) custom-call(s32[2]{0:T(128)S(1)} %pad_add_fusion.scalars, f32[296,128]{1,0:T(8,128)S(1)} %get-tuple-element.32.refs_0_, f32[296,128]{1,0:T(8,128)S(1)} %collective-permute-done.refs_1_, ...), custom_call_target="tpu_custom_call" | custom-call | flops 890000000 | tf_op jit(solution)/shard_map/march/pallas_call | solution.py:805
  34.0 0.4 %collective-permute-start.9 = (f32[128,128]{1,0:T(8,128)S(1)}, f32[128,128]{1,0:T(8,128)S(1)}, u32[]{:S(2)}, u32[]{:S(2)}) collective-permute-start(f32[128,128]{1,0:T(8,128)S(1)} %get-tuple-element.56), channel_id=1, source_target_pairs={{0,8},{8,0},{16,24},{24,16},{1,9},{9,1},{17,25},{25,17},{2,10},{10... | collective-permute-start | bytes 196616 | tf_op jit(solution)/shard_map/ppermute | solution.py:849
  34.4 1.3 %collective-permute-start.10 = (f32[128,128]{1,0:T(8,128)S(1)}, f32[128,128]{1,0:T(8,128)S(1)}, u32[]{:S(2)}, u32[]{:S(2)}) collective-permute-start(f32[128,128]{1,0:T(8,128)S(1)} %get-tuple-element.57), channel_id=1, source_target_pairs={{0,16},{8,24},{16,0},{24,8},{1,17},{9,25},{17,1},{25,9},{2,18},{10... | collective-permute-start | bytes 196616 | tf_op jit(solution)/shard_map/ppermute | solution.py:849
  35.7 0.2 collective-permute-start.11
  35.9 2.8 %collective-permute-done.10.refs_2_ = f32[128,128]{1,0:T(8,128)S(1)} collective-permute-done((f32[128,128]{1,0:T(8,128)S(1)}, f32[128,128]{1,0:T(8,128)S(1)}, u32[]{:S(2)}, u32[]{:S(2)}) %collective-permute-start.10) | collective-permute-done | bytes 65568 | tf_op jit(solution)/shard_map/ppermute | solution.py:849
  38.7 1.4 %collective-permute-done.11.refs_3_ = f32[128,128]{1,0:T(8,128)S(1)} collective-permute-done((f32[128,128]{1,0:T(8,128)S(1)}, f32[128,128]{1,0:T(8,128)S(1)}, u32[]{:S(2)}, u32[]{:S(2)}) %collective-permute-start.11) | collective-permute-done | bytes 65568 | tf_op jit(solution)/shard_map/ppermute | solution.py:849
  40.0 1.5 %unpack.1 = f32[512,128]{1,0:T(8,128)} custom-call(s32[2]{0:T(128)S(1)} %pad_add_fusion.scalars, f32[128,128]{1,0:T(8,128)S(1)} %get-tuple-element.55.refs_0_, f32[128,128]{1,0:T(8,128)S(1)} %collective-permute-done.9.refs_1_, f32[128,128]{1,0:T(8,128)S(1)} %collective-permute-done.10.refs_2_, f32[128,128]{1,0:T(8,128)S(1)} %collective-permute-done.11.refs_3_), custom_call_target="tpu_custom_call" | custom-call | flops 150000000 | tf_op jit(solution)/shard_map/unpack/pallas_call | solution.py:805
  (11 shorter events, 0.1 us)
Async XLA Ops:
  0.1 15.4 %copy-start = (bf16[12416,256]{1,0:T(8,128)(2,1)S(1)}, bf16[12416,256]{1,0:T(8,128)(2,1)}, u32[]{:S(2)}) copy-start(bf16[12416,256]{1,0:T(8,128)(2,1)} %constant.12.clone.refs_1_.refs_21_) | copy-start | bytes 19070980
  3.1 3.1 %collective-permute-start.2 = (f32[272,128]{1,0:T(8,128)S(1)}, f32[272,128]{1,0:T(8,128)S(1)}, u32[]{:S(2)}, u32[]{:S(2)}) collective-permute-start(f32[272,128]{1,0:T(8,128)S(1)} %get-tuple-element.34.own), channel_id=1, source_target_pairs={{0,8},{8,0},{16,24},{24,16},{1,9},{9,1},{17,25},{25,17},{2,10},{10... | collective-permute-start | bytes 417800 | tf_op jit(solution)/shard_map/ppermute | solution.py:849
  3.7 9.3 %collective-permute-start.1 = (f32[296,128]{1,0:T(8,128)S(1)}, f32[296,128]{1,0:T(8,128)S(1)}, u32[]{:S(2)}, u32[]{:S(2)}) collective-permute-start(f32[296,128]{1,0:T(8,128)S(1)} %get-tuple-element.33), channel_id=1, source_target_pairs={{0,16},{8,24},{16,0},{24,8},{1,17},{9,25},{17,1},{25,9},{2,18},{10... | collective-permute-start | bytes 454664 | tf_op jit(solution)/shard_map/ppermute | solution.py:849
  6.8 6.1 %collective-permute-start.3 = (f32[272,128]{1,0:T(8,128)S(1)}, f32[272,128]{1,0:T(8,128)S(1)}, u32[]{:S(2)}, u32[]{:S(2)}) collective-permute-start(f32[272,128]{1,0:T(8,128)S(1)} %get-tuple-element.35), channel_id=1, source_target_pairs={{8,1},{9,2},{10,3},{11,4},{12,5},{13,6},{14,7},{25,24},{26,25},{27... | collective-permute-start | bytes 417800 | tf_op jit(solution)/shard_map/ppermute | solution.py:871
  7.5 5.4 %collective-permute-start.4 = (f32[272,128]{1,0:T(8,128)S(1)}, f32[272,128]{1,0:T(8,128)S(1)}, u32[]{:S(2)}, u32[]{:S(2)}) collective-permute-start(f32[272,128]{1,0:T(8,128)S(1)} %get-tuple-element.36), channel_id=1, source_target_pairs={{24,1},{25,2},{26,3},{27,4},{28,5},{29,6},{30,7},{9,24},{10,25},{1... | collective-permute-start | bytes 417800 | tf_op jit(solution)/shard_map/ppermute | solution.py:871
  8.2 10.9 %collective-permute-start.7 = (f32[864,128]{1,0:T(8,128)S(1)}, f32[864,128]{1,0:T(8,128)S(1)}, u32[]{:S(2)}, u32[]{:S(2)}) collective-permute-start(f32[864,128]{1,0:T(8,128)S(1)} %get-tuple-element.39), channel_id=1, source_target_pairs={{0,16},{8,24},{16,0},{24,8},{1,17},{9,25},{17,1},{25,9},{2,18},{10... | collective-permute-start | bytes 1327112 | tf_op jit(solution)/shard_map/ppermute | solution.py:849
  9.5 4.4 %collective-permute-start = (f32[296,128]{1,0:T(8,128)S(1)}, f32[296,128]{1,0:T(8,128)S(1)}, u32[]{:S(2)}, u32[]{:S(2)}) collective-permute-start(f32[296,128]{1,0:T(8,128)S(1)} %get-tuple-element.32.refs_0_), channel_id=1, source_target_pairs={{0,8},{8,0},{16,24},{24,16},{1,9},{9,1},{17,25},{25,17},{2,10},{10... | collective-permute-start | bytes 454664 | tf_op jit(solution)/shard_map/ppermute | solution.py:849
  12.9 1.4 %collective-permute-start.5 = (f32[296,128]{1,0:T(8,128)S(1)}, f32[296,128]{1,0:T(8,128)S(1)}, u32[]{:S(2)}, u32[]{:S(2)}) collective-permute-start(f32[296,128]{1,0:T(8,128)S(1)} %collective-permute-done.1.refs_2_), channel_id=1, source_target_pairs={{0,8},{8,0},{16,24},{24,16},{1,9},{9,1},{17,25},{25,17},{2,10},{10... | collective-permute-start | bytes 454664 | tf_op jit(solution)/shard_map/ppermute | solution.py:849
  13.0 9.6 %collective-permute-start.6 = (f32[864,128]{1,0:T(8,128)S(1)}, f32[864,128]{1,0:T(8,128)S(1)}, u32[]{:S(2)}, u32[]{:S(2)}) collective-permute-start(f32[864,128]{1,0:T(8,128)S(1)} %get-tuple-element.38.refs_4_), channel_id=1, source_target_pairs={{0,8},{8,0},{16,24},{24,16},{1,9},{9,1},{17,25},{25,17},{2,10},{10... | collective-permute-start | bytes 1327112 | tf_op jit(solution)/shard_map/ppermute | solution.py:849
  15.5 8.5 %copy-start.1 = (bf16[256,3072]{1,0:T(8,128)(2,1)S(1)}, bf16[256,3072]{1,0:T(8,128)(2,1)}, u32[]{:S(2)}) copy-start(bf16[256,3072]{1,0:T(8,128)(2,1)} %constant.13.clone.refs_22_) | copy-start | bytes 4718596
  19.1 5.0 %collective-permute-start.8 = (f32[864,128]{1,0:T(8,128)S(1)}, f32[864,128]{1,0:T(8,128)S(1)}, u32[]{:S(2)}, u32[]{:S(2)}) collective-permute-start(f32[864,128]{1,0:T(8,128)S(1)} %collective-permute-done.7.refs_6_), channel_id=1, source_target_pairs={{0,8},{8,0},{16,24},{24,16},{1,9},{9,1},{17,25},{25,17},{2,10},{10... | collective-permute-start | bytes 1327112 | tf_op jit(solution)/shard_map/ppermute | solution.py:849
  34.0 1.9 %collective-permute-start.9 = (f32[128,128]{1,0:T(8,128)S(1)}, f32[128,128]{1,0:T(8,128)S(1)}, u32[]{:S(2)}, u32[]{:S(2)}) collective-permute-start(f32[128,128]{1,0:T(8,128)S(1)} %get-tuple-element.56), channel_id=1, source_target_pairs={{0,8},{8,0},{16,24},{24,16},{1,9},{9,1},{17,25},{25,17},{2,10},{10... | collective-permute-start | bytes 196616 | tf_op jit(solution)/shard_map/ppermute | solution.py:849
  34.4 4.3 %collective-permute-start.10 = (f32[128,128]{1,0:T(8,128)S(1)}, f32[128,128]{1,0:T(8,128)S(1)}, u32[]{:S(2)}, u32[]{:S(2)}) collective-permute-start(f32[128,128]{1,0:T(8,128)S(1)} %get-tuple-element.57), channel_id=1, source_target_pairs={{0,16},{8,24},{16,0},{24,8},{1,17},{9,25},{17,1},{25,9},{2,18},{10... | collective-permute-start | bytes 196616 | tf_op jit(solution)/shard_map/ppermute | solution.py:849
  35.7 4.4 %collective-permute-start.11 = (f32[128,128]{1,0:T(8,128)S(1)}, f32[128,128]{1,0:T(8,128)S(1)}, u32[]{:S(2)}, u32[]{:S(2)}) collective-permute-start(f32[128,128]{1,0:T(8,128)S(1)} %get-tuple-element.58), channel_id=1, source_target_pairs={{0,24},{8,16},{16,8},{24,0},{1,25},{9,17},{17,9},{25,1},{2,26},{10... | collective-permute-start | bytes 196616 | tf_op jit(solution)/shard_map/ppermute | solution.py:849

commit v5 on v4

--- a/solution.py
+++ b/solution.py
@@ -182,6 +182,7 @@
         self.tip_row = self.whole_units * self.unit_rows
         self.chunk_rows = self.tip_row + self.end_rows
         self.tips_rows = FIELDS * self.end_rows + PARAM_ROWS
+        self.tips_base = len(PARTS[0]) * self.chunk_rows + PARAM_ROWS
 
     def window_pieces(self, source, target, width):
         pieces = []
@@ -257,8 +258,9 @@
 
 
 def pack_kernel(layout, blocks, scalars, *refs):
-    inputs, outs, tips = refs[:5], refs[5 : 5 + 2 * len(PARTS)], refs[5 + 2 * len(PARTS)]
-    *held, packed, arrived = refs[6 + 2 * len(PARTS) :]
+    inputs, outs = refs[:5], refs[5 : 5 + 2 * len(PARTS)]
+    tips = outs[0].at[pl.ds(layout.tips_base, 2 * layout.tips_rows)]
+    *held, packed, arrived = refs[5 + 2 * len(PARTS) :]
     elements = layout.elements
     here, block = scalars[0], scalars[1]
     pairs = list(zip(inputs, held))
@@ -311,11 +313,11 @@
 
 def join_kernel(layout, scalars, own, received, early, late):
     here = scalars[0]
-    rows = layout.tips_rows
+    rows, base = layout.tips_rows, layout.tips_base
     is_even = lax.rem(here, 2) == 0
     lower = here < layout.half
-    own_high, own_low = own[:rows, :], own[rows:, :]
-    other_high, other_low = received[:rows, :], received[rows:, :]
+    own_high, own_low = [own[pl.ds(base + i * rows, rows), :] for i in range(2)]
+    other_high, other_low = [received[pl.ds(base + i * rows, rows), :] for i in range(2)]
     high = [jnp.where(is_even, own_high, other_high), jnp.where(is_even, other_high, own_high)]
     low = [jnp.where(is_even, other_low, own_low), jnp.where(is_even, own_low, other_low)]
     for index in range(2):
@@ -369,13 +371,22 @@
             block = jnp.where(at_last, merged(inner, outer), block)
         return block
 
+    by_tile = []
     for tile in range(layout.tiles):
         blocks = []
         for place in range(per_tile):
             section, index = divmod(tile * per_tile + place, layout.slot_units)
             blocks.append(unit_block(section, index) if index <= final else None)
-        for group, value in enumerate(exchange_groups(blocks, unit)):
-            target[pl.ds(group * rows, rows), pl.ds(tile * LANES, LANES)] = value
+        by_tile.append(exchange_groups(blocks, unit))
+    groups = [jnp.concatenate(values, 1) for values in zip(*by_tile)]
+    joined = 64 // rows
+    planes = [
+        jnp.concatenate(groups[a * joined : (a + 1) * joined], 0) for a in range(LINE_POINT_TOTAL)
+    ]
+    if target is not None:
+        for a, plane in enumerate(planes):
+            target[pl.ds(a * 64, 64), :] = plane
+    return planes
 
 
 def unpack_params(layout, here, chunks, tips):
@@ -412,9 +423,11 @@
 
 
 def to_classes(source, pieces):
+    planes = source
+    if not isinstance(source, list):
+        planes = [source[pl.ds(a * 64, 64), :] for a in range(LINE_POINT_TOTAL)]
     for a in range(HALF):
-        near = source[pl.ds(a * 64, 64), :]
-        far = source[pl.ds((LINE_POINT_TOTAL - 1 - a) * 64, 64), :]
+        near, far = planes[a], planes[LINE_POINT_TOTAL - 1 - a]
         for parity_a, slab in enumerate((near + far, near - far)):
             lower = slab[: HALF * 8]
             upper = jnp.concatenate(
@@ -567,13 +580,43 @@
                 gain_wall[pl.ds(a * 8, 8), :] = factor * face_wall
 
 
+def relax(layout, factors, distance, current, pieces, results, tall, right_side, target):
+    _, keep, gain_k, _, gain_low, gain_high, gain_wall = factors
+    last = LINE_POINT_TOTAL - 1
+    for index in range(4):
+        stiff = tall.at[pl.ds(TALL[16 + index], 2 * CLASS_ROWS)]
+        results[index] = multiply(stiff, pieces[index])
+    from_low = gain_low[...] * shifted(current[pl.ds(last * 64, 64), :], 1)
+    from_high = gain_high[...] * shifted(current[pl.ds(0, 64), :], -1)
+    wall = jnp.concatenate([current[pl.ds(a * 64, 8), :] for a in range(8)], 0)
+    far = jnp.zeros_like(wall)
+    for step in range(1, layout.sections):
+        far = jnp.where(distance == step, shifted(wall, -step * layout.slot), far)
+    from_wall = gain_wall[...] * far
+    for a in range(HALF):
+        for plane, stiffness in zip((a, last - a), from_classes(results, a)):
+            span = pl.ds(plane * 64, 64)
+            value = keep[span, :] * current[span, :] - gain_k[span, :] * stiffness
+            if right_side is not None:
+                value = value + right_side[span, :]
+            if plane == 0:
+                value = value + from_low
+            if plane == last:
+                value = value + from_high
+            at_wall = value[:8] + from_wall[plane * 8 : plane * 8 + 8]
+            target[span, :] = jnp.concatenate([at_wall, value[8:]], 0)
+
+
 def slope_kernel(layout, scalars, *refs):
-    (iterate, tall), slopes = refs[:2], refs[2:5]
-    fine, pieces = [refs[5 + 4 * d : 9 + 4 * d] for d in range(3)], refs[17:21]
+    (iterate, *factors), tall, slopes, first = refs[:8], refs[8], refs[9:12], refs[12]
+    results, refs = refs[13], refs[14:]
+    fine, pieces = [refs[4 * d : 4 * d + 4] for d in range(3)], refs[12:16]
     to_classes(iterate, pieces)
     gradients(tall, pieces, fine)
     for direction in range(3):
         store_slabs(fine[direction], slopes[direction])
+    distance = wall_distance(layout, factors[0][...])
+    relax(layout, factors, distance, iterate, pieces, results, tall, None, first)
 
 
 def point_slabs(source, q):
@@ -640,22 +683,22 @@
         return taken
 
     chunks, tips = [take(sections) for _ in PARTS], take(sections // 2)
-    (initial, param_value, keep, gain_k, gain, gain_low, gain_high, gain_wall) = take(8)
-    slopes, (tall, wide) = take(3), take(2)
+    (initial, *factors), slopes = take(8), take(3)
+    (first, tall, wide) = take(3)
     outs = take(sections)
-    (iterate, held, results, gain_rhs) = take(4)
+    (iterate, results, gain_rhs) = take(3)
     lifted = take(3)
     fine, pieces, fine_pieces = [take(4) for _ in range(3)], take(4), take(4)
 
     for d in range(3):
         part = next(index for index, inside in enumerate(PARTS) if 1 + d in inside)
         base = PARTS[part].index(1 + d) * layout.chunk_rows
-        unpack_field(layout, scalars[0], 1 + d, chunks[part], base, tips, held)
-        to_classes(held, pieces)
+        planes = unpack_field(layout, scalars[0], 1 + d, chunks[part], base, tips, None)
+        to_classes(planes, pieces)
         for index in range(4):
             fine[0][index][...] = multiply(lift_matrix(tall, 0, index), pieces[index])
         store_slabs(fine[0], lifted[d])
-    params = param_value[...]
+    gain, params = factors[3], factors[0][...]
     distance = wall_distance(layout, params)
     fluid = 1.0 - params[1:2]
     weight_b = column_weights(weights, columns)
@@ -686,37 +729,18 @@
                 for c in range(LINE_POINT_TOTAL):
                     span = pl.ds((plane * 8 + c) * 8, 8)
                     mass = weight_b * float(weights[plane] * weights[c] / time_step)
-                    gain_rhs[span, :] = gain[span, :] * (
+                    right_side = gain[span, :] * (
                         mass * current[span, :] - fluid * convected[c * 8 : c * 8 + 8]
                     )
-        for sweep_index in range(SWEEPS):
-            current = initial if step_index == 0 and sweep_index == 0 else iterate
-            if step_index == 0 or sweep_index > 0:
-                to_classes(current, pieces)
-            for index in range(4):
-                stiff = tall.at[pl.ds(TALL[16 + index], 2 * CLASS_ROWS)]
-                results[index] = multiply(stiff, pieces[index])
-            from_low = gain_low[...] * shifted(current[pl.ds(last * 64, 64), :], 1)
-            from_high = gain_high[...] * shifted(current[pl.ds(0, 64), :], -1)
-            wall = jnp.concatenate([current[pl.ds(a * 64, 8), :] for a in range(8)], 0)
-            far = jnp.zeros_like(wall)
-            for step in range(1, sections):
-                far = jnp.where(distance == step, shifted(wall, -step * layout.slot), far)
-            from_wall = gain_wall[...] * far
-            for a in range(HALF):
-                for plane, stiffness in zip((a, last - a), from_classes(results, a)):
-                    span = pl.ds(plane * 64, 64)
-                    value = (
-                        keep[span, :] * current[span, :]
-                        + gain_rhs[span, :]
-                        - gain_k[span, :] * stiffness
-                    )
-                    if plane == 0:
-                        value = value + from_low
-                    if plane == last:
-                        value = value + from_high
-                    at_wall = value[:8] + from_wall[plane * 8 : plane * 8 + 8]
-                    iterate[span, :] = jnp.concatenate([at_wall, value[8:]], 0)
+                    gain_rhs[span, :] = right_side
+                    if step_index == 0:
+                        iterate[span, :] = first[span, :] + right_side
+        for sweep_index in range(1 if step_index == 0 else 0, SWEEPS):
+            if sweep_index > 0:
+                to_classes(iterate, pieces)
+            relax(
+                layout, factors, distance, iterate, pieces, results, tall, gain_rhs, iterate
+            )
 
     rows = layout.main_rows
     lane = lane_iota(rows)
@@ -818,13 +842,16 @@
 
     chunk_shapes = [
         shape_of(len(fields) * layout.chunk_rows + extra, elements)
-        for fields, extra in zip(PARTS, (PARAM_ROWS, 0))
-        for _ in range(2)
+        for fields, extra in (
+            (PARTS[0], PARAM_ROWS + 2 * layout.tips_rows),
+            (PARTS[0], PARAM_ROWS),
+            *((fields, 0) for fields in PARTS[1:] for _ in range(2)),
+        )
     ]
-    *packed, tips = call(
+    packed = call(
         functools.partial(pack_kernel, layout, blocks),
         "pack",
-        chunk_shapes + [shape_of(2 * layout.tips_rows, elements)],
+        chunk_shapes,
         [],
         hbm=[
             thermal_level_points.reshape(POINTS, elements),
@@ -852,11 +879,12 @@
         {0: packed[2 * part], layout.half: across(packed[2 * part + 1], layout.half)}
         for part in range(len(PARTS))
     ]
+    chunks[0][1] = across(packed[0], 1)
     early, late = call(
         functools.partial(join_kernel, layout),
         "join",
         [shape_of(2 * layout.tips_rows, elements)] * 2,
-        [tips, across(tips, 1)],
+        [chunks[0][0], chunks[0][1]],
         busy=0.6,
     )
     tips = []
@@ -875,7 +903,8 @@
         bit = layout.half // 2
         while bit:
             for mask in sorted(chunk):
-                chunk[mask | bit] = across(chunk[mask], bit)
+                if mask | bit not in chunk:
+                    chunk[mask | bit] = across(chunk[mask], bit)
             bit //= 2
         return [chunk[mask] for mask in range(sections)], after
 
@@ -909,12 +938,13 @@
         busy=15.0,
     )
     factors = started
-    slopes = call(
+    chunks[1][0], factors[1] = lax.optimization_barrier((chunks[1][0], factors[1]))
+    *slopes, first = call(
         functools.partial(slope_kernel, layout),
         "slope",
-        [fine_field] * 3,
-        [factors[0], tall],
-        scratch=fine_scratch * 3 + piece_scratch,
+        [fine_field] * 3 + [points],
+        factors + [tall],
+        scratch=[pltpu.VMEM((4, CLASS_ROWS, columns), f32)] + fine_scratch * 3 + piece_scratch,
         busy=15.0,
     )
     chunks[1], slopes[0] = spread(chunks[1], slopes[0])
@@ -922,9 +952,8 @@
         functools.partial(march_kernel, layout, tables),
         "march",
         [shape_of(layout.main_rows, elements)] * sections,
-        chunks[0] + chunks[1] + tips + factors + slopes + [tall, wide],
+        chunks[0] + chunks[1] + tips + factors + slopes + [first, tall, wide],
         scratch=[
-            pltpu.VMEM((POINTS, columns), f32),
             pltpu.VMEM((POINTS, columns), f32),
             pltpu.VMEM((4, CLASS_ROWS, columns), f32),
             pltpu.VMEM((POINTS, columns), f32),

time: 41.6 us -> 41.7 us (level)
  waiting for transfers between devices: 8.05 us -> 9.32 us
  starting transfers between devices: 15.2 us -> 14 us
    ppermute x10 -> x9, waiting for transfers between devices: 8.05 us -> 9.32 us  [across(): return lax.ppermute(array, 'sec', [(i, i ^ mask) for i in range(sections)])]
    ppermute x10 -> x9, starting transfers between devices: 13.9 us -> 12.6 us  [across(): return lax.ppermute(array, 'sec', [(i, i ^ mask) for i in range(sections)])]
  transfers between devices with their start and end apart: 12 -> 11, of which waited for: 6 -> 6; matrix products, arithmetic and copies ran while one was open for 0% -> 0% of each run, Pallas kernels for 9% -> 9%
where the time goes in v5:
time: 41.7 us; the launch traced here: 41.5 us
  Pallas kernels  18.1 us (43%)
  starting transfers between devices  14 us (34%)
  waiting for transfers between devices  9.32 us (22%)
    pallas_call x6, Pallas kernels, call(): pl.pallas_call(kernel, out_shape=out_shape, in_specs=[SCALAR] + in_vmem(l...  18.1 us
    ppermute x9, starting transfers between devices, across(): return lax.ppermute(array, 'sec', [(i, i ^ mask) for i in range(sections)])  12.6 us
    ppermute x9, waiting for transfers between devices, across(): return lax.ppermute(array, 'sec', [(i, i ^ mask) for i in range(sections)])  9.32 us
    ppermute x2, starting transfers between devices, body(): lax.ppermute(early if step < sections // 4 else late, ('sec', 'elem'), pa...  1.34 us
  transfers between devices with their start and end apart: 11, of which 6 were waited for; matrix products, arithmetic and copies ran while one was open for 0% of the time, Pallas kernels for 9%

profile of v5, /device:TPU:0, one launch (start us, length us, event | category | flops | bytes accessed | tf_op | source)
XLA Modules:
  0.0 41.5 jit_solution(17482608970611747640)
XLA Ops:
  0.0 0.1 pad_add_fusion.scalars
  0.1 3.1 %pack.1 = (f32[568,128]{1,0:T(8,128)S(1)}, f32[296,128]{1,0:T(8,128)S(1)}, f32[864,128]{1,0:T(8,128)S(1)}, f32[864,128]{1,0:T(8,128)S(1)}) custom-call(s32[2]{0:T(128)S(1)} %pad_add_fusion.scalars, f32[512,128]{1,0:T(8,128)} %bitcast.6, f32[3,512,128]{2,1,0:T(8,128)} %bitcast.5, f32[1,128]{1,0:T(1,128)} %refs_2_.1, s32[1,128]{1,0:T(1,128)} %refs_3_.1, ...), custom_call_target="tpu_custom_call" | custom-call | flops 330000000 | tf_op jit(solution)/shard_map/pack/pallas_call | solution.py:829
  3.1 0.5 %collective-permute-start = (f32[568,128]{1,0:T(8,128)S(1)}, f32[568,128]{1,0:T(8,128)S(1)}, u32[]{:S(2)}, u32[]{:S(2)}) collective-permute-start(f32[568,128]{1,0:T(8,128)S(1)} %get-tuple-element.34.own.refs_0_), channel_id=1, source_target_pairs={{0,8},{8,0},{16,24},{24,16},{1,9},{9,1},{17,25},{25,17},{2,10},{10... | collective-permute-start | bytes 872456 | tf_op jit(solution)/shard_map/ppermute | solution.py:876
  3.7 2.6 %collective-permute-start.1 = (f32[296,128]{1,0:T(8,128)S(1)}, f32[296,128]{1,0:T(8,128)S(1)}, u32[]{:S(2)}, u32[]{:S(2)}) collective-permute-start(f32[296,128]{1,0:T(8,128)S(1)} %get-tuple-element.35), channel_id=1, source_target_pairs={{0,16},{8,24},{16,0},{24,8},{1,17},{9,25},{17,1},{25,9},{2,18},{10... | collective-permute-start | bytes 454664 | tf_op jit(solution)/shard_map/ppermute | solution.py:876
  6.2 0.0 collective-permute-done.received.refs_1_
  6.2 0.6 %join.1 = (f32[272,128]{1,0:T(8,128)S(1)}, f32[272,128]{1,0:T(8,128)S(1)}) custom-call(s32[2]{0:T(128)S(1)} %pad_add_fusion.scalars, f32[568,128]{1,0:T(8,128)S(1)} %get-tuple-element.34.own.refs_0_, f32[568,128]{1,0:T(8,128)S(1)} %collective-permute-done.received.refs_1_), custom_call_target="tpu_custom_call" | custom-call | flops 60000000 | tf_op jit(solution)/shard_map/join/pallas_call | solution.py:829
  6.8 0.7 %collective-permute-start.2 = (f32[272,128]{1,0:T(8,128)S(1)}, f32[272,128]{1,0:T(8,128)S(1)}, u32[]{:S(2)}, u32[]{:S(2)}) collective-permute-start(f32[272,128]{1,0:T(8,128)S(1)} %get-tuple-element.36), channel_id=1, source_target_pairs={{8,1},{9,2},{10,3},{11,4},{12,5},{13,6},{14,7},{25,24},{26,25},{27... | collective-permute-start | bytes 417800 | tf_op jit(solution)/shard_map/ppermute | solution.py:899
  7.5 0.7 %collective-permute-start.3 = (f32[272,128]{1,0:T(8,128)S(1)}, f32[272,128]{1,0:T(8,128)S(1)}, u32[]{:S(2)}, u32[]{:S(2)}) collective-permute-start(f32[272,128]{1,0:T(8,128)S(1)} %get-tuple-element.37), channel_id=1, source_target_pairs={{24,1},{25,2},{26,3},{27,4},{28,5},{29,6},{30,7},{9,24},{10,25},{1... | collective-permute-start | bytes 417800 | tf_op jit(solution)/shard_map/ppermute | solution.py:899
  8.2 1.6 %collective-permute-start.6 = (f32[864,128]{1,0:T(8,128)S(1)}, f32[864,128]{1,0:T(8,128)S(1)}, u32[]{:S(2)}, u32[]{:S(2)}) collective-permute-start(f32[864,128]{1,0:T(8,128)S(1)} %get-tuple-element.44), channel_id=1, source_target_pairs={{0,16},{8,24},{16,0},{24,8},{1,17},{9,25},{17,1},{25,9},{2,18},{10... | collective-permute-start | bytes 1327112 | tf_op jit(solution)/shard_map/ppermute | solution.py:876
  9.7 1.0 %collective-permute-done.1.refs_2_ = f32[296,128]{1,0:T(8,128)S(1)} collective-permute-done((f32[296,128]{1,0:T(8,128)S(1)}, f32[296,128]{1,0:T(8,128)S(1)}, u32[]{:S(2)}, u32[]{:S(2)}) %collective-permute-start.1) | collective-permute-done | bytes 151584 | tf_op jit(solution)/shard_map/ppermute | solution.py:876
  10.8 2.2 %collective-permute-start.4 = (f32[296,128]{1,0:T(8,128)S(1)}, f32[296,128]{1,0:T(8,128)S(1)}, u32[]{:S(2)}, u32[]{:S(2)}) collective-permute-start(f32[296,128]{1,0:T(8,128)S(1)} %collective-permute-done.1.refs_2_), channel_id=1, source_target_pairs={{0,8},{8,0},{16,24},{24,16},{1,9},{9,1},{17,25},{25,17},{2,10},{10... | collective-permute-start | bytes 454664 | tf_op jit(solution)/shard_map/ppermute | solution.py:876
  13.0 1.0 %collective-permute-done.4.refs_3_ = f32[296,128]{1,0:T(8,128)S(1)} collective-permute-done((f32[296,128]{1,0:T(8,128)S(1)}, f32[296,128]{1,0:T(8,128)S(1)}, u32[]{:S(2)}, u32[]{:S(2)}) %collective-permute-start.4) | collective-permute-done | bytes 151584 | tf_op jit(solution)/shard_map/ppermute | solution.py:876
  14.0 1.1 %start.1 = (f32[512,256]{1,0:T(8,128)S(1)}, f32[8,256]{1,0:T(8,128)S(1)}, f32[512,256]{1,0:T(8,128)S(1)}, f32[512,256]{1,0:T(8,128)S(1)}, f32[512,256]{1,0:T(8,1...) custom-call(s32[2]{0:T(128)S(1)} %pad_add_fusion.scalars, ...), custom_call_target="tpu_custom_call" | custom-call | flops 1500000000 | tf_op jit(solution)/shard_map/start/pallas_call | solution.py:829
  15.1 0.4 %collective-permute-start.5 = (f32[864,128]{1,0:T(8,128)S(1)}, f32[864,128]{1,0:T(8,128)S(1)}, u32[]{:S(2)}, u32[]{:S(2)}) collective-permute-start(f32[864,128]{1,0:T(8,128)S(1)} %get-tuple-element.43.refs_4_), channel_id=1, source_target_pairs={{0,8},{8,0},{16,24},{24,16},{1,9},{9,1},{17,25},{25,17},{2,10},{10... | collective-permute-start | bytes 1327112 | tf_op jit(solution)/shard_map/ppermute | solution.py:876
  15.6 2.2 %slope.1 = (f32[11,128,256]{2,1,0:T(8,128)S(1)}, f32[11,128,256]{2,1,0:T(8,128)S(1)}, f32[11,128,256]{2,1,0:T(8,128)S(1)}, f32[512,256]{1,0:T(8,128)S(1)}) custom-call(s32[2]{0:T(128)S(1)} %pad_add_fusion.scalars, f32[512,256]{1,0:T(8,128)S(1)} %get-tuple-element.45.refs_0_.refs_10_, f32[8,256]{1,0:T(8,128)S(1)} %get-tuple-element.46.refs_1_.refs_11_, ...), custom_call_target="tpu_custom_call" | custom-call | flops 1500000000 | tf_op jit(solution)/shard_map/slope/pallas_call | solution.py:829
  17.8 1.5 %collective-permute-done.6.refs_6_ = f32[864,128]{1,0:T(8,128)S(1)} collective-permute-done((f32[864,128]{1,0:T(8,128)S(1)}, f32[864,128]{1,0:T(8,128)S(1)}, u32[]{:S(2)}, u32[]{:S(2)}) %collective-permute-start.6) | collective-permute-done | bytes 442400 | tf_op jit(solution)/shard_map/ppermute | solution.py:876
  19.2 3.4 %collective-permute-start.7 = (f32[864,128]{1,0:T(8,128)S(1)}, f32[864,128]{1,0:T(8,128)S(1)}, u32[]{:S(2)}, u32[]{:S(2)}) collective-permute-start(f32[864,128]{1,0:T(8,128)S(1)} %collective-permute-done.6.refs_6_), channel_id=1, source_target_pairs={{0,8},{8,0},{16,24},{24,16},{1,9},{9,1},{17,25},{25,17},{2,10},{10... | collective-permute-start | bytes 1327112 | tf_op jit(solution)/shard_map/ppermute | solution.py:876
  22.6 1.4 %collective-permute-done.7.refs_7_ = f32[864,128]{1,0:T(8,128)S(1)} collective-permute-done((f32[864,128]{1,0:T(8,128)S(1)}, f32[864,128]{1,0:T(8,128)S(1)}, u32[]{:S(2)}, u32[]{:S(2)}) %collective-permute-start.7) | collective-permute-done | bytes 442400 | tf_op jit(solution)/shard_map/ppermute | solution.py:876
  24.0 9.7 %march.1 = (f32[128,128]{1,0:T(8,128)S(1)}, f32[128,128]{1,0:T(8,128)S(1)}, f32[128,128]{1,0:T(8,128)S(1)}, f32[128,128]{1,0:T(8,128)S(1)}) custom-call(s32[2]{0:T(128)S(1)} %pad_add_fusion.scalars, f32[568,128]{1,0:T(8,128)S(1)} %get-tuple-element.34.own.refs_0_, f32[568,128]{1,0:T(8,128)S(1)} %collective-permute-done.received.refs_1_, ...), custom_call_target="tpu_custom_call" | custom-call | flops 890000000 | tf_op jit(solution)/shard_map/march/pallas_call | solution.py:829
  33.7 0.4 %collective-permute-start.8 = (f32[128,128]{1,0:T(8,128)S(1)}, f32[128,128]{1,0:T(8,128)S(1)}, u32[]{:S(2)}, u32[]{:S(2)}) collective-permute-start(f32[128,128]{1,0:T(8,128)S(1)} %get-tuple-element.60), channel_id=1, source_target_pairs={{0,8},{8,0},{16,24},{24,16},{1,9},{9,1},{17,25},{25,17},{2,10},{10... | collective-permute-start | bytes 196616 | tf_op jit(solution)/shard_map/ppermute | solution.py:876
  34.2 1.5 %collective-permute-start.9 = (f32[128,128]{1,0:T(8,128)S(1)}, f32[128,128]{1,0:T(8,128)S(1)}, u32[]{:S(2)}, u32[]{:S(2)}) collective-permute-start(f32[128,128]{1,0:T(8,128)S(1)} %get-tuple-element.61), channel_id=1, source_target_pairs={{0,16},{8,24},{16,0},{24,8},{1,17},{9,25},{17,1},{25,9},{2,18},{10... | collective-permute-start | bytes 196616 | tf_op jit(solution)/shard_map/ppermute | solution.py:876
  35.7 2.7 %collective-permute-done.9.refs_2_ = f32[128,128]{1,0:T(8,128)S(1)} collective-permute-done((f32[128,128]{1,0:T(8,128)S(1)}, f32[128,128]{1,0:T(8,128)S(1)}, u32[]{:S(2)}, u32[]{:S(2)}) %collective-permute-start.9) | collective-permute-done | bytes 65568 | tf_op jit(solution)/shard_map/ppermute | solution.py:876
  38.4 1.6 %collective-permute-done.10.refs_3_ = f32[128,128]{1,0:T(8,128)S(1)} collective-permute-done((f32[128,128]{1,0:T(8,128)S(1)}, f32[128,128]{1,0:T(8,128)S(1)}, u32[]{:S(2)}, u32[]{:S(2)}) %collective-permute-start.10) | collective-permute-done | bytes 65568 | tf_op jit(solution)/shard_map/ppermute | solution.py:876
  40.1 1.5 %unpack.1 = f32[512,128]{1,0:T(8,128)} custom-call(s32[2]{0:T(128)S(1)} %pad_add_fusion.scalars, f32[128,128]{1,0:T(8,128)S(1)} %get-tuple-element.59.refs_0_, f32[128,128]{1,0:T(8,128)S(1)} %collective-permute-done.8.refs_1_, f32[128,128]{1,0:T(8,128)S(1)} %collective-permute-done.9.refs_2_, f32[128,128]{1,0:T(8,128)S(1)} %collective-permute-done.10.refs_3_), custom_call_target="tpu_custom_call" | custom-call | flops 150000000 | tf_op jit(solution)/shard_map/unpack/pallas_call | solution.py:829
  (9 shorter events, 0.0 us)
Async XLA Ops:
  0.1 15.5 %copy-start = (bf16[12416,256]{1,0:T(8,128)(2,1)S(1)}, bf16[12416,256]{1,0:T(8,128)(2,1)}, u32[]{:S(2)}) copy-start(bf16[12416,256]{1,0:T(8,128)(2,1)} %constant.12.clone.refs_8_.refs_22_) | copy-start | bytes 19070980
  3.1 3.1 %collective-permute-start = (f32[568,128]{1,0:T(8,128)S(1)}, f32[568,128]{1,0:T(8,128)S(1)}, u32[]{:S(2)}, u32[]{:S(2)}) collective-permute-start(f32[568,128]{1,0:T(8,128)S(1)} %get-tuple-element.34.own.refs_0_), channel_id=1, source_target_pairs={{0,8},{8,0},{16,24},{24,16},{1,9},{9,1},{17,25},{25,17},{2,10},{10... | collective-permute-start | bytes 872456 | tf_op jit(solution)/shard_map/ppermute | solution.py:876
  3.7 7.1 %collective-permute-start.1 = (f32[296,128]{1,0:T(8,128)S(1)}, f32[296,128]{1,0:T(8,128)S(1)}, u32[]{:S(2)}, u32[]{:S(2)}) collective-permute-start(f32[296,128]{1,0:T(8,128)S(1)} %get-tuple-element.35), channel_id=1, source_target_pairs={{0,16},{8,24},{16,0},{24,8},{1,17},{9,25},{17,1},{25,9},{2,18},{10... | collective-permute-start | bytes 454664 | tf_op jit(solution)/shard_map/ppermute | solution.py:876
  6.8 3.9 %collective-permute-start.2 = (f32[272,128]{1,0:T(8,128)S(1)}, f32[272,128]{1,0:T(8,128)S(1)}, u32[]{:S(2)}, u32[]{:S(2)}) collective-permute-start(f32[272,128]{1,0:T(8,128)S(1)} %get-tuple-element.36), channel_id=1, source_target_pairs={{8,1},{9,2},{10,3},{11,4},{12,5},{13,6},{14,7},{25,24},{26,25},{27... | collective-permute-start | bytes 417800 | tf_op jit(solution)/shard_map/ppermute | solution.py:899
  7.5 3.3 %collective-permute-start.3 = (f32[272,128]{1,0:T(8,128)S(1)}, f32[272,128]{1,0:T(8,128)S(1)}, u32[]{:S(2)}, u32[]{:S(2)}) collective-permute-start(f32[272,128]{1,0:T(8,128)S(1)} %get-tuple-element.37), channel_id=1, source_target_pairs={{24,1},{25,2},{26,3},{27,4},{28,5},{29,6},{30,7},{9,24},{10,25},{1... | collective-permute-start | bytes 417800 | tf_op jit(solution)/shard_map/ppermute | solution.py:899
  8.2 11.1 %collective-permute-start.6 = (f32[864,128]{1,0:T(8,128)S(1)}, f32[864,128]{1,0:T(8,128)S(1)}, u32[]{:S(2)}, u32[]{:S(2)}) collective-permute-start(f32[864,128]{1,0:T(8,128)S(1)} %get-tuple-element.44), channel_id=1, source_target_pairs={{0,16},{8,24},{16,0},{24,8},{1,17},{9,25},{17,1},{25,9},{2,18},{10... | collective-permute-start | bytes 1327112 | tf_op jit(solution)/shard_map/ppermute | solution.py:876
  10.8 3.2 %collective-permute-start.4 = (f32[296,128]{1,0:T(8,128)S(1)}, f32[296,128]{1,0:T(8,128)S(1)}, u32[]{:S(2)}, u32[]{:S(2)}) collective-permute-start(f32[296,128]{1,0:T(8,128)S(1)} %collective-permute-done.1.refs_2_), channel_id=1, source_target_pairs={{0,8},{8,0},{16,24},{24,16},{1,9},{9,1},{17,25},{25,17},{2,10},{10... | collective-permute-start | bytes 454664 | tf_op jit(solution)/shard_map/ppermute | solution.py:876
  15.1 7.5 %collective-permute-start.5 = (f32[864,128]{1,0:T(8,128)S(1)}, f32[864,128]{1,0:T(8,128)S(1)}, u32[]{:S(2)}, u32[]{:S(2)}) collective-permute-start(f32[864,128]{1,0:T(8,128)S(1)} %get-tuple-element.43.refs_4_), channel_id=1, source_target_pairs={{0,8},{8,0},{16,24},{24,16},{1,9},{9,1},{17,25},{25,17},{2,10},{10... | collective-permute-start | bytes 1327112 | tf_op jit(solution)/shard_map/ppermute | solution.py:876
  15.6 8.4 %copy-start.1 = (bf16[256,3072]{1,0:T(8,128)(2,1)S(1)}, bf16[256,3072]{1,0:T(8,128)(2,1)}, u32[]{:S(2)}) copy-start(bf16[256,3072]{1,0:T(8,128)(2,1)} %constant.13.clone.refs_23_) | copy-start | bytes 4718596
  19.2 4.8 %collective-permute-start.7 = (f32[864,128]{1,0:T(8,128)S(1)}, f32[864,128]{1,0:T(8,128)S(1)}, u32[]{:S(2)}, u32[]{:S(2)}) collective-permute-start(f32[864,128]{1,0:T(8,128)S(1)} %collective-permute-done.6.refs_6_), channel_id=1, source_target_pairs={{0,8},{8,0},{16,24},{24,16},{1,9},{9,1},{17,25},{25,17},{2,10},{10... | collective-permute-start | bytes 1327112 | tf_op jit(solution)/shard_map/ppermute | solution.py:876
  33.7 2.0 %collective-permute-start.8 = (f32[128,128]{1,0:T(8,128)S(1)}, f32[128,128]{1,0:T(8,128)S(1)}, u32[]{:S(2)}, u32[]{:S(2)}) collective-permute-start(f32[128,128]{1,0:T(8,128)S(1)} %get-tuple-element.60), channel_id=1, source_target_pairs={{0,8},{8,0},{16,24},{24,16},{1,9},{9,1},{17,25},{25,17},{2,10},{10... | collective-permute-start | bytes 196616 | tf_op jit(solution)/shard_map/ppermute | solution.py:876
  34.2 4.3 %collective-permute-start.9 = (f32[128,128]{1,0:T(8,128)S(1)}, f32[128,128]{1,0:T(8,128)S(1)}, u32[]{:S(2)}, u32[]{:S(2)}) collective-permute-start(f32[128,128]{1,0:T(8,128)S(1)} %get-tuple-element.61), channel_id=1, source_target_pairs={{0,16},{8,24},{16,0},{24,8},{1,17},{9,25},{17,1},{25,9},{2,18},{10... | collective-permute-start | bytes 196616 | tf_op jit(solution)/shard_map/ppermute | solution.py:876
  35.7 4.4 %collective-permute-start.10 = (f32[128,128]{1,0:T(8,128)S(1)}, f32[128,128]{1,0:T(8,128)S(1)}, u32[]{:S(2)}, u32[]{:S(2)}) collective-permute-start(f32[128,128]{1,0:T(8,128)S(1)} %get-tuple-element.62), channel_id=1, source_target_pairs={{0,24},{8,16},{16,8},{24,0},{1,25},{9,17},{17,9},{25,1},{2,26},{10... | collective-permute-start | bytes 196616 | tf_op jit(solution)/shard_map/ppermute | solution.py:876
